TPU v7x, 32 devices: a whole 2x2x4 slice. The times are simulated.
32 devices in a mesh: mem: 32 (over z, y, x, core).
Axes of the slice: x: 2, y: 2, z: 4, core: 2. Of those that a mesh axis runs over, the one named last changes fastest.
Arguments:
- query_feats: float32 [32768, 8], P('mem'), may hold values from -6 to 6
- feature_mask: int32 [32768, 8], P('mem'), may hold values from 0 to 1, as said below
- query_task: int32 [32768], P('mem'), may hold values from 0 to 3
- target_class: int32 [32768], P('mem'), may hold values from 0 to 15
- target_mask: int32 [32768], P('mem'), may hold values from 0 to 1, as said below
- memory_feats: float32 [2048, 8], P('mem'), may hold values from -6 to 6
- memory_task: int32 [2048], replicated, may hold values from 0 to 3, as said below
- memory_mask: int32 [2048], replicated, may hold values from 0 to 1, as said below
- anneal: float32 [1], replicated, may hold values from 0.3 to 0.7
- w_qkv: float32 [196608], P('mem'), may hold values from -0.375 to 0.375
- w_out: float32 [65536], P('mem'), may hold values from -6 to 6
- w_heads: float32 [6144], P('mem'), may hold values from -0.375 to 0.375
- w_small: float32 [1056], P('mem'), may hold values from 0.1 to 1.9
- m_qkv: float32 [196608], P('mem'), may hold values from -0.00015258789 to 0.00015258789
- m_out: float32 [65536], P('mem'), may hold values from -0.00015258789 to 0.00015258789
- m_heads: float32 [6144], P('mem'), may hold values from -0.00015258789 to 0.00015258789
- m_small: float32 [1056], P('mem'), may hold values from -0.00061035156 to 0.00061035156
- v_qkv: float32 [196608], P('mem'), may hold values from 9.536743e-12 to 3.814697e-11
- v_out: float32 [65536], P('mem'), may hold values from 9.536743e-13 to 3.8146973e-12
- v_heads: float32 [6144], P('mem'), may hold values from 9.536743e-12 to 3.814697e-11
- v_small: float32 [1056], P('mem'), may hold values from 1.5258789e-10 to 6.1035155e-10
Outputs:
- new_qkv: float32 [196608], P('mem')
- new_out: float32 [65536], P('mem')
- new_heads: float32 [6144], P('mem')
- new_small: float32 [1056], P('mem')
- first_qkv: float32 [196608], P('mem')
- first_out: float32 [65536], P('mem')
- first_heads: float32 [6144], P('mem')
- first_small: float32 [1056], P('mem')
- second_qkv: float32 [196608], P('mem')
- second_out: float32 [65536], P('mem')
- second_heads: float32 [6144], P('mem')
- second_small: float32 [1056], P('mem')
- copy_qkv: bfloat16 [196608], P('mem')
- copy_out: bfloat16 [65536], P('mem')
- copy_heads: bfloat16 [6144], P('mem')
- copy_small: bfloat16 [1056], P('mem')
- loss_value: float32 [1], replicated
- grad_norm: float32 [1], replicated
Inputs may be any that keep to these rules, and one draw needn't show every extreme that they name: `memory_mask`: the live rows of each device's 64 memory rows are a prefix of a quarter of them or more; the first device's rows are all live. `memory_task`: the first 4 memory rows have the tasks 0 to 3 in order. `target_mask`: the share of labelled queries rises along the query rows from about a quarter to about three quarters. `feature_mask`: the share of hidden features rises along the query rows from about a quarter to about three quarters.
All inputs are finite; a program needn't handle non-finite values.
Results may differ from a plain program's by a relative error of at most 0.0087.
Values may be sent and summed in bfloat16 or wider, within the bound.
A program may use at most 128 MiB of HBM per device.

v0:
```python
import math

import jax
import jax.numpy as jnp
from jax import lax
from jax.sharding import PartitionSpec as P

F = 8
D = 256
H = 8
C = 16
STEP = 10


eps_norm = 1e-05
max_norm = 0.05
beta_one = 0.9
beta_two = 0.999
adam_eps = 1e-08
decay_rate = 0.01
learn_rates = (0.05, 1.0, 0.05, 0.5)
masked_score = -1e30


def embed(feature_rows, table_flat, emb_bias):
    emb_table = table_flat.reshape(feature_rows.shape[1], -1)
    return (feature_rows[:, :, None] * emb_table[None]).reshape(
        feature_rows.shape[0], -1
    ) + emb_bias


def standard(hidden):
    centred = hidden - jnp.mean(hidden, -1, keepdims=True)
    inverse = lax.rsqrt(jnp.mean(centred * centred, -1, keepdims=True) + eps_norm)
    return (centred * inverse, inverse)


def norm_back(grad_out, hidden, gain_vec):
    normed, inverse = standard(hidden)
    grad_gain = jnp.sum(grad_out * normed, 0)
    grad_scaled = grad_out * gain_vec
    grad_hidden = inverse * (
        grad_scaled
        - jnp.mean(grad_scaled, -1, keepdims=True)
        - normed * jnp.mean(grad_scaled * normed, -1, keepdims=True)
    )
    return (grad_hidden, grad_gain)


def split_pair(values):
    upper = values.astype(jnp.bfloat16)
    lower = (values - upper.astype(jnp.float32)).astype(jnp.bfloat16)
    return (upper, lower)


def adamw(weight, first_mom, second, grad_in, factor, step_num, step_rate):
    clipped = grad_in * factor
    first_new = beta_one * first_mom + (1 - beta_one) * clipped
    second_new = beta_two * second + (1 - beta_two) * clipped * clipped
    fix_one = 1 - beta_one**step_num
    fix_two = 1 - beta_two**step_num
    weight_new = weight - step_rate * (
        first_new / fix_one / (jnp.sqrt(second_new / fix_two) + adam_eps) + decay_rate * weight
    )
    return (first_new, second_new, weight_new)


def local(
    query_feats,
    feature_mask,
    query_task,
    target_class,
    target_mask,
    memory_feats,
    memory_task,
    memory_mask,
    anneal,
    w_qkv,
    w_out,
    w_heads,
    w_small,
    m_qkv,
    m_out,
    m_heads,
    m_small,
    v_qkv,
    v_out,
    v_heads,
    v_small,
):
    high = lax.Precision.HIGHEST
    head_size = D // H
    full_qkv, full_out, full_heads, full_small = (
        lax.all_gather(w_qkv, "mem", axis=0, tiled=True),
        lax.all_gather(w_out, "mem", axis=0, tiled=True),
        lax.all_gather(w_heads, "mem", axis=0, tiled=True),
        lax.all_gather(w_small, "mem", axis=0, tiled=True),
    )
    emb_table = full_small[:D]
    emb_bias = full_small[D : 2 * D]
    gain_in = full_small[2 * D : 3 * D]
    gain_out = full_small[3 * D : 4 * D]
    score_coef = full_small[4 * D : 4 * D + H] * head_size ** (-0.5)
    qkv_low = full_qkv.reshape(D, 3 * D).astype(jnp.bfloat16)
    out_low = full_out.reshape(D, D).astype(jnp.bfloat16)
    heads_low = full_heads.reshape(D, C + F).astype(jnp.bfloat16)
    mem_hidden = embed(memory_feats, emb_table, emb_bias)
    mem_normed = (standard(mem_hidden)[0] * gain_in).astype(jnp.bfloat16)
    mem_kv = jnp.dot(mem_normed, qkv_low[:, D:], preferred_element_type=jnp.float32).astype(
        jnp.bfloat16
    )
    all_kv = lax.all_gather(mem_kv, "mem", axis=0, tiled=True)
    memory_rows = all_kv.shape[0]
    block_keys = math.gcd(memory_rows, 512)
    num_blocks = memory_rows // block_keys
    key_rows = all_kv[:, :D].reshape(num_blocks, block_keys, H, head_size)
    value_rows = all_kv[:, D:].reshape(num_blocks, block_keys, H, head_size)
    task_blocks = memory_task.reshape(num_blocks, block_keys)
    live_blocks = memory_mask.reshape(num_blocks, block_keys)
    key_blocks = (key_rows, value_rows, task_blocks, live_blocks)
    kept_input = query_feats * (1 - feature_mask).astype(jnp.float32)
    hidden_in = embed(kept_input, emb_table, emb_bias)
    query_normed = (standard(hidden_in)[0] * gain_in).astype(jnp.bfloat16)
    queries = (
        jnp.dot(query_normed, qkv_low[:, :D], preferred_element_type=jnp.float32)
        .astype(jnp.bfloat16)
        .reshape(-1, H, head_size)
    )
    num_rows = queries.shape[0]

    def allowed_of(task_row, live_row):
        return ((query_task[:, None] == task_row[None, :]) & (live_row[None, :] > 0))[None]

    def scores_of(key_block, allowed):
        raw_scores = jnp.einsum(
            "qhd,khd->hqk", queries, key_block, preferred_element_type=jnp.float32
        )
        return (
            raw_scores,
            jnp.where(allowed, score_coef[:, None, None] * raw_scores, masked_score),
        )

    def stats_step(state_in, block_data):
        row_top, row_sum = state_in
        key_block, value_block, task_row, live_row = block_data
        allowed = allowed_of(task_row, live_row)
        scores = scores_of(key_block, allowed)[1]
        new_top = jnp.maximum(row_top, jnp.max(scores, -1))
        shifted = jnp.where(allowed, jnp.exp(scores - new_top[..., None]), 0.0)
        return ((new_top, row_sum * jnp.exp(row_top - new_top) + jnp.sum(shifted, -1)), None)

    start_state = (
        jnp.full((H, num_rows), masked_score, jnp.float32),
        jnp.zeros((H, num_rows), jnp.float32),
    )
    (row_top, row_sum), unused = lax.scan(stats_step, start_state, key_blocks)

    def probs_of(scores, allowed):
        return jnp.where(allowed, jnp.exp(scores - row_top[..., None]), 0.0) / row_sum[..., None]

    def value_step(accum, block_data):
        key_block, value_block, task_row, live_row = block_data
        allowed = allowed_of(task_row, live_row)
        probs_low = probs_of(scores_of(key_block, allowed)[1], allowed).astype(jnp.bfloat16)
        return (
            accum
            + jnp.einsum(
                "hqk,khd->qhd", probs_low, value_block, preferred_element_type=jnp.float32
            ),
            None,
        )

    attn_sum, unused = lax.scan(
        value_step, jnp.zeros((num_rows, H, head_size), jnp.float32), key_blocks
    )
    attended = attn_sum.reshape(num_rows, D).astype(jnp.bfloat16)
    residual = hidden_in + jnp.dot(attended, out_low, preferred_element_type=jnp.float32)
    final_normed = (standard(residual)[0] * gain_out).astype(jnp.bfloat16)
    head_out = jnp.dot(final_normed, heads_low, preferred_element_type=jnp.float32)
    logits = head_out[:, :C]
    recon_err = head_out[:, C:] - query_feats
    label_mask = target_mask.astype(jnp.float32)
    feat_mask = feature_mask.astype(jnp.float32)
    onehot_class = jax.nn.one_hot(target_class, C, dtype=jnp.float32)
    picked = jnp.sum(logits * onehot_class, -1)
    sum_target, sum_recon, count_target, count_recon = lax.psum(
        (
            jnp.sum(label_mask * (jax.nn.logsumexp(logits, -1) - picked)),
            jnp.sum(feat_mask * recon_err**2),
            jnp.sum(label_mask),
            jnp.sum(feat_mask),
        ),
        "mem",
    )
    count_target = jnp.maximum(count_target, 1.0)
    count_recon = jnp.maximum(count_recon, 1.0)
    weight_a = anneal[0]
    loss_value = weight_a * sum_target / count_target + (1 - weight_a) * sum_recon / count_recon
    grad_logits = (
        weight_a / count_target * label_mask[:, None] * (jax.nn.softmax(logits, -1) - onehot_class)
    )
    grad_recon = (1 - weight_a) / count_recon * feat_mask * 2.0 * recon_err
    grad_head_out = jnp.concatenate([grad_logits, grad_recon], 1).astype(jnp.bfloat16)
    grad_heads = jnp.dot(final_normed.T, grad_head_out, preferred_element_type=jnp.float32)
    grad_final = jnp.dot(grad_head_out, heads_low.T, preferred_element_type=jnp.float32)
    grad_resid, grad_gain_out = norm_back(grad_final, residual, gain_out)
    grad_branch = grad_resid.astype(jnp.bfloat16)
    grad_wout = jnp.dot(attended.T, grad_branch, preferred_element_type=jnp.float32)
    grad_attn = (
        jnp.dot(grad_branch, out_low.T, preferred_element_type=jnp.float32)
        .astype(jnp.bfloat16)
        .reshape(num_rows, H, head_size)
    )
    row_delta = jnp.sum(
        grad_attn.astype(jnp.float32)
        * attended.reshape(num_rows, H, head_size).astype(jnp.float32),
        -1,
    ).T

    def back_step(state_in, block_data):
        key_block, value_block, task_row, live_row = block_data
        allowed = allowed_of(task_row, live_row)
        raw_scores, scores = scores_of(key_block, allowed)
        soft_probs = probs_of(scores, allowed)
        grad_probs = jnp.einsum(
            "qhd,khd->hqk", grad_attn, value_block, preferred_element_type=jnp.float32
        )
        grad_scores = (soft_probs * (grad_probs - row_delta[..., None])).astype(jnp.bfloat16)
        grad_beta = jnp.sum(grad_scores.astype(jnp.float32) * raw_scores, (1, 2))
        grad_query = jnp.einsum(
            "hqk,khd->qhd", grad_scores, key_block, preferred_element_type=jnp.float32
        )
        grad_key = (
            jnp.einsum("hqk,qhd->khd", grad_scores, queries, preferred_element_type=jnp.float32)
            * score_coef[None, :, None]
        )
        grad_value = jnp.einsum(
            "hqk,qhd->khd",
            soft_probs.astype(jnp.bfloat16),
            grad_attn,
            preferred_element_type=jnp.float32,
        )
        block_rows = key_block.shape[0]
        grad_kv = jnp.concatenate(
            [grad_key.reshape(block_rows, D), grad_value.reshape(block_rows, D)], 1
        )
        return ((state_in[0] + grad_query, state_in[1] + grad_beta), grad_kv)

    init_state = (jnp.zeros((num_rows, H, head_size), jnp.float32), jnp.zeros((H,), jnp.float32))
    (grad_q_sum, grad_beta_sum), kv_parts = lax.scan(back_step, init_state, key_blocks)
    kv_grad = lax.psum_scatter(
        kv_parts.reshape(memory_rows, 2 * D), "mem", scatter_dimension=0, tiled=True
    )
    grad_q_low = (grad_q_sum * score_coef[None, :, None]).reshape(num_rows, D).astype(jnp.bfloat16)
    grad_wq = jnp.dot(query_normed.T, grad_q_low, preferred_element_type=jnp.float32)
    grad_qn = jnp.dot(grad_q_low, qkv_low[:, :D].T, preferred_element_type=jnp.float32)
    grad_in_q, gain_in_q = norm_back(grad_qn, hidden_in, gain_in)
    grad_hidden = grad_resid + grad_in_q
    kv_upper, kv_lower = split_pair(kv_grad)
    grad_wkv = jnp.dot(mem_normed.T, kv_upper, preferred_element_type=jnp.float32) + jnp.dot(
        mem_normed.T, kv_lower, preferred_element_type=jnp.float32
    )
    grad_mn = jnp.dot(kv_upper, qkv_low[:, D:].T, preferred_element_type=jnp.float32) + jnp.dot(
        kv_lower, qkv_low[:, D:].T, preferred_element_type=jnp.float32
    )
    grad_mem, gain_in_m = norm_back(grad_mn, mem_hidden, gain_in)
    grad_table = jnp.einsum(
        "qf,qfe->fe", kept_input, grad_hidden.reshape(num_rows, F, -1), precision=high
    )
    grad_table = grad_table + jnp.einsum(
        "qf,qfe->fe", memory_feats, grad_mem.reshape(memory_feats.shape[0], F, -1), precision=high
    )
    grad_bias = jnp.sum(grad_hidden, 0) + jnp.sum(grad_mem, 0)
    small_size = full_small.shape[0]
    grad_small = jnp.concatenate(
        [
            grad_table.reshape(-1),
            grad_bias,
            gain_in_q + gain_in_m,
            grad_gain_out,
            grad_beta_sum * head_size ** (-0.5),
            jnp.zeros((small_size - 4 * D - H,), jnp.float32),
        ]
    )
    grad_qkv = jnp.concatenate([grad_wq, grad_wkv], 1).reshape(-1)
    shards = (
        lax.psum_scatter(grad_qkv, "mem", scatter_dimension=0, tiled=True),
        lax.psum_scatter(grad_wout.reshape(-1), "mem", scatter_dimension=0, tiled=True),
        lax.psum_scatter(grad_heads.reshape(-1), "mem", scatter_dimension=0, tiled=True),
        lax.psum_scatter(grad_small, "mem", scatter_dimension=0, tiled=True),
    )
    local_squares = sum((jnp.sum(piece_grad * piece_grad) for piece_grad in shards))
    grad_total = jnp.sqrt(lax.psum(local_squares, "mem"))
    factor = jnp.minimum(1.0, max_norm / (grad_total + 1e-06))
    step_num = float(STEP)
    weights_all = (w_qkv, w_out, w_heads, w_small)
    firsts = (m_qkv, m_out, m_heads, m_small)
    seconds = (v_qkv, v_out, v_heads, v_small)
    results = [
        adamw(weight, first_mom, second, grad_in, factor, step_num, step_rate)
        for weight, first_mom, second, grad_in, step_rate in zip(
            weights_all, firsts, seconds, shards, learn_rates
        )
    ]
    new_w = [entry[2] for entry in results]
    return (
        new_w[0],
        new_w[1],
        new_w[2],
        new_w[3],
        results[0][0],
        results[1][0],
        results[2][0],
        results[3][0],
        results[0][1],
        results[1][1],
        results[2][1],
        results[3][1],
        new_w[0].astype(jnp.bfloat16),
        new_w[1].astype(jnp.bfloat16),
        new_w[2].astype(jnp.bfloat16),
        new_w[3].astype(jnp.bfloat16),
        loss_value.reshape(1),
        grad_total.reshape(1),
    )


def solution(mesh):
    placed = (
        P("mem", None),
        P("mem", None),
        P("mem"),
        P("mem"),
        P("mem"),
        P("mem", None),
        P(),
        P(),
        P(),
        P("mem"),
        P("mem"),
        P("mem"),
        P("mem"),
        P("mem"),
        P("mem"),
        P("mem"),
        P("mem"),
        P("mem"),
        P("mem"),
        P("mem"),
        P("mem"),
    )
    return jax.shard_map(
        local,
        mesh=mesh,
        in_specs=placed,
        out_specs=(
            P("mem"),
            P("mem"),
            P("mem"),
            P("mem"),
            P("mem"),
            P("mem"),
            P("mem"),
            P("mem"),
            P("mem"),
            P("mem"),
            P("mem"),
            P("mem"),
            P("mem"),
            P("mem"),
            P("mem"),
            P("mem"),
            P(),
            P(),
        ),
        check_vma=False,
    )
```

profile of v0, /device:TPU:0, one launch (start us, length us, event | category | flops | bytes accessed | tf_op | source)
XLA Modules:
  0.0 763.3 jit_solution(16829456224447970304)
XLA Ops:
  9.7 42.3 %all-reduce.9 = (f32[1056]{0:T(1024)S(1)}, bf16[6144]{0:T(1024)(128)(2,1)S(1)}) all-reduce(f32[1056]{0:T(1024)S(1)} %dynamic-update-slice, f32[6144]{0:T(1024)S(1)} %dynamic-update-slice.1), channel_id=1, replica_groups=mesh['mem'=32] {'mem'}, use_global_device_ids=true, to_apply=%add | all-reduce | flops 7200 | bytes 45312
  55.3 41.3 %all_gather.16 = bf16[196608]{0:T(1024)(128)(2,1)S(1)} all-gather(bf16[6144]{0:T(1024)(128)(2,1)S(1)} %convert.24), channel_id=1, replica_groups=mesh['mem'=32] {'mem'}, dimensions={0}, use_global_device_ids=true | all-gather | bytes 405504 | tf_op jit(solution)/shard_map/all_gather | solution.py:94
  101.4 37.2 %all_gather.18 = bf16[65536]{0:T(1024)(128)(2,1)S(1)} all-gather(bf16[2048]{0:T(1024)(128)(2,1)S(1)} %convert.25), channel_id=1, replica_groups=mesh['mem'=32] {'mem'}, dimensions={0}, use_global_device_ids=true | all-gather | bytes 135168 | tf_op jit(solution)/shard_map/all_gather | solution.py:95
  142.2 8.4 %all-gather.2.cloned.1.call-done = bf16[2048,512]{1,0:T(8,128)(2,1)} async-done(((bf16[64,512]{1,0:T(8,128)(2,1)}), bf16[2048,512]{1,0:T(8,128)(2,1)}) %all-gather.2.cloned.1.call-update) | async-done | bytes 2097168 | tf_op jit(solution)/shard_map/all_gather | solution.py:112
  150.6 2.7 fusion.89
  159.5 35.7 %while.39 = (s32[]{:T(128)}, f32[8,1024]{1,0:T(8,128)S(1)}, f32[8,1024]{1,0:T(8,128)S(1)}, s32[1024]{0:T(1024)S(1)}, s32[4,512]{1,0:T(4,128)S(1)}, /*index=5*/s3...) while((s32[]{:T(128)}, f32[8,1024]{1,0:T(8,128)S(1)}, ...), condition=%wide.region_7.8_spmd.clone, body=%wide.region_4.7_spmd.clone.sunk | while | flops 303079936 | bytes 36353224 | solution.py:156
  160.0 4.1 fusion.140
  164.2 4.3 select_reduce_fusion.3
  169.0 4.1 fusion.140
  173.1 4.3 select_reduce_fusion.3
  177.9 4.1 fusion.140
  182.0 4.3 select_reduce_fusion.3
  186.8 4.1 fusion.140
  191.0 4.3 select_reduce_fusion.3
  195.4 33.0 %while.40 = (s32[]{:T(128)}, f32[1024,8,32]{0,2,1:T(8,128)S(1)}, bf16[4,512,8,32]{1,3,2,0:T(8,128)(2,1)}, s32[1024]{0:T(1024)S(1)}, s32[4,512]{1,0:T(4,128)S(1)}...) while((s32[]{:T(128)}, f32[1024,8,32]{0,2,1:T(8,128)S(1)}, ...), condition=%wide.region_9.10_spmd.clone, body=%wide.region_8.9_spmd.clone.sunk | while | flops 563610112 | bytes 4274870 | solution.py:173
  196.0 7.7 %fusion.145 = f32[1024,8,32]{0,2,1:T(8,128)S(1)} fusion(bf16[1024,8,32]{0,2,1:T(8,128)(2,1)S(1)} %get-tuple-element.853, f32[8,1024]{1,0:T(8,128)S(1)} %get-tuple-element.855, f32[8,1024]{1,0:T(8,128)S(1)} %get-tuple-element.854, f32[8]{0:T(128)S(1)} %get-tuple-element.851, pred[1024,512]{0,1:T(8,128)(4,1)S(1)} %compare_and_fusion.7, ...), kind=kOutput, calls=%fused_computation.28.clone.1 | convolution fusion | flops 562561024 | bytes 3737120 | tf_op jit(solution)/shard_map/while/body/eval_jaxpr/hqk,khd->qhd/dot_general | solution.py:167
  204.3 7.7 %fusion.145 = f32[1024,8,32]{0,2,1:T(8,128)S(1)} fusion(bf16[1024,8,32]{0,2,1:T(8,128)(2,1)S(1)} %get-tuple-element.853, f32[8,1024]{1,0:T(8,128)S(1)} %get-tuple-element.855, f32[8,1024]{1,0:T(8,128)S(1)} %get-tuple-element.854, f32[8]{0:T(128)S(1)} %get-tuple-element.851, pred[1024,512]{0,1:T(8,128)(4,1)S(1)} %compare_and_fusion.7, ...), kind=kOutput, calls=%fused_computation.28.clone.1 | convolution fusion | flops 562561024 | bytes 3737120 | tf_op jit(solution)/shard_map/while/body/eval_jaxpr/hqk,khd->qhd/dot_general | solution.py:167
  212.5 7.7 %fusion.145 = f32[1024,8,32]{0,2,1:T(8,128)S(1)} fusion(bf16[1024,8,32]{0,2,1:T(8,128)(2,1)S(1)} %get-tuple-element.853, f32[8,1024]{1,0:T(8,128)S(1)} %get-tuple-element.855, f32[8,1024]{1,0:T(8,128)S(1)} %get-tuple-element.854, f32[8]{0:T(128)S(1)} %get-tuple-element.851, pred[1024,512]{0,1:T(8,128)(4,1)S(1)} %compare_and_fusion.7, ...), kind=kOutput, calls=%fused_computation.28.clone.1 | convolution fusion | flops 562561024 | bytes 3737120 | tf_op jit(solution)/shard_map/while/body/eval_jaxpr/hqk,khd->qhd/dot_general | solution.py:167
  220.7 7.7 %fusion.145 = f32[1024,8,32]{0,2,1:T(8,128)S(1)} fusion(bf16[1024,8,32]{0,2,1:T(8,128)(2,1)S(1)} %get-tuple-element.853, f32[8,1024]{1,0:T(8,128)S(1)} %get-tuple-element.855, f32[8,1024]{1,0:T(8,128)S(1)} %get-tuple-element.854, f32[8]{0:T(128)S(1)} %get-tuple-element.851, pred[1024,512]{0,1:T(8,128)(4,1)S(1)} %compare_and_fusion.7, ...), kind=kOutput, calls=%fused_computation.28.clone.1 | convolution fusion | flops 562561024 | bytes 3737120 | tf_op jit(solution)/shard_map/while/body/eval_jaxpr/hqk,khd->qhd/dot_general | solution.py:167
  233.9 38.7 %all-reduce.8 = (f32[]{:T(128)}, f32[]{:T(128)}) all-reduce(f32[]{:T(128)} %get-tuple-element.440, f32[]{:T(128)} %get-tuple-element.442), channel_id=1, replica_groups=mesh['mem'=32] {'mem'}, use_global_device_ids=true, to_apply=%region_17.18 | all-reduce | flops 2 | bytes 16 | tf_op jit(solution)/shard_map/psum | solution.py:186
  278.2 150.5 %while.41 = (s32[]{:T(128)}, f32[1024,8,32]{0,2,1:T(8,128)}, f32[8]{0:T(128)}, f32[4,512,512]{2,1,0:T(8,128)}, bf16[4,512,8,32]{1,3,2,0:T(8,128)(2,1)}, /*index=...) while((s32[]{:T(128)}, f32[1024,8,32]{0,2,1:T(8,128)}, ...), condition=%wide.region_23.24_spmd.clone, body=%wide.region_21.23_spmd.clone.sunk | while | flops 1415447040 | bytes 156940240 | solution.py:250
  279.7 3.3 fusion.155
  283.0 5.7 copy-done
  288.7 6.7 fusion.159
  295.4 12.7 %fusion.156 = (f32[8]{0:T(128)S(1)}, bf16[8,1024,512]{1,2,0:T(8,128)(2,1)S(1)}) fusion(f32[8,512,1024]{2,1,0:T(8,128)} %copy-done, f32[8,1024]{1,0:T(8,128)} %get-tuple-element.906, bf16[1024,8,32]{0,2,1:T(8,128)(2,1)} %get-tuple-element.905, bf16[4,512,8,32]{1,3,2,0:T(8,128)(2,1)} %get-tuple-element.904, s32[]{:T(128)S(6)} %copy.149, ...), kind=kOutput, calls=%fused_computation.47.clone.1 | convolution fusion | flops 314572800 | bytes 26574916 | tf_op jit(solution)/shard_map/while/body/eval_jaxpr/qhd,khd->hqk/dot_general | solution.py:225
  308.1 2.6 convolution_multiply_fusion.2
  310.7 3.5 fusion.157
  316.9 3.3 fusion.155
  320.3 5.7 copy-done
  326.0 6.7 fusion.159
  332.6 12.7 %fusion.156 = (f32[8]{0:T(128)S(1)}, bf16[8,1024,512]{1,2,0:T(8,128)(2,1)S(1)}) fusion(f32[8,512,1024]{2,1,0:T(8,128)} %copy-done, f32[8,1024]{1,0:T(8,128)} %get-tuple-element.906, bf16[1024,8,32]{0,2,1:T(8,128)(2,1)} %get-tuple-element.905, bf16[4,512,8,32]{1,3,2,0:T(8,128)(2,1)} %get-tuple-element.904, s32[]{:T(128)S(6)} %copy.149, ...), kind=kOutput, calls=%fused_computation.47.clone.1 | convolution fusion | flops 314572800 | bytes 26574916 | tf_op jit(solution)/shard_map/while/body/eval_jaxpr/qhd,khd->hqk/dot_general | solution.py:225
  345.4 2.6 convolution_multiply_fusion.2
  348.0 3.9 fusion.157
  354.6 3.3 fusion.155
  357.9 5.7 copy-done
  363.6 6.7 fusion.159
  370.3 12.7 %fusion.156 = (f32[8]{0:T(128)S(1)}, bf16[8,1024,512]{1,2,0:T(8,128)(2,1)S(1)}) fusion(f32[8,512,1024]{2,1,0:T(8,128)} %copy-done, f32[8,1024]{1,0:T(8,128)} %get-tuple-element.906, bf16[1024,8,32]{0,2,1:T(8,128)(2,1)} %get-tuple-element.905, bf16[4,512,8,32]{1,3,2,0:T(8,128)(2,1)} %get-tuple-element.904, s32[]{:T(128)S(6)} %copy.149, ...), kind=kOutput, calls=%fused_computation.47.clone.1 | convolution fusion | flops 314572800 | bytes 26574916 | tf_op jit(solution)/shard_map/while/body/eval_jaxpr/qhd,khd->hqk/dot_general | solution.py:225
  385.6 3.9 fusion.157
  392.1 3.3 fusion.155
  395.5 5.7 copy-done
  401.2 6.7 fusion.159
  407.9 12.7 %fusion.156 = (f32[8]{0:T(128)S(1)}, bf16[8,1024,512]{1,2,0:T(8,128)(2,1)S(1)}) fusion(f32[8,512,1024]{2,1,0:T(8,128)} %copy-done, f32[8,1024]{1,0:T(8,128)} %get-tuple-element.906, bf16[1024,8,32]{0,2,1:T(8,128)(2,1)} %get-tuple-element.905, bf16[4,512,8,32]{1,3,2,0:T(8,128)(2,1)} %get-tuple-element.904, s32[]{:T(128)S(6)} %copy.149, ...), kind=kOutput, calls=%fused_computation.47.clone.1 | convolution fusion | flops 314572800 | bytes 26574916 | tf_op jit(solution)/shard_map/while/body/eval_jaxpr/qhd,khd->hqk/dot_general | solution.py:225
  420.6 2.6 convolution_multiply_fusion.2
  423.2 3.9 fusion.157
  442.3 128.3 %reduce-scatter.2.cloned.1.call-done = f32[64,512]{1,0:T(8,128)} async-done(((f32[2048,512]{1,0:T(8,128)}), f32[64,512]{1,0:T(8,128)}) %reduce-scatter.2.cloned.1.call-update) | async-done | bytes 131088 | tf_op jit(solution)/shard_map/reduce_scatter | solution.py:251
  577.4 37.3 %all-reduce.7 = (f32[6144]{0:T(1024)S(1)}, f32[1056]{0:T(1024)S(1)}) all-reduce(f32[6144]{0:T(1024)S(1)} %reshape.518, f32[1056]{0:T(1024)S(1)} %concatenate.15), channel_id=5, replica_groups=mesh['mem'=32] {'mem'}, use_global_device_ids=true, to_apply=%region_29.30.clone | all-reduce | flops 7200 | bytes 57600
  616.1 87.1 %all-reduce.13.cloned.1.call-done = (f32[196608]{0:T(1024)}, f32[65536]{0:T(1024)}) async-done(((f32[196608]{0:T(1024)}, f32[65536]{0:T(1024)}), (f32[196608]{0:T(1024)}, f32[65536]{0:T(1024)})) %all-reduce.13.cloned.1.call-update) | async-done | bytes 1048592
  708.4 39.5 %all-reduce.6 = (f32[]{:T(128)}, f32[]{:T(128)}, f32[]{:T(128)}) all-reduce(f32[]{:T(128)S(6)} %add.225, f32[]{:T(128)} %get-tuple-element.441, f32[]{:T(128)} %get-tuple-element.439), channel_id=1, replica_groups=mesh['mem'=32] {'mem'}, use_global_device_ids=true, to_apply=%region_42.43 | all-reduce | flops 3 | bytes 24 | tf_op jit(solution)/shard_map/psum | solution.py:293
  (324 shorter events, 73.9 us)
Async XLA Ops:
  7.2 152.3 %copy-start.16 = (s32[1024]{0:T(1024)S(1)}, s32[1024]{0:T(1024)}, u32[]{:S(2)}) copy-start(s32[1024]{0:T(1024)} %param.29) | copy-start | bytes 12292
  7.2 143.4 %all-gather.2.cloned.1.call-start = ((), (), s32[]{:S(2)}) async-start(), calls=%async_computation.1 | async-start | bytes 2162688 | tf_op jit(solution)/shard_map/all_gather | solution.py:112
  52.6 106.9 %copy-start.33 = (f32[256]{0:T(256)}, f32[256]{0:T(256)S(1)}, u32[]{:S(2)}) copy-start(f32[256]{0:T(256)S(1)} %get-tuple-element.553) | copy-start | bytes 3076
  52.6 106.9 %copy-start.35 = (f32[256]{0:T(256)}, f32[256]{0:T(256)S(1)}, u32[]{:S(2)}) copy-start(f32[256]{0:T(256)S(1)} %get-tuple-element.554) | copy-start | bytes 3076
  52.6 106.9 %copy-start.37 = (f32[256]{0:T(256)}, f32[256]{0:T(256)S(1)}, u32[]{:S(2)}) copy-start(f32[256]{0:T(256)S(1)} %get-tuple-element.555) | copy-start | bytes 3076
  52.7 106.8 %copy-start.27 = (f32[8,32]{1,0:T(8,128)}, f32[8,32]{1,0:T(8,128)S(1)}, u32[]{:S(2)}) copy-start(f32[8,32]{1,0:T(8,128)S(1)} %add.204) | copy-start | bytes 3076
  52.8 106.8 %copy-start.28 = (f32[8,32]{1,0:T(8,128)}, f32[8,32]{1,0:T(8,128)S(1)}, u32[]{:S(2)}) copy-start(f32[8,32]{1,0:T(8,128)S(1)} %mul.534) | copy-start | bytes 3076
  53.6 85.7 %copy-start.46 = (f32[64]{0:T(128)}, f32[64]{0:T(128)S(1)}, u32[]{:S(2)}) copy-start(f32[64]{0:T(128)S(1)} %broadcast_multiply_fusion.9) | copy-start | bytes 772
  54.5 105.1 %copy-start.50 = (f32[64]{0:T(128)}, f32[64]{0:T(128)S(1)}, u32[]{:S(2)}) copy-start(f32[64]{0:T(128)S(1)} %add_rsqrt_fusion.2) | copy-start | bytes 772
  55.3 86.6 %copy-start.11 = (f32[64,256]{1,0:T(8,128)}, f32[64,256]{1,0:T(8,128)S(1)}, u32[]{:S(2)}) copy-start(f32[64,256]{1,0:T(8,128)S(1)} %copy.69) | copy-start | bytes 196612
  96.9 56.3 %copy-start.6 = (bf16[256,768]{1,0:T(8,128)(2,1)}, bf16[256,768]{1,0:T(8,128)(2,1)S(1)}, u32[]{:S(2)}) copy-start(bf16[256,768]{1,0:T(8,128)(2,1)S(1)} %convert_element_type.124) | copy-start | bytes 1179652
  97.8 472.8 %reduce-scatter.2.cloned.1.call-start = ((), (), s32[]{:S(2)}) async-start(), calls=%async_computation.2 | async-start | bytes 4325376 | tf_op jit(solution)/shard_map/reduce_scatter | solution.py:251
  159.5 35.8 %copy-start.14 = (f32[1024,8,32]{0,2,1:T(8,128)S(1)}, f32[1024,8,32]{0,2,1:T(8,128)}, u32[]{:S(2)}) copy-start(f32[1024,8,32]{0,2,1:T(8,128)} %custom-call.2) | copy-start | bytes 3145732
  195.3 36.0 %copy-start.43 = (f32[256]{0:T(256)S(1)}, f32[256]{0:T(256)}, u32[]{:S(2)}) copy-start(f32[256]{0:T(256)} %get-tuple-element.552) | copy-start | bytes 3076
  195.3 37.0 %copy-start.19 = (bf16[256,24]{1,0:T(8,128)(2,1)S(1)}, bf16[256,24]{1,0:T(8,128)(2,1)}, u32[]{:S(2)}) copy-start(bf16[256,24]{1,0:T(8,128)(2,1)} %convert_element_type.135) | copy-start | bytes 36868
  195.3 37.2 %copy-start.21 = (f32[1024,8]{0,1:T(8,128)S(1)}, f32[1024,8]{0,1:T(8,128)}, u32[]{:S(2)}) copy-start(f32[1024,8]{0,1:T(8,128)} %param.27) | copy-start | bytes 98308
  195.4 37.2 %copy-start.22 = (s32[1024,8]{0,1:T(8,128)S(1)}, s32[1024,8]{0,1:T(8,128)}, u32[]{:S(2)}) copy-start(s32[1024,8]{0,1:T(8,128)} %param.28) | copy-start | bytes 98308
  195.4 37.9 %copy-start.44 = (s32[1024]{0:T(1024)S(1)}, s32[1024]{0:T(1024)}, u32[]{:S(2)}) copy-start(s32[1024]{0:T(1024)} %param.30) | copy-start | bytes 12292
  195.4 37.9 %copy-start.45 = (s32[1024]{0:T(1024)S(1)}, s32[1024]{0:T(1024)}, u32[]{:S(2)}) copy-start(s32[1024]{0:T(1024)} %param.31) | copy-start | bytes 12292
  229.4 44.5 %copy-start.29 = (f32[8]{0:T(128)}, f32[8]{0:T(128)S(1)}, u32[]{:S(2)}) copy-start(f32[8]{0:T(128)S(1)} %get-tuple-element.934) | copy-start | bytes 100
  229.4 48.7 %copy-start.8 = (f32[8,1024]{1,0:T(8,128)}, f32[8,1024]{1,0:T(8,128)S(1)}, u32[]{:S(2)}) copy-start(f32[8,1024]{1,0:T(8,128)S(1)} %get-tuple-element.919) | copy-start | bytes 98308
  229.4 48.7 %copy-start.17 = (f32[8,1024]{1,0:T(8,128)}, f32[8,1024]{1,0:T(8,128)S(1)}, u32[]{:S(2)}) copy-start(f32[8,1024]{1,0:T(8,128)S(1)} %get-tuple-element.928) | copy-start | bytes 98308
  229.4 48.7 %copy-start.23 = (s32[4,512]{1,0:T(4,128)}, s32[4,512]{1,0:T(4,128)S(1)}, u32[]{:S(2)}) copy-start(s32[4,512]{1,0:T(4,128)S(1)} %get-tuple-element.932) | copy-start | bytes 24580
  230.8 47.5 %copy-start.2 = (bf16[1024,8,32]{0,2,1:T(8,128)(2,1)}, bf16[1024,8,32]{0,2,1:T(8,128)(2,1)S(1)}, u32[]{:S(2)}) copy-start(bf16[1024,8,32]{0,2,1:T(8,128)(2,1)S(1)} %convert_element_type.128) | copy-start | bytes 1572868
  278.2 151.7 %copy-start.25 = (f32[1024]{0:T(1024)S(1)}, f32[1024]{0:T(1024)}, u32[]{:S(2)}) copy-start(f32[1024]{0:T(1024)} %copy-done.24) | copy-start | bytes 12292
  278.2 152.8 %copy-start.4 = (bf16[1024,256]{0,1:T(8,128)(2,1)S(1)}, bf16[1024,256]{0,1:T(8,128)(2,1)}, u32[]{:S(2)}) copy-start(bf16[1024,256]{0,1:T(8,128)(2,1)} %copy-done.3) | copy-start | bytes 1572868
  278.2 158.0 %copy-start.7 = (bf16[256,768]{1,0:T(8,128)(2,1)S(1)}, bf16[256,768]{1,0:T(8,128)(2,1)}, u32[]{:S(2)}) copy-start(bf16[256,768]{1,0:T(8,128)(2,1)} %copy-done.6) | copy-start | bytes 1179652
  428.8 142.9 %copy-start.12 = (f32[64,256]{1,0:T(8,128)S(1)}, f32[64,256]{1,0:T(8,128)}, u32[]{:S(2)}) copy-start(f32[64,256]{1,0:T(8,128)} %copy-done.11) | copy-start | bytes 196612
  428.8 142.9 %copy-start.34 = (f32[256]{0:T(256)S(1)}, f32[256]{0:T(256)}, u32[]{:S(2)}) copy-start(f32[256]{0:T(256)} %copy-done.33) | copy-start | bytes 3076
  428.8 142.9 %copy-start.36 = (f32[256]{0:T(256)S(1)}, f32[256]{0:T(256)}, u32[]{:S(2)}) copy-start(f32[256]{0:T(256)} %copy-done.35) | copy-start | bytes 3076
  428.8 142.9 %copy-start.38 = (f32[256]{0:T(256)S(1)}, f32[256]{0:T(256)}, u32[]{:S(2)}) copy-start(f32[256]{0:T(256)} %copy-done.37) | copy-start | bytes 3076
  428.8 142.9 %copy-start.47 = (f32[64]{0:T(128)S(1)}, f32[64]{0:T(128)}, u32[]{:S(2)}) copy-start(f32[64]{0:T(128)} %copy-done.46) | copy-start | bytes 772
  428.9 142.9 %copy-start.51 = (f32[64]{0:T(128)S(1)}, f32[64]{0:T(128)}, u32[]{:S(2)}) copy-start(f32[64]{0:T(128)} %copy-done.50) | copy-start | bytes 772
  428.9 148.0 %copy-start.39 = (f32[64,8]{0,1:T(8,128)S(1)}, f32[64,8]{0,1:T(8,128)}, u32[]{:S(2)}) copy-start(f32[64,8]{0,1:T(8,128)} %param.32) | copy-start | bytes 6148
  428.9 148.4 %copy-start.54 = (f32[256]{0:T(256)S(1)}, f32[256]{0:T(256)}, u32[]{:S(2)}) copy-start(f32[256]{0:T(256)} %get-tuple-element.427) | copy-start | bytes 3076
  428.9 321.1 %copy-start.32 = (f32[6144]{0:T(1024)S(1)}, f32[6144]{0:T(1024)}, u32[]{:S(2)}) copy-start(f32[6144]{0:T(1024)} %param.36) | copy-start | bytes 73732
  428.9 321.1 %copy-start.41 = (f32[6144]{0:T(1024)S(1)}, f32[6144]{0:T(1024)}, u32[]{:S(2)}) copy-start(f32[6144]{0:T(1024)} %param.40) | copy-start | bytes 73732
  428.9 321.1 %copy-start.42 = (f32[6144]{0:T(1024)S(1)}, f32[6144]{0:T(1024)}, u32[]{:S(2)}) copy-start(f32[6144]{0:T(1024)} %param.44) | copy-start | bytes 73732
  428.9 322.5 %copy-start.40 = (f32[2048]{0:T(1024)S(1)}, f32[2048]{0:T(1024)}, u32[]{:S(2)}) copy-start(f32[2048]{0:T(1024)} %param.37) | copy-start | bytes 24580
  428.9 322.5 %copy-start.52 = (f32[2048]{0:T(1024)S(1)}, f32[2048]{0:T(1024)}, u32[]{:S(2)}) copy-start(f32[2048]{0:T(1024)} %param.41) | copy-start | bytes 24580
  428.9 322.5 %copy-start.53 = (f32[2048]{0:T(1024)S(1)}, f32[2048]{0:T(1024)}, u32[]{:S(2)}) copy-start(f32[2048]{0:T(1024)} %param.45) | copy-start | bytes 24580
  429.0 323.8 %copy-start.55 = (f32[192]{0:T(256)S(1)}, f32[192]{0:T(256)}, u32[]{:S(2)}) copy-start(f32[192]{0:T(256)} %param.38) | copy-start | bytes 2308
  429.0 323.8 %copy-start.56 = (f32[192]{0:T(256)S(1)}, f32[192]{0:T(256)}, u32[]{:S(2)}) copy-start(f32[192]{0:T(256)} %param.42) | copy-start | bytes 2308
  429.0 323.8 %copy-start.57 = (f32[192]{0:T(256)S(1)}, f32[192]{0:T(256)}, u32[]{:S(2)}) copy-start(f32[192]{0:T(256)} %param.46) | copy-start | bytes 2308
  429.0 324.5 %copy-start.58 = (f32[33]{0:T(128)S(1)}, f32[33]{0:T(128)}, u32[]{:S(2)}) copy-start(f32[33]{0:T(128)} %param.39) | copy-start | bytes 400
  429.0 324.4 %copy-start.59 = (f32[33]{0:T(128)S(1)}, f32[33]{0:T(128)}, u32[]{:S(2)}) copy-start(f32[33]{0:T(128)} %param.43) | copy-start | bytes 400
  429.0 324.4 %copy-start.60 = (f32[33]{0:T(128)S(1)}, f32[33]{0:T(128)}, u32[]{:S(2)}) copy-start(f32[33]{0:T(128)} %param.47) | copy-start | bytes 400
  429.1 274.1 %all-reduce.13.cloned.1.call-start = ((), (), s32[]{:S(2)}) async-start(), calls=%async_computation.3 | async-start | bytes 2097152
  (34 other events, 337.9 us)
Sparse Core Ops, SparseCore 0:
  97.9 52.6 all-gather.1
  429.2 141.3 reduce-scatter.1
  576.8 126.3 all-reduce.12
where the time goes:
time: 773 us; the launch traced here: 763 us
  blocking collectives  236 us (31%)
  waiting for transfers between devices  224 us (29%)
  matrix products  180 us (23%)
  local copies, waits for them, and re-layouts  49.9 us (6%)
  other arithmetic  47.9 us (6%)
  between operations  24.2 us (3%)
    reduce_scatter x1, waiting for transfers between devices, local(): lax.psum_scatter(kv_parts.reshape(memory_rows, 2 * D), 'mem', scatter_dim...  128 us
    unnamed x4, waiting for transfers between devices  87.1 us
    unnamed x2, blocking collectives  79.6 us
    dot_general x4, matrix products, back_step(): jnp.einsum('qhd,khd->hqk', grad_attn, value_block, preferred_element_type...  50.8 us
    all_gather x1, blocking collectives, local(): lax.all_gather(w_qkv, 'mem', axis=0, tiled=True)  41.3 us
    psum x1, blocking collectives, local(): grad_total = jnp.sqrt(lax.psum(local_squares, 'mem'))  39.5 us
    psum x1, blocking collectives, local(): lax.psum((jnp.sum(label_mask * (jax.nn.logsumexp(logits, -1) - picked)),...  38.7 us
    all_gather x1, blocking collectives, local(): lax.all_gather(w_out, 'mem', axis=0, tiled=True)  37.2 us
  transfers between devices with their start and end apart: 3, of which 3 were waited for; matrix products, arithmetic and copies ran while one was open for 3% of the time, Pallas kernels for 0%

commit v1 on v0

--- a/solution.py
+++ b/solution.py
@@ -1,14 +1,18 @@
+import functools
 import math
 
 import jax
 import jax.numpy as jnp
 from jax import lax
+from jax.experimental import pallas as pl
+from jax.experimental.pallas import tpu as pltpu
 from jax.sharding import PartitionSpec as P
 
 F = 8
 D = 256
 H = 8
 C = 16
+TASKS = 4
 STEP = 10
 
 
@@ -325,6 +329,924 @@
     )
 
 
+f32 = jnp.float32
+bf16 = jnp.bfloat16
+LOG2E = math.log2(math.e)
+QB = 128
+KC = 384
+VROWS = 80
+E_CAP = 16
+SMALL_LANE = 88
+COUNT_LANE = 122
+
+
+def place_of(dev, planes):
+    return (dev % 2) * (4 * planes) + ((dev // 2) % 4) * planes + dev // 8
+
+
+def nt(a, b):
+    return lax.dot_general(a, b, (((1,), (1,)), ((), ())), preferred_element_type=f32)
+
+
+def tn(a, b):
+    return lax.dot_general(a, b, (((0,), (0,)), ((), ())), preferred_element_type=f32)
+
+
+def nn(a, b):
+    return jnp.dot(a, b, preferred_element_type=f32)
+
+
+def iota(shape, dim):
+    return lax.broadcasted_iota(jnp.int32, shape, dim)
+
+
+def split3(v):
+    hi = v.astype(bf16).astype(f32)
+    rest = v - hi
+    mid = rest.astype(bf16).astype(f32)
+    return hi, mid, rest - mid
+
+
+def wide(v, lanes):
+    return jnp.concatenate([v] * (lanes // v.shape[1]), axis=1) if lanes > v.shape[1] else v
+
+
+def embed_t(kept, table, bias):
+    parts = []
+    for f in range(F):
+        rows = slice(32 * f, 32 * f + 32)
+        parts.append(kept[f : f + 1] * table[rows] + bias[rows])
+    return jnp.concatenate(parts, axis=0)
+
+
+def norm_t(v):
+    centred = v - jnp.mean(v, axis=0, keepdims=True)
+    inverse = lax.rsqrt(jnp.mean(centred * centred, axis=0, keepdims=True) + eps_norm)
+    return centred * inverse, inverse
+
+
+def norm_back_t(grad, normed, inverse, gain):
+    scaled = grad * gain
+    return inverse * (
+        scaled
+        - jnp.mean(scaled, axis=0, keepdims=True)
+        - normed * jnp.mean(scaled * normed, axis=0, keepdims=True)
+    )
+
+
+def sizes(n, num_q, num_mem):
+    q_blocks = (num_q + TASKS * (QB - 1)) // QB
+    q_blocks += q_blocks % 2
+    k_chunks = (num_mem + TASKS * (KC - 1)) // KC
+    return q_blocks, k_chunks
+
+
+def step_kernel(
+    n, num_q, num_mem, small_size,
+    qf, fm, qt, tc, tm, mt, mm, an, gw, gf,
+    out_s, out_l,
+    w_s, wt_s, wh_s, wht_s, kdup_s, vaug_w,
+    cols, coefb,
+    posq, posm, xs, fs, ct, f3_s, mfeat,
+    kaug, vaug, kt_s, vt_s, mnt, gk, gv,
+    qn_s, q_s, qhi, qlo, att, il_s, gres, fn_s, gho_s, gb_s, dap, dneg, dq_s, stat_q,
+    ebuf, sbuf, ecur, acc, m_s,
+    acc_gain, gqkv, gout, ghead,
+    blk_c0, blk_nc, blk_tile, ch_base, ch_end,
+):
+    planes = n // 8
+    rows_dev = D // n
+    per_small = small_size // n
+    q_blocks, k_chunks = sizes(n, num_q, num_mem)
+    qs = q_blocks * QB
+
+    pieces = [gw[place_of(d, planes)].astype(f32) for d in range(n)]
+    for col in range(8):
+        block = jnp.concatenate([piece[8 * col : 8 * col + 8] for piece in pieces], axis=0)
+        w_s[:, 128 * col : 128 * col + 128] = block.astype(bf16)
+        wt_s[128 * col : 128 * col + 128, :] = block.T.astype(bf16)
+    lane = iota((8, 128), 1)
+    tiles = [gf[8 * place_of(d, planes) : 8 * place_of(d, planes) + 8, :] for d in range(n)]
+    lane_w = iota((D, 128), 1)
+    heads = pltpu.roll(jnp.concatenate(tiles, axis=0), 64, 1)
+    heads = jnp.where(lane_w < C + F, heads, 0.0)
+    wh_s[...] = heads.astype(bf16)
+    wht_s[...] = heads.T[:32].astype(bf16)
+    feats = []
+    for b in range(n // 2):
+        feats.append(jnp.where(lane < 64, tiles[2 * b], pltpu.roll(tiles[2 * b + 1], 64, 1)))
+    feats = jnp.concatenate(feats, axis=1)
+    f3_s[...] = jnp.concatenate(list(split3(feats)) + [jnp.zeros_like(feats)], axis=0).astype(bf16)
+    dup_r = iota((D, 4 * 128), 0)
+    dup_l = iota((D, 4 * 128), 1)
+    low6 = dup_l & 127
+    dup = (dup_r == 64 * (dup_l >> 7) + (low6 & 63)).astype(f32).astype(bf16)
+    once = ((dup_r == 64 * (dup_l >> 7) + low6) & (low6 < 64)).astype(f32).astype(bf16)
+    kdup_s[...] = nn(w_s[:, D : 2 * D], dup).astype(bf16)
+    vaug_w[...] = nn(w_s[:, 2 * D : 3 * D], once).astype(bf16)
+
+    small_rows = gf[pl.ds(0, n, stride=8), :]
+    lane_n = iota((n, 128), 1)
+    count_t = jnp.maximum(jnp.sum(jnp.where(lane_n == COUNT_LANE, small_rows, 0.0)), 1.0)
+    count_r = jnp.maximum(jnp.sum(jnp.where(lane_n == COUNT_LANE + 1, small_rows, 0.0)), 1.0)
+    used = 4 * D + 2 * H
+    s3 = jnp.concatenate(
+        list(split3(small_rows)) + [jnp.zeros((128 - 3 * n, 128), f32)], axis=0
+    ).astype(bf16)
+    row = iota((used, 128), 0)
+    lan = iota((used, 128), 1)
+    slot = lan & (n - 1)
+    core_of = slot // (4 * planes)
+    dev_of = (slot % planes) * 8 + ((slot // planes) % 4) * 2 + core_of
+    pick = (row >= per_small * dev_of) & (row < per_small * dev_of + per_small) & (lan < 3 * n)
+    spread = nn(pick.astype(f32).astype(bf16), s3)
+    row_dev = jnp.floor((row.astype(f32) + 0.5) * (1.0 / per_small)).astype(jnp.int32)
+    here = (lan - SMALL_LANE) == (row - per_small * row_dev)
+    column = jnp.sum(jnp.where(here, spread, 0.0), axis=1, keepdims=True)
+    cols[...] = jnp.broadcast_to(column[: 4 * D], (4 * D, 128))
+    for h in range(H):
+        coefb[32 * h : 32 * h + 32, :] = jnp.broadcast_to(
+            column[4 * D + h : 4 * D + h + 1] * (32 ** (-0.5)), (32, 128)
+        )
+
+    task_row = iota((8, 256), 0)
+    marks = []
+    for b in range(num_q // 256):
+        marks.append((qt[:, 256 * b : 256 * b + 256] == task_row).astype(f32))
+    for b in range(num_mem // 256):
+        cut = slice(256 * b, 256 * b + 256)
+        marks.append(((mt[:, cut] == task_row) & (mm[:, cut] > 0)).astype(f32))
+    marks_all = jnp.concatenate(marks, axis=0)
+    tri = (iota((256, 256), 0) < iota((256, 256), 1)).astype(f32).astype(bf16)
+    ranks = nn(marks_all.astype(bf16), tri)
+    totals = jnp.sum(marks_all, axis=1, keepdims=True)
+    task_col = iota((8, 1), 0)
+
+    def lay_out(first, count, unit):
+        carry = jnp.zeros((8, 1), f32)
+        before = []
+        for b in range(count):
+            before.append(carry)
+            at = 8 * (first + b)
+            carry = carry + totals[at : at + 8]
+        base = jnp.int32(0)
+        bases, counts, units = [], [], []
+        base_vec = jnp.zeros((8, 1), f32)
+        for t in range(TASKS):
+            num = jnp.sum(jnp.where(task_col == t, carry, 0.0)).astype(jnp.int32)
+            bases.append(base)
+            counts.append(num)
+            used_units = lax.div(num + (unit - 1), jnp.int32(unit))
+            units.append(used_units)
+            base_vec = base_vec + jnp.where(task_col == t, base.astype(f32), 0.0)
+            base = base + used_units * unit
+        places = []
+        for b in range(count):
+            at = 8 * (first + b)
+            places.append(
+                jnp.sum(
+                    marks[first + b] * (base_vec + before[b] + ranks[at : at + 8]),
+                    axis=0,
+                    keepdims=True,
+                )
+                - (1.0 - jnp.sum(marks[first + b], axis=0, keepdims=True))
+            )
+        return jnp.concatenate(places, axis=1), bases, counts, units
+
+    place_q, q_base, q_count, q_units = lay_out(0, num_q // 256, QB)
+    place_m, m_base, m_count, m_units = lay_out(num_q // 256, num_mem // 256, KC)
+    posq[...] = place_q
+    posm[...] = place_m
+
+    tile = jnp.int32(0)
+    for t in range(TASKS):
+        first_chunk = lax.div(m_base[t], jnp.int32(KC))
+        first_block = lax.div(q_base[t], jnp.int32(QB))
+
+        def fill_chunk(i, carry, t=t, first_chunk=first_chunk):
+            ch_base[first_chunk + i] = m_base[t]
+            ch_end[first_chunk + i] = m_base[t] + m_count[t]
+            return carry
+
+        lax.fori_loop(0, m_units[t], fill_chunk, 0)
+
+        def fill_block(i, tile_in, t=t, first_chunk=first_chunk, first_block=first_block):
+            blk_c0[first_block + i] = first_chunk
+            blk_nc[first_block + i] = m_units[t]
+            blk_tile[first_block + i] = tile_in
+            return tile_in + m_units[t]
+
+        tile = lax.fori_loop(0, q_units[t], fill_block, tile)
+    num_blocks = q_units[0] + q_units[1] + q_units[2] + q_units[3]
+    num_chunks = m_units[0] + m_units[1] + m_units[2] + m_units[3]
+
+    xq = qf[...]
+    fmq = fm[...].astype(f32)
+    row8 = iota((8, num_q), 0)
+    label_rows = jnp.where(
+        row8 == 0, tc[...].astype(f32), jnp.where(row8 == 1, tm[...].astype(f32), 0.0)
+    )
+    q_rows = jnp.concatenate(
+        list(split3(xq)) + [fmq, label_rows, jnp.zeros((8, num_q), f32)], axis=0
+    ).astype(bf16)
+    for b in range(qs // 256):
+        chosen = (
+            (place_q == (iota((256, 1), 0) + 256 * b).astype(f32)).astype(f32).astype(bf16)
+        )
+        got = nt(q_rows, chosen)
+        cut = slice(256 * b, 256 * b + 256)
+        xs[:, cut] = got[0:8] + got[8:16] + got[16:24]
+        fs[:, cut] = got[24:32]
+        ct[:, cut] = got[32:40]
+
+    emb_w = lambda lanes: wide(cols[0:D, :], lanes)
+    emb_b = lambda lanes: wide(cols[D : 2 * D, :], lanes)
+    gain_in = lambda lanes: wide(cols[2 * D : 3 * D, :], lanes)
+    gain_out = lambda lanes: wide(cols[3 * D : 4 * D, :], lanes)
+
+    def mem_chunk(c, carry):
+        at = pl.ds(pl.multiple_of(c * KC, KC), KC)
+        base, end = ch_base[c], ch_end[c]
+        s_col = iota((KC, 1), 0) + c * KC
+        source = jnp.where(s_col < end, s_col, base).astype(f32)
+        chosen = (posm[...] == source).astype(f32).astype(bf16)
+        got = nt(f3_s[...], chosen)
+        feats_c = got[0:8] + got[8:16] + got[16:24]
+        mfeat[:, at] = feats_c
+        hidden = embed_t(feats_c, emb_w(KC), emb_b(KC))
+        normed, unused = norm_t(hidden)
+        mn = (normed * gain_in(KC)).astype(bf16)
+        mnt[:, at] = mn
+        kt_s[:, at] = nn(wt_s[D : 2 * D, :], mn).astype(bf16)
+        live_row = ((iota((1, KC), 1) + c * KC) < end).astype(f32)
+        vt = nn(wt_s[2 * D : 3 * D, :], mn) * live_row
+        tail = jnp.where(iota((16, KC), 0) == 0, live_row, 0.0)
+        vt_s[:, at] = jnp.concatenate(
+            [part for p in range(4) for part in (vt[64 * p : 64 * p + 64], tail)], axis=0
+        ).astype(bf16)
+        kaug[at, :] = tn(mn, kdup_s[...]).astype(bf16)
+        live_col = (s_col < end).astype(f32)
+        low = iota((KC, 512), 1) & 127
+        vn = jnp.where((low == 64) | (low == 65), 1.0, tn(mn, vaug_w[...]))
+        vaug[at, :] = (vn * live_col).astype(bf16)
+        gk[at, :] = jnp.zeros((KC, D), f32)
+        gv[at, :] = jnp.zeros((KC, D), f32)
+        return carry
+
+    lax.fori_loop(0, num_chunks, mem_chunk, 0)
+
+    coef2 = wide(coefb[...], 256)
+
+    def pre_block(j, carry):
+        at = pl.ds(pl.multiple_of(j * 256, 256), 256)
+        kept = xs[:, at] * (1.0 - fs[:, at])
+        hidden = embed_t(kept, emb_w(256), emb_b(256))
+        normed, unused = norm_t(hidden)
+        qn = (normed * gain_in(256)).astype(bf16)
+        qn_s[:, at] = qn
+        q = nn(wt_s[0:D, :], qn).astype(bf16)
+        q_s[:, at] = q
+        scaled = q.astype(f32) * (coef2 * LOG2E)
+        upper = scaled.astype(bf16)
+        qhi[:, at] = upper
+        qlo[:, at] = (scaled - upper.astype(f32)).astype(bf16)
+        att[:, at] = jnp.zeros((D, 256), bf16)
+        il_s[:, at] = jnp.zeros((H, 256), f32)
+        dq_s[:, at] = jnp.zeros((D, 256), f32)
+        return carry
+
+    lax.fori_loop(0, qs // 256, pre_block, 0)
+
+    zero_h = jnp.zeros((32, 128), bf16)
+
+    def diagonal(ref, at, p):
+        return [
+            jnp.concatenate([ref[64 * p : 64 * p + 32, at], zero_h], axis=1),
+            jnp.concatenate([zero_h, ref[64 * p + 32 : 64 * p + 64, at]], axis=1),
+        ]
+
+    def score_operand(at, p):
+        return jnp.concatenate(diagonal(qhi, at, p) + diagonal(qlo, at, p), axis=0)
+
+    def finish_forward(at, p, got):
+        inverse = 1.0 / got[64:65, :]
+        il_s[2 * p : 2 * p + 1, at] = inverse[:, :128]
+        il_s[2 * p + 1 : 2 * p + 2, at] = inverse[:, 128:]
+        att[64 * p : 64 * p + 32, at] = (got[0:32, :128] * inverse[:, :128]).astype(bf16)
+        att[64 * p + 32 : 64 * p + 64, at] = (got[32:64, 128:] * inverse[:, 128:]).astype(bf16)
+
+    def pair(p, width):
+        return slice(width * p, width * p + width)
+
+    def forward_block(i, carry):
+        at = pl.ds(pl.multiple_of(i * QB, QB), QB)
+        c0, nc, tile0 = blk_c0[i], blk_nc[i], blk_tile[i]
+
+        @pl.when(nc == 1)
+        def one():
+            keys = pl.ds(pl.multiple_of(c0 * KC, KC), KC)
+            keep = jnp.minimum(tile0, E_CAP)
+            for p in range(4):
+                s = nn(kaug[keys, pair(p, 128)], score_operand(at, p))
+                top = jnp.max(s, axis=0, keepdims=True)
+                m_s[i, :, pair(p, 256)] = top
+                e = jnp.exp2(s - top).astype(bf16)
+                ebuf[keep, :, pair(p, 256)] = e
+                finish_forward(at, p, nn(vt_s[pair(p, VROWS), keys], e))
+
+        @pl.when(nc > 1)
+        def many():
+            m_s[i] = jnp.full((1, 1024), -3e38, f32)
+            acc[...] = jnp.zeros_like(acc)
+
+            def tops(c, inner):
+                keys = pl.ds(pl.multiple_of((c0 + c) * KC, KC), KC)
+                for p in range(4):
+                    s = nn(kaug[keys, pair(p, 128)], score_operand(at, p))
+                    m_s[i, :, pair(p, 256)] = jnp.maximum(
+                        m_s[i, :, pair(p, 256)], jnp.max(s, axis=0, keepdims=True)
+                    )
+                return inner
+
+            lax.fori_loop(0, nc, tops, 0)
+
+            def sums(c, inner):
+                keys = pl.ds(pl.multiple_of((c0 + c) * KC, KC), KC)
+                keep = jnp.minimum(tile0 + c, E_CAP)
+                for p in range(4):
+                    s = nn(kaug[keys, pair(p, 128)], score_operand(at, p))
+                    e = jnp.exp2(s - m_s[i, :, pair(p, 256)]).astype(bf16)
+                    ebuf[keep, :, pair(p, 256)] = e
+                    acc[pair(p, VROWS), :] += nn(vt_s[pair(p, VROWS), keys], e)
+                return inner
+
+            lax.fori_loop(0, nc, sums, 0)
+            for p in range(4):
+                finish_forward(at, p, acc[pair(p, VROWS), :])
+
+        return carry
+
+    lax.fori_loop(0, num_blocks, forward_block, 0)
+
+    weight_a = an[0]
+    scale_t = weight_a / count_t
+    scale_r = (1.0 - weight_a) / count_r
+    acc_gain[...] = jnp.zeros_like(acc_gain)
+    out_l[...] = jnp.zeros_like(out_l)
+
+    def fold(v):
+        return v[:, :128] + v[:, 128:256]
+
+    def mid_block(j, carry):
+        at = pl.ds(pl.multiple_of(j * 256, 256), 256)
+        x = xs[:, at]
+        fmask = fs[:, at]
+        kept = x * (1.0 - fmask)
+        hidden = embed_t(kept, emb_w(256), emb_b(256))
+        attended = att[:, at]
+        residual = hidden + nn(wt_s[3 * D : 4 * D, :], attended)
+        normed, inverse = norm_t(residual)
+        fn = (normed * gain_out(256)).astype(bf16)
+        fn_s[:, at] = fn
+        head = nn(wht_s[...], fn)
+        logits = head[0:C]
+        err = head[C : C + F] - x
+        label = ct[1:2, at]
+        hot = (iota((C, 256), 0).astype(f32) == ct[0:1, at]).astype(f32)
+        top = jnp.max(logits, axis=0, keepdims=True)
+        e = jnp.exp(logits - top)
+        total = jnp.sum(e, axis=0, keepdims=True)
+        picked = jnp.sum(logits * hot, axis=0, keepdims=True)
+        out_l[0:1, :] += fold(
+            scale_t * label * (jnp.log(total) + top - picked)
+            + scale_r * jnp.sum(fmask * err * err, axis=0, keepdims=True)
+        )
+        g_log = scale_t * label * (e / total - hot)
+        g_rec = scale_r * fmask * 2.0 * err
+        gho = jnp.concatenate([g_log, g_rec, jnp.zeros((8, 256), f32)], axis=0).astype(bf16)
+        gho_s[:, at] = gho
+        g_final = nn(wh_s[:, :32], gho)
+        acc_gain[D : 2 * D, :] += fold(g_final * normed)
+        g_res = norm_back_t(g_final, normed, inverse, gain_out(256))
+        gres[:, at] = g_res
+        gb = g_res.astype(bf16)
+        gb_s[:, at] = gb
+        ga = nn(w_s[:, 3 * D : 4 * D], gb).astype(bf16).astype(f32)
+        attf = attended.astype(f32)
+        for h in range(H):
+            rows = slice(32 * h, 32 * h + 32)
+            da = (ga[rows] * il_s[h : h + 1, at]).astype(bf16)
+            dap[rows, at] = da
+            dneg[h : h + 1, at] = -jnp.sum(da.astype(f32) * attf[rows], axis=0, keepdims=True)
+        return carry
+
+    lax.fori_loop(0, qs // 256, mid_block, 0)
+
+    zero_p = jnp.zeros((64, 256), bf16)
+
+    def backward_chunk(at, c, e_of):
+        keys = pl.ds(pl.multiple_of(c * KC, KC), KC)
+        dks, dvs, dqs = [], [], []
+        ds_all, e_all, qd_all, da_all = [], [], [], []
+        for p in range(4):
+            e = e_of(p)
+            da = jnp.concatenate(diagonal(dap, at, p), axis=0)
+            qd = jnp.concatenate(diagonal(q_s, at, p), axis=0)
+            neg = jnp.concatenate(
+                [dneg[2 * p : 2 * p + 1, at], dneg[2 * p + 1 : 2 * p + 2, at]], axis=1
+            )
+            neg_hi = neg.astype(bf16).astype(f32)
+            r16 = iota((16, 256), 0)
+            tail = jnp.where(r16 == 0, neg_hi, jnp.where(r16 == 1, neg - neg_hi, 0.0)).astype(bf16)
+            operand = jnp.concatenate([da, tail, jnp.zeros((48, 256), bf16)], axis=0)
+            dp = nn(vaug[keys, pair(p, 128)], operand)
+            ds = (e.astype(f32) * dp).astype(bf16)
+            dq = nn(kt_s[64 * p : 64 * p + 64, keys], ds)
+            dq_s[64 * p : 64 * p + 32, at] += dq[0:32, :128]
+            dq_s[64 * p + 32 : 64 * p + 64, at] += dq[32:64, 128:]
+            order = (lambda v: [v, zero_p]) if p % 2 == 0 else (lambda v: [zero_p, v])
+            dvs.append(nt(e, jnp.concatenate(order(da), axis=0)))
+            dks.append(nt(ds, jnp.concatenate(order(qd), axis=0)))
+        for half in range(2):
+            lanes = slice(128 * half, 128 * half + 128)
+            gk[keys, lanes] += dks[2 * half] + dks[2 * half + 1]
+            gv[keys, lanes] += dvs[2 * half] + dvs[2 * half + 1]
+
+    def backward_block(i, carry):
+        at = pl.ds(pl.multiple_of(i * QB, QB), QB)
+        c0, nc, tile0 = blk_c0[i], blk_nc[i], blk_tile[i]
+        simple = (nc == 1) & (tile0 < E_CAP)
+
+        @pl.when(simple)
+        def one():
+            backward_chunk(at, c0, lambda p: ebuf[tile0, :, pair(p, 256)])
+
+        @pl.when(jnp.logical_not(simple))
+        def many():
+            def one_chunk(c, inner):
+                @pl.when(tile0 + c < E_CAP)
+                def kept():
+                    ecur[...] = ebuf[tile0 + c]
+
+                @pl.when(tile0 + c >= E_CAP)
+                def again():
+                    keys = pl.ds(pl.multiple_of((c0 + c) * KC, KC), KC)
+                    for p in range(4):
+                        s = nn(kaug[keys, pair(p, 128)], score_operand(at, p))
+                        ecur[:, pair(p, 256)] = jnp.exp2(
+                            s - m_s[i, :, pair(p, 256)]
+                        ).astype(bf16)
+
+                backward_chunk(at, c0 + c, lambda p: ecur[:, pair(p, 256)])
+                return inner
+
+            lax.fori_loop(0, nc, one_chunk, 0)
+
+        return carry
+
+    lax.fori_loop(0, num_blocks, backward_block, 0)
+
+    def sum_in(grad, normed, kept, lanes):
+        by_feature = jnp.concatenate(
+            [kept[f : f + 1] * grad[32 * f : 32 * f + 32] for f in range(F)], axis=0
+        )
+        outs = []
+        for v in (by_feature, grad):
+            total = v[:, :128]
+            for k in range(1, lanes // 128):
+                total = total + v[:, 128 * k : 128 * k + 128]
+            outs.append(total)
+        return outs
+
+    def post_block(j, carry):
+        at = pl.ds(pl.multiple_of(j * 256, 256), 256)
+        kept = xs[:, at] * (1.0 - fs[:, at])
+        hidden = embed_t(kept, emb_w(256), emb_b(256))
+        normed, inverse = norm_t(hidden)
+        dq = dq_s[:, at]
+        gq = (dq * coef2).astype(bf16)
+        prod = fold(dq * q_s[:, at].astype(f32))
+        for h in range(H):
+            acc_gain[4 * D + h : 4 * D + h + 1, :] += jnp.sum(
+                prod[32 * h : 32 * h + 32], axis=0, keepdims=True
+            )
+        gqkv[:, 0:D] += nt(qn_s[:, at], gq)
+        gqn = nn(w_s[:, 0:D], gq)
+        acc_gain[0:D, :] += fold(gqn * normed)
+        gh = gres[:, at] + norm_back_t(gqn, normed, inverse, gain_in(256))
+        by_f, plain = sum_in(gh, normed, kept, 256)
+        acc_gain[2 * D : 3 * D, :] += by_f
+        acc_gain[3 * D : 4 * D, :] += plain
+        return carry
+
+    gqkv[...] = jnp.zeros_like(gqkv)
+    lax.fori_loop(0, qs // 256, post_block, 0)
+    gout[...] = nt(att[...], gb_s[...])
+    ghead[...] = nt(fn_s[...], gho_s[...])
+
+    def mem_back(c, carry):
+        at = pl.ds(pl.multiple_of(c * KC, KC), KC)
+        live = ((iota((KC, 1), 0) + c * KC) < ch_end[c]).astype(f32)
+        coef_lane = carry
+        gk_c = (gk[at, :] * coef_lane * live).astype(bf16)
+        gv_c = (gv[at, :] * live).astype(bf16)
+        mn = mnt[:, at]
+        gqkv[:, D : 2 * D] += nn(mn, gk_c)
+        gqkv[:, 2 * D : 3 * D] += nn(mn, gv_c)
+        gmn = nt(w_s[:, D : 2 * D], gk_c) + nt(w_s[:, 2 * D : 3 * D], gv_c)
+        feats_c = mfeat[:, at]
+        hidden = embed_t(feats_c, emb_w(KC), emb_b(KC))
+        normed, inverse = norm_t(hidden)
+        dgain = gmn * normed
+        acc_gain[0:D, :] += dgain[:, :128] + dgain[:, 128:256] + dgain[:, 256:384]
+        gm = norm_back_t(gmn, normed, inverse, gain_in(KC))
+        by_f, plain = sum_in(gm, normed, feats_c, KC)
+        acc_gain[2 * D : 3 * D, :] += by_f
+        acc_gain[3 * D : 4 * D, :] += plain
+        return carry
+
+    coef_lane = jnp.concatenate([coefb[0:128, :].T[0:1], coefb[128:256, :].T[0:1]], axis=1)
+    lax.fori_loop(0, num_chunks, mem_back, coef_lane)
+
+    sums = jnp.sum(acc_gain[...], axis=1, keepdims=True)
+    small = jnp.concatenate(
+        [
+            sums[2 * D : 3 * D],
+            sums[3 * D : 4 * D],
+            sums[0:D],
+            sums[D : 2 * D],
+            sums[4 * D : 4 * D + H] * (32 ** (-0.5)),
+            jnp.zeros((H, 1), f32),
+        ],
+        axis=0,
+    )
+    placed = jnp.where(lan == (row - per_small * row_dev), small, 0.0).astype(bf16)
+    r_dev = iota((n, used), 0)
+    r_row = iota((n, used), 1)
+    mine = (r_row >= per_small * r_dev) & (r_row < per_small * r_dev + per_small)
+    small_rows_out = nn(mine.astype(f32).astype(bf16), placed)
+    to_flat_r = iota((32, 256), 0)
+    to_flat_l = iota((32, 256), 1)
+    lane_row = jnp.floor((to_flat_l.astype(f32) + 0.5) * (1.0 / (C + F))).astype(jnp.int32)
+    to_flat = ((to_flat_l - (C + F) * lane_row == to_flat_r) & (to_flat_r < C + F)).astype(f32)
+    spread_h = nn(ghead[...].astype(bf16), to_flat.astype(bf16))
+    lr = iota((D, 256), 1)
+    lr_row = jnp.floor((lr.astype(f32) + 0.5) * (1.0 / (C + F))).astype(jnp.int32)
+    spread_h = jnp.where(lr_row == (iota((D, 256), 0) & (rows_dev - 1)), spread_h, 0.0)
+    r8 = iota((8, 128), 0)
+    for d in range(n):
+        rows = slice(rows_dev * d, rows_dev * d + rows_dev)
+        head_flat = jnp.sum(spread_h[rows], axis=0, keepdims=True)
+        extra = jnp.where(
+            r8 == 0,
+            head_flat[:, :128],
+            jnp.where(r8 == 1, head_flat[:, 128:], jnp.where(r8 == 2, small_rows_out[d : d + 1], 0.0)),
+        )
+        block = [gqkv[rows, 128 * k : 128 * k + 128] for k in range(6)]
+        block += [gout[rows, 128 * k : 128 * k + 128] for k in range(2)]
+        block += [extra, jnp.zeros((8, 128), f32)]
+        out_s[place_of(d, planes)] = jnp.concatenate(block, axis=0).astype(bf16)
+
+
+def step_call(n, small_size, qf, fm, qt, tc, tm, mt, mm, an, gw, gf):
+    num_q, num_mem = qf.shape[1], mt.shape[1]
+    q_blocks, k_chunks = sizes(n, num_q, num_mem)
+    qs, ks = q_blocks * QB, k_chunks * KC
+    V = pltpu.VMEM
+    S = pltpu.SMEM
+    vm = pl.BlockSpec(memory_space=pltpu.VMEM)
+    scratch = [
+        V((D, 4 * D), bf16), V((4 * D, D), bf16), V((D, 128), bf16), V((32, D), bf16),
+        V((D, 512), bf16), V((D, 512), bf16),
+        V((4 * D, 128), f32), V((D, 128), f32),
+        V((1, num_q), f32), V((1, num_mem), f32), V((8, qs), f32), V((8, qs), f32), V((8, qs), f32),
+        V((32, num_mem), bf16), V((8, ks), f32),
+        V((ks, 512), bf16), V((ks, 512), bf16), V((D, ks), bf16), V((4 * VROWS, ks), bf16),
+        V((D, ks), bf16), V((ks, D), f32), V((ks, D), f32),
+        V((D, qs), bf16), V((D, qs), bf16), V((D, qs), bf16), V((D, qs), bf16), V((D, qs), bf16),
+        V((H, qs), f32), V((D, qs), f32), V((D, qs), bf16), V((32, qs), bf16), V((D, qs), bf16),
+        V((D, qs), bf16), V((H, qs), f32), V((D, qs), f32), V((8, qs), f32),
+        V((E_CAP + 1, KC, 1024), bf16), V((8, 128), f32), V((KC, 1024), bf16),
+        V((4 * VROWS, 256), f32), V((q_blocks, 1, 1024), f32),
+        V((4 * D + H, 128), f32), V((D, 3 * D), f32), V((D, D), f32), V((D, 32), f32),
+        S((q_blocks,), jnp.int32), S((q_blocks,), jnp.int32), S((q_blocks,), jnp.int32),
+        S((k_chunks,), jnp.int32), S((k_chunks,), jnp.int32),
+    ]
+    return pl.pallas_call(
+        functools.partial(step_kernel, n, num_q, num_mem, small_size),
+        out_shape=(
+            jax.ShapeDtypeStruct((n, 80, 128), bf16),
+            jax.ShapeDtypeStruct((8, 128), f32),
+        ),
+        in_specs=[vm] * 7 + [pl.BlockSpec(memory_space=pltpu.SMEM)] + [vm] * 2,
+        out_specs=(vm, vm),
+        scratch_shapes=scratch,
+        compiler_params=pltpu.CompilerParams(vmem_limit_bytes=58 * 1024 * 1024),
+    )(qf, fm, qt, tc, tm, mt, mm, an, gw, gf)
+
+
+MESH = pl.DeviceIdType.MESH
+
+
+def greet(targets):
+    barrier = pltpu.get_barrier_semaphore()
+    for target in targets:
+        pl.semaphore_signal(barrier, inc=1, device_id=(target,), device_id_type=MESH)
+    return barrier
+
+
+def send(src, dst, send_sem, recv_sem, target):
+    copy = pltpu.make_async_remote_copy(
+        src_ref=src,
+        dst_ref=dst,
+        send_sem=send_sem,
+        recv_sem=recv_sem,
+        device_id=(target,),
+        device_id_type=MESH,
+    )
+    copy.start()
+    return copy
+
+
+def where_am_i(planes):
+    me = lax.axis_index("mem")
+    core = lax.rem(me, 2)
+    square = lax.rem(lax.div(me, 2), 4)
+    plane = lax.div(me, 8)
+    return me, core, square, plane
+
+
+def gather_kernel(
+    n, w_qkv, w_out, w_heads, w_small, mfeat, fm, tm, gw, gf,
+    send_z, recv_z, send_s, recv_s, send_c, recv_c,
+):
+    planes = n // 8
+    me, core, square, plane = where_am_i(planes)
+    in_plane = core + 2 * square
+    z_of = [lax.rem(plane + k, planes) * 8 + in_plane for k in range(1, planes)]
+    s_of = [plane * 8 + lax.rem(square + k, 4) * 2 + core for k in range(1, 4)]
+    c_of = plane * 8 + square * 2 + (1 - core)
+    barrier = greet(z_of + s_of + [c_of])
+
+    place = core * (4 * planes) + square * planes + plane
+    rows = []
+    for c in range(6):
+        rows.append(w_qkv[pl.ds(c, 8, stride=6), :])
+    for c in range(2):
+        rows.append(w_out[pl.ds(c, 8, stride=2), :])
+    gw[place] = jnp.concatenate(rows, axis=0).astype(bf16)
+    per_head = w_heads.shape[1]
+    lane = iota((8, 256), 1)
+    head_row = jnp.concatenate([w_heads[...], jnp.zeros((1, 256 - per_head), f32)], axis=1)
+    owner = jnp.floor((lane.astype(f32) + 0.5) * (1.0 / (C + F))).astype(jnp.int32)
+    kept_heads = jnp.where(owner == iota((8, 256), 0), head_row, 0.0).astype(bf16)
+    fold_r = iota((256, 128), 0)
+    fold_row = jnp.floor((fold_r.astype(f32) + 0.5) * (1.0 / (C + F))).astype(jnp.int32)
+    fold_m = (fold_r - (C + F) * fold_row == iota((256, 128), 1) - 64).astype(f32).astype(bf16)
+    heads = nn(kept_heads, fold_m)
+    per_small = w_small.shape[1]
+    small = jnp.concatenate([w_small[...], jnp.zeros((1, 128 - per_small), f32)], axis=1)
+    small = pltpu.roll(jnp.broadcast_to(small, (8, 128)), SMALL_LANE, 1)
+    feats = jnp.concatenate([mfeat[...], jnp.zeros((8, 64), f32)], axis=1)
+    lane8 = iota((8, 128), 1)
+    row8 = iota((8, 128), 0)
+    num_t = jnp.sum(tm[...].astype(f32), axis=1, keepdims=True)
+    num_r = jnp.sum(jnp.sum(fm[...].astype(f32), axis=0, keepdims=True), axis=1, keepdims=True)
+    block = feats + heads
+    first = (row8 == 0) & (lane8 >= SMALL_LANE) & (lane8 < SMALL_LANE + per_small)
+    block = jnp.where(first, small, block)
+    block = jnp.where((row8 == 0) & (lane8 == COUNT_LANE), num_t, block)
+    block = jnp.where((row8 == 0) & (lane8 == COUNT_LANE + 1), num_r, block)
+    gf[place] = block
+
+    pl.semaphore_wait(barrier, planes - 1 + 4)
+    copies = []
+    for k in range(planes - 1):
+        for i, ref in enumerate((gf, gw)):
+            copies.append(
+                send(ref.at[place], ref.at[place], send_z.at[i, k], recv_z.at[i, k], z_of[k])
+            )
+    for copy in copies:
+        copy.wait_recv()
+    done = list(copies)
+    line = pl.ds(core * (4 * planes) + square * planes, planes)
+    copies = []
+    for k in range(3):
+        for i, ref in enumerate((gf, gw)):
+            copies.append(
+                send(ref.at[line], ref.at[line], send_s.at[i, k], recv_s.at[i, k], s_of[k])
+            )
+    for copy in copies:
+        copy.wait_recv()
+    done += copies
+    half = pl.ds(core * (4 * planes), 4 * planes)
+    copies = []
+    for i, ref in enumerate((gf, gw)):
+        copies.append(send(ref.at[half], ref.at[half], send_c.at[i], recv_c.at[i], c_of))
+    for copy in copies:
+        copy.wait_recv()
+    done += copies
+    for copy in done:
+        copy.wait_send()
+
+
+def gather_call(n, w_qkv, w_out, w_heads, w_small, mfeat, fm, tm):
+    planes = n // 8
+    vm = pl.BlockSpec(memory_space=pltpu.VMEM)
+    dma = pltpu.SemaphoreType.DMA
+    return pl.pallas_call(
+        functools.partial(gather_kernel, n),
+        out_shape=(
+            jax.ShapeDtypeStruct((n, 64, 128), bf16),
+            jax.ShapeDtypeStruct((n, 8, 128), f32),
+        ),
+        in_specs=[vm] * 7,
+        out_specs=(vm, vm),
+        scratch_shapes=[
+            dma((2, planes - 1)), dma((2, planes - 1)), dma((2, 3)), dma((2, 3)), dma((2,)), dma((2,)),
+        ],
+        compiler_params=pltpu.CompilerParams(collective_id=0, has_side_effects=True),
+    )(w_qkv, w_out, w_heads, w_small, mfeat, fm, tm)
+
+
+def reduce_kernel(
+    n, s_in, l_in, g_out, t_out,
+    r_core, r_square, r_plane, t_square, t_plane, own, n_mine, n_square, n_sum, n_plane,
+    send_c, recv_c, send_s, recv_s, send_z, recv_z, send_n, recv_n, send_m, recv_m,
+):
+    planes = n // 8
+    me, core, square, plane = where_am_i(planes)
+    in_plane = core + 2 * square
+    p_of = [plane * 8 + lax.rem(in_plane + k, 8) for k in range(1, 8)]
+    z_of = [lax.rem(plane + k, planes) * 8 + in_plane for k in range(1, planes)]
+    s_of = [plane * 8 + lax.rem(square + k, 4) * 2 + core for k in range(1, 4)]
+    c_of = plane * 8 + square * 2 + (1 - core)
+    barrier = greet(p_of + z_of)
+    pl.semaphore_wait(barrier, planes - 1 + 7)
+
+    lines = 4 * planes
+    done = []
+    copy = send(s_in.at[pl.ds((1 - core) * lines, lines)], r_core, send_c, recv_c, c_of)
+    done.append(copy)
+    copy.wait_recv()
+    copies = []
+    for k in range(1, 4):
+        line = lax.rem(square + k, 4) * planes
+        for z in range(planes):
+            t_square[k - 1, z] = (
+                s_in[core * lines + line + z].astype(f32) + r_core[line + z].astype(f32)
+            ).astype(bf16)
+        copies.append(
+            send(t_square.at[k - 1], r_square.at[k - 1], send_s.at[k - 1], recv_s.at[k - 1], s_of[k - 1])
+        )
+    line = square * planes
+    for z in range(planes):
+        own[z] = s_in[core * lines + line + z].astype(f32) + r_core[line + z].astype(f32)
+    for copy in copies:
+        copy.wait_recv()
+    done += copies
+    copies = []
+    for k in range(1, planes):
+        z = lax.rem(plane + k, planes)
+        total = own[z]
+        for j in range(3):
+            total = total + r_square[j, z].astype(f32)
+        t_plane[k - 1] = total.astype(bf16)
+        copies.append(
+            send(t_plane.at[k - 1], r_plane.at[k - 1], send_z.at[k - 1], recv_z.at[k - 1], z_of[k - 1])
+        )
+    total = own[plane]
+    for j in range(3):
+        total = total + r_square[j, plane].astype(f32)
+    for copy in copies:
+        copy.wait_recv()
+    done += copies
+    for k in range(planes - 1):
+        total = total + r_plane[k].astype(f32)
+    g_out[...] = total
+    squares = jnp.sum(total * total, axis=0, keepdims=True)
+    row8 = iota((8, 128), 0)
+    n_mine[...] = jnp.where(row8 == 0, squares, jnp.where(row8 == 1, l_in[0:1, :], 0.0))
+    copies = []
+    for k in range(7):
+        copies.append(send(n_mine, n_square.at[k], send_n.at[k], recv_n.at[k], p_of[k]))
+    for copy in copies:
+        copy.wait_recv()
+    done += copies
+    total = n_mine[...]
+    for k in range(7):
+        total = total + n_square[k]
+    n_sum[...] = total
+    copies = []
+    for k in range(planes - 1):
+        copies.append(send(n_sum, n_plane.at[k], send_m.at[k], recv_m.at[k], z_of[k]))
+    for copy in copies:
+        copy.wait_recv()
+    done += copies
+    parts = jnp.zeros((8, 128), f32)
+    total = n_sum[...]
+    for k in range(planes - 1):
+        total = total + n_plane[k]
+    t_out[...] = total
+    for copy in done:
+        copy.wait_send()
+
+
+def reduce_call(n, s_in, l_in):
+    planes = n // 8
+    rows = s_in.shape[1]
+    vm = pl.BlockSpec(memory_space=pltpu.VMEM)
+    dma = pltpu.SemaphoreType.DMA
+    V = pltpu.VMEM
+    z = planes - 1
+    return pl.pallas_call(
+        functools.partial(reduce_kernel, n),
+        out_shape=(
+            jax.ShapeDtypeStruct((rows, 128), f32),
+            jax.ShapeDtypeStruct((8, 128), f32),
+        ),
+        in_specs=[vm] * 2,
+        out_specs=(vm, vm),
+        scratch_shapes=[
+            V((4 * planes, rows, 128), bf16), V((3, planes, rows, 128), bf16), V((z, rows, 128), bf16),
+            V((3, planes, rows, 128), bf16), V((z, rows, 128), bf16), V((planes, rows, 128), f32),
+            V((8, 128), f32), V((7, 8, 128), f32), V((8, 128), f32), V((z, 8, 128), f32),
+            dma, dma, dma((3,)), dma((3,)), dma((z,)), dma((z,)), dma((7,)), dma((7,)), dma((z,)), dma((z,)),
+        ],
+        compiler_params=pltpu.CompilerParams(collective_id=1, has_side_effects=True),
+    )(s_in, l_in)
+
+
+def update_kernel(g, tot, *refs):
+    weights, firsts, seconds = refs[0:4], refs[4:8], refs[8:12]
+    new, first_o, second_o, copy_o = refs[12:16], refs[16:20], refs[20:24], refs[24:28]
+    loss_o, norm_o, gq_s, go_s = refs[28:32]
+    for c in range(6):
+        gq_s[pl.ds(c, 8, stride=6), :] = g[8 * c : 8 * c + 8, :]
+    for c in range(2):
+        go_s[pl.ds(c, 8, stride=2), :] = g[48 + 8 * c : 56 + 8 * c, :]
+    norm = jnp.sqrt(jnp.sum(tot[0:1, :], axis=1, keepdims=True))
+    loss_o[...] = jnp.sum(tot[1:2, :], axis=1, keepdims=True)
+    norm_o[...] = norm
+    factor = jnp.minimum(1.0, max_norm / (norm + 1e-06))
+    per_head, per_small = weights[2].shape[1], weights[3].shape[1]
+    grads = (
+        gq_s[...],
+        go_s[...],
+        jnp.concatenate([g[64:65, :], g[65:66, : per_head - 128]], axis=1),
+        g[66:67, :per_small],
+    )
+    for i in range(4):
+        first_new, second_new, weight_new = adamw(
+            weights[i][...], firsts[i][...], seconds[i][...], grads[i], factor, float(STEP), learn_rates[i]
+        )
+        new[i][...] = weight_new
+        first_o[i][...] = first_new
+        second_o[i][...] = second_new
+        copy_o[i][...] = weight_new.astype(bf16)
+
+
+def update_call(g, tot, weights, firsts, seconds):
+    vm = pl.BlockSpec(memory_space=pltpu.VMEM)
+    shapes = [w.shape for w in weights]
+    outs = [jax.ShapeDtypeStruct(s, f32) for s in shapes] * 3
+    outs += [jax.ShapeDtypeStruct(s, bf16) for s in shapes]
+    outs += [jax.ShapeDtypeStruct((1, 1), f32)] * 2
+    return pl.pallas_call(
+        update_kernel,
+        out_shape=tuple(outs),
+        in_specs=[vm] * 14,
+        out_specs=(vm,) * 18,
+        scratch_shapes=[pltpu.VMEM((48, 128), f32), pltpu.VMEM((16, 128), f32)],
+    )(g, tot, *weights, *firsts, *seconds)
+
+
+def local_fast(
+    n, query_feats, feature_mask, query_task, target_class, target_mask, memory_feats, memory_task,
+    memory_mask, anneal, w_qkv, w_out, w_heads, w_small, m_qkv, m_out, m_heads, m_small,
+    v_qkv, v_out, v_heads, v_small,
+):
+    def row(v):
+        return v.reshape(1, -1)
+
+    def tiles(v):
+        return v.reshape(-1, 128)
+
+    fm = feature_mask.T
+    tm = row(target_mask)
+    weights = (tiles(w_qkv), tiles(w_out), row(w_heads), row(w_small))
+    firsts = (tiles(m_qkv), tiles(m_out), row(m_heads), row(m_small))
+    seconds = (tiles(v_qkv), tiles(v_out), row(v_heads), row(v_small))
+    gw, gf = gather_call(n, *weights, memory_feats.T, fm, tm)
+    pieces, losses = step_call(
+        n, w_small.shape[0] * n, query_feats.T, fm, row(query_task), row(target_class), tm,
+        row(memory_task), row(memory_mask), anneal, gw, gf.reshape(n * 8, 128),
+    )
+    grads, totals = reduce_call(n, pieces, losses)
+    outs = update_call(grads, totals, weights, firsts, seconds)
+    return tuple(out.reshape(-1) for out in outs)
+
+
 def solution(mesh):
     placed = (
         P("mem", None),
@@ -349,8 +1271,15 @@
         P("mem"),
         P("mem"),
     )
+    n = mesh.shape["mem"]
+
+    def choose(*args):
+        if D // n == 8 and args[6].shape[0] <= 4096:
+            return local_fast(n, *args)
+        return local(*args)
+
     return jax.shard_map(
-        local,
+        choose,
         mesh=mesh,
         in_specs=placed,
         out_specs=(

time: 773 us -> 101 us (0.13); the launches traced: 763 us -> 100 us
  blocking collectives: 236 us -> 0 us
  waiting for transfers between devices: 224 us -> 0 us
  matrix products: 180 us -> 0 us
  Pallas kernels: 0 us -> 97.7 us
  local copies, waits for them, and re-layouts: 49.9 us -> 0.66 us
  other arithmetic: 47.9 us -> 0.53 us
  between operations: 24.2 us -> 1.33 us
    dot_general x44 -> x0, matrix products: 180 us -> none  [the longest x4 50.8 us: back_step(): jnp.einsum('qhd,khd->hqk', grad_attn, value_block, preferred_element_type...]
    reduce_scatter x1 -> x0, waiting for transfers between devices: 128 us -> none  [local(): lax.psum_scatter(kv_parts.reshape(memory_rows, 2 * D), 'mem', scatter_dim...]
    pallas_call x0 -> x4, Pallas kernels: none -> 97.7 us  [the longest x1 51.7 us: step_call(): pl.pallas_call(functools.partial(step_kernel, n, num_q, num_mem, small_si...]
    unnamed x4 -> x0, waiting for transfers between devices: 87.1 us -> none
    unnamed x2 -> x0, blocking collectives: 79.6 us -> none
    all_gather x2 -> x0, blocking collectives: 78.5 us -> none  [the longest x1 41.3 us: local(): lax.all_gather(w_qkv, 'mem', axis=0, tiled=True)]
    psum x2 -> x0, blocking collectives: 78.2 us -> none  [the longest x1 39.5 us: local(): grad_total = jnp.sqrt(lax.psum(local_squares, 'mem'))]
    reduce_sum x18 -> x0, other arithmetic: 26.7 us -> none  [the longest x4 17.1 us: stats_step(): jnp.sum(shifted, -1)]
  transfers between devices with their start and end apart: 3 -> 0, of which waited for: 3 -> 0; matrix products, arithmetic and copies ran while one was open for 3% -> 0% of each run, Pallas kernels for 0% -> 0%
where the time goes in v1:
time: 101 us; the launch traced here: 100 us
  Pallas kernels  97.7 us (97%)
  between operations  1.33 us (1%)
    pallas_call x1, Pallas kernels, step_call(): pl.pallas_call(functools.partial(step_kernel, n, num_q, num_mem, small_si...  51.7 us
    pallas_call x1, Pallas kernels, reduce_call(): pl.pallas_call(functools.partial(reduce_kernel, n), out_shape=(jax.ShapeD...  27.9 us
    pallas_call x1, Pallas kernels, gather_call(): pl.pallas_call(functools.partial(gather_kernel, n), out_shape=(jax.ShapeD...  16.3 us

profile of v1, /device:TPU:0, one launch (start us, length us, event | category | flops | bytes accessed | tf_op | source)
XLA Modules:
  0.0 100.2 jit_solution(10690874325371701518)
XLA Ops:
  1.3 16.3 %shard_map.340 = (bf16[32,64,128]{2,1,0:T(8,128)(2,1)}, f32[32,8,128]{2,1,0:T(8,128)}) custom-call(f32[48,128]{1,0:T(8,128)} %bitcast.41, f32[16,128]{1,0:T(8,128)} %bitcast.44, f32[1,192]{1,0:T(1,128)} %bitcast.56, f32[1,33]{1,0:T(1,128)} %bitcast.59, f32[8,64]{1,0:T(8,128)} %bitcast.58, s32[8,1024]{1,0:T(8,128)} %bitcast.39, s32[1,1024]{1,0:T(1,128)} %bitcast.48), custom_call_target="tpu_custom_call" | custom-call | tf_op jit(solution)/shard_map/pallas_call | solution.py:1057
  17.6 51.7 %shard_map.341 = (bf16[32,80,128]{2,1,0:T(8,128)(2,1)}, f32[8,128]{1,0:T(8,128)}) custom-call(f32[8,1024]{1,0:T(8,128)} %bitcast.43, s32[8,1024]{1,0:T(8,128)} %bitcast.40, s32[1,1024]{1,0:T(1,128)} %bitcast.54, s32[1,1024]{1,0:T(1,128)} %bitcast.55, s32[1,1024]{1,0:T(1,128)} %bitcast.49, s32[1,2048]{1,0:T(1,128)} %bitcast.50, s32[1,2048]{1,0:T(1,128)} %bitcast.51, ...), custom_call_target="tpu_custom_call" | custom-call | tf_op jit(solution)/shard_map/pallas_call | solution.py:935
  69.3 27.9 %shard_map.342 = (f32[80,128]{1,0:T(8,128)}, f32[8,128]{1,0:T(8,128)}) custom-call(bf16[32,80,128]{2,1,0:T(8,128)(2,1)} %get-tuple-element.44.s_in, f32[8,128]{1,0:T(8,128)} %get-tuple-element.45.l_in), custom_call_target="tpu_custom_call" | custom-call | tf_op jit(solution)/shard_map/pallas_call | solution.py:1162
  97.2 1.8 %shard_map.343 = (f32[48,128]{1,0:T(8,128)}, f32[16,128]{1,0:T(8,128)}, f32[1,192]{1,0:T(1,128)}, f32[1,33]{1,0:T(1,128)}, f32[48,128]{1,0:T(8,128)}, /*index=5*...) custom-call(f32[80,128]{1,0:T(8,128)} %get-tuple-element.46.g, ...), custom_call_target="tpu_custom_call" | custom-call | tf_op jit(solution)/shard_map/pallas_call | solution.py:1215
  99.0 0.0 copy-start
  99.0 0.7 copy-done
  99.7 0.5 reduce
Async XLA Ops:
  99.0 0.7 copy-start

commit v2 on v1

v2 whole, which is shorter than its diff:
```python
import functools
import math

import jax
import jax.numpy as jnp
from jax import lax
from jax.experimental import pallas as pl
from jax.experimental.pallas import tpu as pltpu
from jax.sharding import PartitionSpec as P

F = 8
D = 256
H = 8
C = 16
TASKS = 4
STEP = 10


eps_norm = 1e-05
max_norm = 0.05
beta_one = 0.9
beta_two = 0.999
adam_eps = 1e-08
decay_rate = 0.01
learn_rates = (0.05, 1.0, 0.05, 0.5)
masked_score = -1e30


def embed(feature_rows, table_flat, emb_bias):
    emb_table = table_flat.reshape(feature_rows.shape[1], -1)
    return (feature_rows[:, :, None] * emb_table[None]).reshape(
        feature_rows.shape[0], -1
    ) + emb_bias


def standard(hidden):
    centred = hidden - jnp.mean(hidden, -1, keepdims=True)
    inverse = lax.rsqrt(jnp.mean(centred * centred, -1, keepdims=True) + eps_norm)
    return (centred * inverse, inverse)


def norm_back(grad_out, hidden, gain_vec):
    normed, inverse = standard(hidden)
    grad_gain = jnp.sum(grad_out * normed, 0)
    grad_scaled = grad_out * gain_vec
    grad_hidden = inverse * (
        grad_scaled
        - jnp.mean(grad_scaled, -1, keepdims=True)
        - normed * jnp.mean(grad_scaled * normed, -1, keepdims=True)
    )
    return (grad_hidden, grad_gain)


def split_pair(values):
    upper = values.astype(jnp.bfloat16)
    lower = (values - upper.astype(jnp.float32)).astype(jnp.bfloat16)
    return (upper, lower)


def adamw(weight, first_mom, second, grad_in, factor, step_num, step_rate):
    clipped = grad_in * factor
    first_new = beta_one * first_mom + (1 - beta_one) * clipped
    second_new = beta_two * second + (1 - beta_two) * clipped * clipped
    fix_one = 1 - beta_one**step_num
    fix_two = 1 - beta_two**step_num
    weight_new = weight - step_rate * (
        first_new / fix_one / (jnp.sqrt(second_new / fix_two) + adam_eps) + decay_rate * weight
    )
    return (first_new, second_new, weight_new)


def local(
    query_feats,
    feature_mask,
    query_task,
    target_class,
    target_mask,
    memory_feats,
    memory_task,
    memory_mask,
    anneal,
    w_qkv,
    w_out,
    w_heads,
    w_small,
    m_qkv,
    m_out,
    m_heads,
    m_small,
    v_qkv,
    v_out,
    v_heads,
    v_small,
):
    high = lax.Precision.HIGHEST
    head_size = D // H
    full_qkv, full_out, full_heads, full_small = (
        lax.all_gather(w_qkv, "mem", axis=0, tiled=True),
        lax.all_gather(w_out, "mem", axis=0, tiled=True),
        lax.all_gather(w_heads, "mem", axis=0, tiled=True),
        lax.all_gather(w_small, "mem", axis=0, tiled=True),
    )
    emb_table = full_small[:D]
    emb_bias = full_small[D : 2 * D]
    gain_in = full_small[2 * D : 3 * D]
    gain_out = full_small[3 * D : 4 * D]
    score_coef = full_small[4 * D : 4 * D + H] * head_size ** (-0.5)
    qkv_low = full_qkv.reshape(D, 3 * D).astype(jnp.bfloat16)
    out_low = full_out.reshape(D, D).astype(jnp.bfloat16)
    heads_low = full_heads.reshape(D, C + F).astype(jnp.bfloat16)
    mem_hidden = embed(memory_feats, emb_table, emb_bias)
    mem_normed = (standard(mem_hidden)[0] * gain_in).astype(jnp.bfloat16)
    mem_kv = jnp.dot(mem_normed, qkv_low[:, D:], preferred_element_type=jnp.float32).astype(
        jnp.bfloat16
    )
    all_kv = lax.all_gather(mem_kv, "mem", axis=0, tiled=True)
    memory_rows = all_kv.shape[0]
    block_keys = math.gcd(memory_rows, 512)
    num_blocks = memory_rows // block_keys
    key_rows = all_kv[:, :D].reshape(num_blocks, block_keys, H, head_size)
    value_rows = all_kv[:, D:].reshape(num_blocks, block_keys, H, head_size)
    task_blocks = memory_task.reshape(num_blocks, block_keys)
    live_blocks = memory_mask.reshape(num_blocks, block_keys)
    key_blocks = (key_rows, value_rows, task_blocks, live_blocks)
    kept_input = query_feats * (1 - feature_mask).astype(jnp.float32)
    hidden_in = embed(kept_input, emb_table, emb_bias)
    query_normed = (standard(hidden_in)[0] * gain_in).astype(jnp.bfloat16)
    queries = (
        jnp.dot(query_normed, qkv_low[:, :D], preferred_element_type=jnp.float32)
        .astype(jnp.bfloat16)
        .reshape(-1, H, head_size)
    )
    num_rows = queries.shape[0]

    def allowed_of(task_row, live_row):
        return ((query_task[:, None] == task_row[None, :]) & (live_row[None, :] > 0))[None]

    def scores_of(key_block, allowed):
        raw_scores = jnp.einsum(
            "qhd,khd->hqk", queries, key_block, preferred_element_type=jnp.float32
        )
        return (
            raw_scores,
            jnp.where(allowed, score_coef[:, None, None] * raw_scores, masked_score),
        )

    def stats_step(state_in, block_data):
        row_top, row_sum = state_in
        key_block, value_block, task_row, live_row = block_data
        allowed = allowed_of(task_row, live_row)
        scores = scores_of(key_block, allowed)[1]
        new_top = jnp.maximum(row_top, jnp.max(scores, -1))
        shifted = jnp.where(allowed, jnp.exp(scores - new_top[..., None]), 0.0)
        return ((new_top, row_sum * jnp.exp(row_top - new_top) + jnp.sum(shifted, -1)), None)

    start_state = (
        jnp.full((H, num_rows), masked_score, jnp.float32),
        jnp.zeros((H, num_rows), jnp.float32),
    )
    (row_top, row_sum), unused = lax.scan(stats_step, start_state, key_blocks)

    def probs_of(scores, allowed):
        return jnp.where(allowed, jnp.exp(scores - row_top[..., None]), 0.0) / row_sum[..., None]

    def value_step(accum, block_data):
        key_block, value_block, task_row, live_row = block_data
        allowed = allowed_of(task_row, live_row)
        probs_low = probs_of(scores_of(key_block, allowed)[1], allowed).astype(jnp.bfloat16)
        return (
            accum
            + jnp.einsum(
                "hqk,khd->qhd", probs_low, value_block, preferred_element_type=jnp.float32
            ),
            None,
        )

    attn_sum, unused = lax.scan(
        value_step, jnp.zeros((num_rows, H, head_size), jnp.float32), key_blocks
    )
    attended = attn_sum.reshape(num_rows, D).astype(jnp.bfloat16)
    residual = hidden_in + jnp.dot(attended, out_low, preferred_element_type=jnp.float32)
    final_normed = (standard(residual)[0] * gain_out).astype(jnp.bfloat16)
    head_out = jnp.dot(final_normed, heads_low, preferred_element_type=jnp.float32)
    logits = head_out[:, :C]
    recon_err = head_out[:, C:] - query_feats
    label_mask = target_mask.astype(jnp.float32)
    feat_mask = feature_mask.astype(jnp.float32)
    onehot_class = jax.nn.one_hot(target_class, C, dtype=jnp.float32)
    picked = jnp.sum(logits * onehot_class, -1)
    sum_target, sum_recon, count_target, count_recon = lax.psum(
        (
            jnp.sum(label_mask * (jax.nn.logsumexp(logits, -1) - picked)),
            jnp.sum(feat_mask * recon_err**2),
            jnp.sum(label_mask),
            jnp.sum(feat_mask),
        ),
        "mem",
    )
    count_target = jnp.maximum(count_target, 1.0)
    count_recon = jnp.maximum(count_recon, 1.0)
    weight_a = anneal[0]
    loss_value = weight_a * sum_target / count_target + (1 - weight_a) * sum_recon / count_recon
    grad_logits = (
        weight_a / count_target * label_mask[:, None] * (jax.nn.softmax(logits, -1) - onehot_class)
    )
    grad_recon = (1 - weight_a) / count_recon * feat_mask * 2.0 * recon_err
    grad_head_out = jnp.concatenate([grad_logits, grad_recon], 1).astype(jnp.bfloat16)
    grad_heads = jnp.dot(final_normed.T, grad_head_out, preferred_element_type=jnp.float32)
    grad_final = jnp.dot(grad_head_out, heads_low.T, preferred_element_type=jnp.float32)
    grad_resid, grad_gain_out = norm_back(grad_final, residual, gain_out)
    grad_branch = grad_resid.astype(jnp.bfloat16)
    grad_wout = jnp.dot(attended.T, grad_branch, preferred_element_type=jnp.float32)
    grad_attn = (
        jnp.dot(grad_branch, out_low.T, preferred_element_type=jnp.float32)
        .astype(jnp.bfloat16)
        .reshape(num_rows, H, head_size)
    )
    row_delta = jnp.sum(
        grad_attn.astype(jnp.float32)
        * attended.reshape(num_rows, H, head_size).astype(jnp.float32),
        -1,
    ).T

    def back_step(state_in, block_data):
        key_block, value_block, task_row, live_row = block_data
        allowed = allowed_of(task_row, live_row)
        raw_scores, scores = scores_of(key_block, allowed)
        soft_probs = probs_of(scores, allowed)
        grad_probs = jnp.einsum(
            "qhd,khd->hqk", grad_attn, value_block, preferred_element_type=jnp.float32
        )
        grad_scores = (soft_probs * (grad_probs - row_delta[..., None])).astype(jnp.bfloat16)
        grad_beta = jnp.sum(grad_scores.astype(jnp.float32) * raw_scores, (1, 2))
        grad_query = jnp.einsum(
            "hqk,khd->qhd", grad_scores, key_block, preferred_element_type=jnp.float32
        )
        grad_key = (
            jnp.einsum("hqk,qhd->khd", grad_scores, queries, preferred_element_type=jnp.float32)
            * score_coef[None, :, None]
        )
        grad_value = jnp.einsum(
            "hqk,qhd->khd",
            soft_probs.astype(jnp.bfloat16),
            grad_attn,
            preferred_element_type=jnp.float32,
        )
        block_rows = key_block.shape[0]
        grad_kv = jnp.concatenate(
            [grad_key.reshape(block_rows, D), grad_value.reshape(block_rows, D)], 1
        )
        return ((state_in[0] + grad_query, state_in[1] + grad_beta), grad_kv)

    init_state = (jnp.zeros((num_rows, H, head_size), jnp.float32), jnp.zeros((H,), jnp.float32))
    (grad_q_sum, grad_beta_sum), kv_parts = lax.scan(back_step, init_state, key_blocks)
    kv_grad = lax.psum_scatter(
        kv_parts.reshape(memory_rows, 2 * D), "mem", scatter_dimension=0, tiled=True
    )
    grad_q_low = (grad_q_sum * score_coef[None, :, None]).reshape(num_rows, D).astype(jnp.bfloat16)
    grad_wq = jnp.dot(query_normed.T, grad_q_low, preferred_element_type=jnp.float32)
    grad_qn = jnp.dot(grad_q_low, qkv_low[:, :D].T, preferred_element_type=jnp.float32)
    grad_in_q, gain_in_q = norm_back(grad_qn, hidden_in, gain_in)
    grad_hidden = grad_resid + grad_in_q
    kv_upper, kv_lower = split_pair(kv_grad)
    grad_wkv = jnp.dot(mem_normed.T, kv_upper, preferred_element_type=jnp.float32) + jnp.dot(
        mem_normed.T, kv_lower, preferred_element_type=jnp.float32
    )
    grad_mn = jnp.dot(kv_upper, qkv_low[:, D:].T, preferred_element_type=jnp.float32) + jnp.dot(
        kv_lower, qkv_low[:, D:].T, preferred_element_type=jnp.float32
    )
    grad_mem, gain_in_m = norm_back(grad_mn, mem_hidden, gain_in)
    grad_table = jnp.einsum(
        "qf,qfe->fe", kept_input, grad_hidden.reshape(num_rows, F, -1), precision=high
    )
    grad_table = grad_table + jnp.einsum(
        "qf,qfe->fe", memory_feats, grad_mem.reshape(memory_feats.shape[0], F, -1), precision=high
    )
    grad_bias = jnp.sum(grad_hidden, 0) + jnp.sum(grad_mem, 0)
    small_size = full_small.shape[0]
    grad_small = jnp.concatenate(
        [
            grad_table.reshape(-1),
            grad_bias,
            gain_in_q + gain_in_m,
            grad_gain_out,
            grad_beta_sum * head_size ** (-0.5),
            jnp.zeros((small_size - 4 * D - H,), jnp.float32),
        ]
    )
    grad_qkv = jnp.concatenate([grad_wq, grad_wkv], 1).reshape(-1)
    shards = (
        lax.psum_scatter(grad_qkv, "mem", scatter_dimension=0, tiled=True),
        lax.psum_scatter(grad_wout.reshape(-1), "mem", scatter_dimension=0, tiled=True),
        lax.psum_scatter(grad_heads.reshape(-1), "mem", scatter_dimension=0, tiled=True),
        lax.psum_scatter(grad_small, "mem", scatter_dimension=0, tiled=True),
    )
    local_squares = sum((jnp.sum(piece_grad * piece_grad) for piece_grad in shards))
    grad_total = jnp.sqrt(lax.psum(local_squares, "mem"))
    factor = jnp.minimum(1.0, max_norm / (grad_total + 1e-06))
    step_num = float(STEP)
    weights_all = (w_qkv, w_out, w_heads, w_small)
    firsts = (m_qkv, m_out, m_heads, m_small)
    seconds = (v_qkv, v_out, v_heads, v_small)
    results = [
        adamw(weight, first_mom, second, grad_in, factor, step_num, step_rate)
        for weight, first_mom, second, grad_in, step_rate in zip(
            weights_all, firsts, seconds, shards, learn_rates
        )
    ]
    new_w = [entry[2] for entry in results]
    return (
        new_w[0],
        new_w[1],
        new_w[2],
        new_w[3],
        results[0][0],
        results[1][0],
        results[2][0],
        results[3][0],
        results[0][1],
        results[1][1],
        results[2][1],
        results[3][1],
        new_w[0].astype(jnp.bfloat16),
        new_w[1].astype(jnp.bfloat16),
        new_w[2].astype(jnp.bfloat16),
        new_w[3].astype(jnp.bfloat16),
        loss_value.reshape(1),
        grad_total.reshape(1),
    )


f32 = jnp.float32
bf16 = jnp.bfloat16
LOG2E = math.log2(math.e)
QB = 128
KC = 384
VROWS = 80
E_CAP = 16
SMALL_LANE = 88
COUNT_LANE = 122


def place_of(dev, planes):
    return (dev % 2) * (4 * planes) + ((dev // 2) % 4) * planes + dev // 8


def nt(a, b):
    return lax.dot_general(a, b, (((1,), (1,)), ((), ())), preferred_element_type=f32)


def tn(a, b):
    return lax.dot_general(a, b, (((0,), (0,)), ((), ())), preferred_element_type=f32)


def nn(a, b):
    return jnp.dot(a, b, preferred_element_type=f32)


def iota(shape, dim):
    return lax.broadcasted_iota(jnp.int32, shape, dim)


def split2(v):
    hi = v.astype(bf16).astype(f32)
    return hi, v - hi


def split3(v):
    hi, rest = split2(v)
    mid = rest.astype(bf16).astype(f32)
    return hi, mid, rest - mid


def wide(v, lanes):
    return jnp.concatenate([v] * (lanes // v.shape[1]), axis=1) if lanes > v.shape[1] else v


def embed_t(kept, table, bias):
    parts = []
    for f in range(F):
        rows = slice(32 * f, 32 * f + 32)
        parts.append(kept[f : f + 1] * table[rows] + bias[rows])
    return jnp.concatenate(parts, axis=0)


def norm_t(v):
    centred = v - jnp.mean(v, axis=0, keepdims=True)
    inverse = lax.rsqrt(jnp.mean(centred * centred, axis=0, keepdims=True) + eps_norm)
    return centred * inverse, inverse


def norm_back_t(grad, normed, inverse, gain):
    scaled = grad * gain
    return inverse * (
        scaled
        - jnp.mean(scaled, axis=0, keepdims=True)
        - normed * jnp.mean(scaled * normed, axis=0, keepdims=True)
    )


def sizes(n, num_q, num_mem):
    q_blocks = (num_q + TASKS * (QB - 1)) // QB
    q_blocks += q_blocks % 2
    k_chunks = (num_mem + TASKS * (KC - 1)) // KC
    return q_blocks, k_chunks


def step_kernel(
    n, num_q, num_mem, small_size,
    xs, fs, ct, posm, units, an, gw,
    gqkv, gout, ghead, out_sums, out_l,
    w_s, wt_s, wh_s, wht_s, kdup_s, vaug_w,
    cols, coefb,
    f2_s, mfeat,
    kaug, vaug, kt_s, vt_s, mnt, gk, gv,
    qn_s, q_s, qhi, qlo, att, il_s, gres, fn_s, gho_s, gb_s, dap, dneg, dq_s, stat_q,
    ebuf, sbuf, ecur, acc, m_s,
    acc_gain,
    blk_c0, blk_nc, blk_tile, ch_base, ch_end,
):
    planes = n // 8
    rows_dev = D // n
    per_small = small_size // n
    qs = num_q

    pieces = [gw[place_of(d, planes)].astype(f32) for d in range(n)]
    for col in range(8):
        block = jnp.concatenate([piece[8 * col : 8 * col + 8] for piece in pieces], axis=0)
        w_s[:, 128 * col : 128 * col + 128] = block.astype(bf16)
        wt_s[128 * col : 128 * col + 128, :] = block.T.astype(bf16)
    lane = iota((8, 128), 1)
    tiles = [piece[64:72] + piece[72:80] for piece in pieces]
    lane_w = iota((D, 128), 1)
    heads = pltpu.roll(jnp.concatenate(tiles, axis=0), 64, 1)
    heads = jnp.where(lane_w < C + F, heads, 0.0)
    wh_s[...] = heads.astype(bf16)
    wht_s[...] = heads.T[:32].astype(bf16)
    feats = []
    for b in range(n // 2):
        feats.append(jnp.where(lane < 64, tiles[2 * b], pltpu.roll(tiles[2 * b + 1], 64, 1)))
    feats = jnp.concatenate(feats, axis=1)
    f2_s[...] = jnp.concatenate(split2(feats), axis=0).astype(bf16)
    dup_r = iota((D, 4 * 128), 0)
    dup_l = iota((D, 4 * 128), 1)
    low6 = dup_l & 127
    dup = (dup_r == 64 * (dup_l >> 7) + (low6 & 63)).astype(f32).astype(bf16)
    once = ((dup_r == 64 * (dup_l >> 7) + low6) & (low6 < 64)).astype(f32).astype(bf16)
    kdup_s[...] = nn(w_s[:, D : 2 * D], dup).astype(bf16)
    vaug_w[...] = nn(w_s[:, 2 * D : 3 * D], once).astype(bf16)

    small_rows = jnp.concatenate([tile[0:1] for tile in tiles], axis=0)
    lane_n = iota((n, 128), 1)
    count_t = jnp.maximum(jnp.sum(jnp.where(lane_n == COUNT_LANE, small_rows, 0.0)), 1.0)
    count_r = jnp.maximum(jnp.sum(jnp.where(lane_n == COUNT_LANE + 1, small_rows, 0.0)), 1.0)
    used = 4 * D + 2 * H
    s2 = jnp.concatenate(
        list(split2(small_rows)) + [jnp.zeros((128 - 2 * n, 128), f32)], axis=0
    ).astype(bf16)
    row = iota((used, 128), 0)
    lan = iota((used, 128), 1)
    dev_of = lan & (n - 1)
    pick = (row >= per_small * dev_of) & (row < per_small * dev_of + per_small) & (lan < 2 * n)
    spread = nn(pick.astype(f32).astype(bf16), s2)
    row_dev = jnp.floor((row.astype(f32) + 0.5) * (1.0 / per_small)).astype(jnp.int32)
    here = (lan - SMALL_LANE) == (row - per_small * row_dev)
    column = jnp.sum(jnp.where(here, spread, 0.0), axis=1, keepdims=True)
    cols[...] = jnp.broadcast_to(column[: 4 * D], (4 * D, 128))
    for h in range(H):
        coefb[32 * h : 32 * h + 32, :] = jnp.broadcast_to(
            column[4 * D + h : 4 * D + h + 1] * (32 ** (-0.5)), (32, 128)
        )

    m_base = [units[t] for t in range(TASKS)]
    m_count = [units[TASKS + t] for t in range(TASKS)]
    m_units = [units[2 * TASKS + t] for t in range(TASKS)]
    q_base = [units[3 * TASKS + t] for t in range(TASKS)]
    q_units = [units[4 * TASKS + t] for t in range(TASKS)]
    tile = jnp.int32(0)
    for t in range(TASKS):
        first_chunk = lax.div(m_base[t], jnp.int32(KC))
        first_block = lax.div(q_base[t], jnp.int32(QB))

        def fill_chunk(i, carry, t=t, first_chunk=first_chunk):
            ch_base[first_chunk + i] = m_base[t]
            ch_end[first_chunk + i] = m_base[t] + m_count[t]
            return carry

        lax.fori_loop(0, m_units[t], fill_chunk, 0)

        def fill_block(i, tile_in, t=t, first_chunk=first_chunk, first_block=first_block):
            blk_c0[first_block + i] = first_chunk
            blk_nc[first_block + i] = m_units[t]
            blk_tile[first_block + i] = tile_in
            return tile_in + m_units[t]

        tile = lax.fori_loop(0, q_units[t], fill_block, tile)
    num_blocks = q_units[0] + q_units[1] + q_units[2] + q_units[3]
    num_chunks = m_units[0] + m_units[1] + m_units[2] + m_units[3]

    emb_w = lambda lanes: wide(cols[0:D, :], lanes)
    emb_b = lambda lanes: wide(cols[D : 2 * D, :], lanes)
    gain_in = lambda lanes: wide(cols[2 * D : 3 * D, :], lanes)
    gain_out = lambda lanes: wide(cols[3 * D : 4 * D, :], lanes)

    def mem_chunk(c, carry):
        at = pl.ds(pl.multiple_of(c * KC, KC), KC)
        base, end = ch_base[c], ch_end[c]
        s_col = iota((KC, 1), 0) + c * KC
        source = jnp.where(s_col < end, s_col, base).astype(f32)
        chosen = (posm[...] == source).astype(f32).astype(bf16)
        got = nt(f2_s[...], chosen)
        feats_c = got[0:8] + got[8:16]
        mfeat[:, at] = feats_c
        hidden = embed_t(feats_c, emb_w(KC), emb_b(KC))
        normed, unused = norm_t(hidden)
        mn = (normed * gain_in(KC)).astype(bf16)
        mnt[:, at] = mn
        kt_s[:, at] = nn(wt_s[D : 2 * D, :], mn).astype(bf16)
        live_row = ((iota((1, KC), 1) + c * KC) < end).astype(f32)
        vt = nn(wt_s[2 * D : 3 * D, :], mn) * live_row
        tail = jnp.where(iota((16, KC), 0) == 0, live_row, 0.0)
        vt_s[:, at] = jnp.concatenate(
            [part for p in range(4) for part in (vt[64 * p : 64 * p + 64], tail)], axis=0
        ).astype(bf16)
        kaug[at, :] = tn(mn, kdup_s[...]).astype(bf16)
        live_col = (s_col < end).astype(f32)
        low = iota((KC, 512), 1) & 127
        vn = jnp.where((low == 64) | (low == 65), 1.0, tn(mn, vaug_w[...]))
        vaug[at, :] = (vn * live_col).astype(bf16)
        gk[at, :] = jnp.zeros((KC, D), f32)
        gv[at, :] = jnp.zeros((KC, D), f32)
        return carry

    lax.fori_loop(0, num_chunks, mem_chunk, 0)

    coef2 = wide(coefb[...], 256)

    def pre_block(j, carry):
        at = pl.ds(pl.multiple_of(j * 256, 256), 256)
        kept = xs[:, at] * (1.0 - fs[:, at])
        hidden = embed_t(kept, emb_w(256), emb_b(256))
        normed, unused = norm_t(hidden)
        qn = (normed * gain_in(256)).astype(bf16)
        qn_s[:, at] = qn
        q = nn(wt_s[0:D, :], qn).astype(bf16)
        q_s[:, at] = q
        scaled = q.astype(f32) * (coef2 * LOG2E)
        upper = scaled.astype(bf16)
        qhi[:, at] = upper
        qlo[:, at] = (scaled - upper.astype(f32)).astype(bf16)
        att[:, at] = jnp.zeros((D, 256), bf16)
        il_s[:, at] = jnp.zeros((H, 256), f32)
        dq_s[:, at] = jnp.zeros((D, 256), f32)
        return carry

    lax.fori_loop(0, qs // 256, pre_block, 0)

    zero_h = jnp.zeros((32, 128), bf16)

    def diagonal(ref, at, p):
        return [
            jnp.concatenate([ref[64 * p : 64 * p + 32, at], zero_h], axis=1),
            jnp.concatenate([zero_h, ref[64 * p + 32 : 64 * p + 64, at]], axis=1),
        ]

    def score_operand(at, p):
        return jnp.concatenate(diagonal(qhi, at, p) + diagonal(qlo, at, p), axis=0)

    def finish_forward(at, p, got):
        inverse = 1.0 / got[64:65, :]
        il_s[2 * p : 2 * p + 1, at] = inverse[:, :128]
        il_s[2 * p + 1 : 2 * p + 2, at] = inverse[:, 128:]
        att[64 * p : 64 * p + 32, at] = (got[0:32, :128] * inverse[:, :128]).astype(bf16)
        att[64 * p + 32 : 64 * p + 64, at] = (got[32:64, 128:] * inverse[:, 128:]).astype(bf16)

    def pair(p, width):
        return slice(width * p, width * p + width)

    def forward_block(i, carry):
        at = pl.ds(pl.multiple_of(i * QB, QB), QB)
        c0, nc, tile0 = blk_c0[i], blk_nc[i], blk_tile[i]

        @pl.when(nc == 1)
        def one():
            keys = pl.ds(pl.multiple_of(c0 * KC, KC), KC)
            keep = jnp.minimum(tile0, E_CAP)
            operands = [score_operand(at, p) for p in range(4)]
            values = [vt_s[pair(p, VROWS), keys] for p in range(4)]
            scores = [nn(kaug[keys, pair(p, 128)], operands[p]) for p in range(4)]
            tops = [jnp.max(s, axis=0, keepdims=True) for s in scores]
            es = [jnp.exp2(scores[p] - tops[p]).astype(bf16) for p in range(4)]
            sums = [nn(values[p], es[p]) for p in range(4)]
            for p in range(4):
                m_s[i, :, pair(p, 256)] = tops[p]
                ebuf[keep, :, pair(p, 256)] = es[p]
                finish_forward(at, p, sums[p])

        @pl.when(nc > 1)
        def many():
            m_s[i] = jnp.full((1, 1024), -3e38, f32)
            acc[...] = jnp.zeros_like(acc)

            def tops(c, inner):
                keys = pl.ds(pl.multiple_of((c0 + c) * KC, KC), KC)
                for p in range(4):
                    s = nn(kaug[keys, pair(p, 128)], score_operand(at, p))
                    m_s[i, :, pair(p, 256)] = jnp.maximum(
                        m_s[i, :, pair(p, 256)], jnp.max(s, axis=0, keepdims=True)
                    )
                return inner

            lax.fori_loop(0, nc, tops, 0)

            def sums(c, inner):
                keys = pl.ds(pl.multiple_of((c0 + c) * KC, KC), KC)
                keep = jnp.minimum(tile0 + c, E_CAP)
                for p in range(4):
                    s = nn(kaug[keys, pair(p, 128)], score_operand(at, p))
                    e = jnp.exp2(s - m_s[i, :, pair(p, 256)]).astype(bf16)
                    ebuf[keep, :, pair(p, 256)] = e
                    acc[pair(p, VROWS), :] += nn(vt_s[pair(p, VROWS), keys], e)
                return inner

            lax.fori_loop(0, nc, sums, 0)
            for p in range(4):
                finish_forward(at, p, acc[pair(p, VROWS), :])

        return carry

    lax.fori_loop(0, num_blocks, forward_block, 0)

    weight_a = an[0]
    scale_t = weight_a / count_t
    scale_r = (1.0 - weight_a) / count_r
    acc_gain[...] = jnp.zeros_like(acc_gain)
    out_l[...] = jnp.zeros_like(out_l)

    def fold(v):
        return v[:, :128] + v[:, 128:256]

    def mid_block(j, carry):
        at = pl.ds(pl.multiple_of(j * 256, 256), 256)
        x = xs[:, at]
        fmask = fs[:, at]
        kept = x * (1.0 - fmask)
        hidden = embed_t(kept, emb_w(256), emb_b(256))
        attended = att[:, at]
        residual = hidden + nn(wt_s[3 * D : 4 * D, :], attended)
        normed, inverse = norm_t(residual)
        fn = (normed * gain_out(256)).astype(bf16)
        fn_s[:, at] = fn
        head = nn(wht_s[...], fn)
        logits = head[0:C]
        err = head[C : C + F] - x
        label = ct[1:2, at]
        hot = (iota((C, 256), 0).astype(f32) == ct[0:1, at]).astype(f32)
        top = jnp.max(logits, axis=0, keepdims=True)
        e = jnp.exp(logits - top)
        total = jnp.sum(e, axis=0, keepdims=True)
        picked = jnp.sum(logits * hot, axis=0, keepdims=True)
        out_l[0:1, :] += fold(
            scale_t * label * (jnp.log(total) + top - picked)
            + scale_r * jnp.sum(fmask * err * err, axis=0, keepdims=True)
        )
        g_log = scale_t * label * (e / total - hot)
        g_rec = scale_r * fmask * 2.0 * err
        gho = jnp.concatenate([g_log, g_rec, jnp.zeros((8, 256), f32)], axis=0).astype(bf16)
        gho_s[:, at] = gho
        g_final = nn(wh_s[:, :32], gho)
        acc_gain[D : 2 * D, :] += fold(g_final * normed)
        g_res = norm_back_t(g_final, normed, inverse, gain_out(256))
        gres[:, at] = g_res
        gb = g_res.astype(bf16)
        gb_s[:, at] = gb
        ga = nn(w_s[:, 3 * D : 4 * D], gb).astype(bf16).astype(f32)
        attf = attended.astype(f32)
        for h in range(H):
            rows = slice(32 * h, 32 * h + 32)
            da = (ga[rows] * il_s[h : h + 1, at]).astype(bf16)
            dap[rows, at] = da
            dneg[h : h + 1, at] = -jnp.sum(da.astype(f32) * attf[rows], axis=0, keepdims=True)
        return carry

    lax.fori_loop(0, qs // 256, mid_block, 0)

    zero_p = jnp.zeros((64, 256), bf16)
    zero_t = jnp.zeros((48, 256), bf16)
    r16 = iota((16, 256), 0)

    def backward_chunk(at, c, e_of):
        keys = pl.ds(pl.multiple_of(c * KC, KC), KC)
        es = [e_of(p) for p in range(4)]
        das = [jnp.concatenate(diagonal(dap, at, p), axis=0) for p in range(4)]
        qds = [jnp.concatenate(diagonal(q_s, at, p), axis=0) for p in range(4)]
        negs = dneg[:, at]
        vals = [vaug[keys, pair(p, 128)] for p in range(4)]
        kts = [kt_s[64 * p : 64 * p + 64, keys] for p in range(4)]
        old_dq = dq_s[:, at]
        old_gk = gk[keys, :]
        old_gv = gv[keys, :]
        operands = []
        for p in range(4):
            neg = jnp.concatenate([negs[2 * p : 2 * p + 1], negs[2 * p + 1 : 2 * p + 2]], axis=1)
            neg_hi = neg.astype(bf16).astype(f32)
            tail = jnp.where(r16 == 0, neg_hi, jnp.where(r16 == 1, neg - neg_hi, 0.0)).astype(bf16)
            operands.append(jnp.concatenate([das[p], tail, zero_t], axis=0))
        dps = [nn(vals[p], operands[p]) for p in range(4)]
        dss = [(es[p].astype(f32) * dps[p]).astype(bf16) for p in range(4)]
        dqs = [nn(kts[p], dss[p]) for p in range(4)]

        def by_key(grads, others):
            halves = []
            for a in (0, 2):
                left = jnp.concatenate([grads[a], grads[a + 1]], axis=1)
                upper = jnp.concatenate([others[a], zero_p], axis=1)
                lower = jnp.concatenate([zero_p, others[a + 1]], axis=1)
                halves.append(nt(left, jnp.concatenate([upper, lower], axis=0)))
            return jnp.concatenate(halves, axis=1)

        new_gv = old_gv + by_key(es, das)
        new_gk = old_gk + by_key(dss, qds)
        parts = []
        for p in range(4):
            parts += [dqs[p][0:32, :128], dqs[p][32:64, 128:]]
        dq_s[:, at] = old_dq + jnp.concatenate(parts, axis=0)
        gk[keys, :] = new_gk
        gv[keys, :] = new_gv

    def backward_block(i, carry):
        at = pl.ds(pl.multiple_of(i * QB, QB), QB)
        c0, nc, tile0 = blk_c0[i], blk_nc[i], blk_tile[i]
        simple = (nc == 1) & (tile0 < E_CAP)

        @pl.when(simple)
        def one():
            backward_chunk(at, c0, lambda p: ebuf[tile0, :, pair(p, 256)])

        @pl.when(jnp.logical_not(simple))
        def many():
            def one_chunk(c, inner):
                @pl.when(tile0 + c < E_CAP)
                def kept():
                    ecur[...] = ebuf[tile0 + c]

                @pl.when(tile0 + c >= E_CAP)
                def again():
                    keys = pl.ds(pl.multiple_of((c0 + c) * KC, KC), KC)
                    for p in range(4):
                        s = nn(kaug[keys, pair(p, 128)], score_operand(at, p))
                        ecur[:, pair(p, 256)] = jnp.exp2(
                            s - m_s[i, :, pair(p, 256)]
                        ).astype(bf16)

                backward_chunk(at, c0 + c, lambda p: ecur[:, pair(p, 256)])
                return inner

            lax.fori_loop(0, nc, one_chunk, 0)

        return carry

    lax.fori_loop(0, num_blocks, backward_block, 0)

    def sum_in(grad, normed, kept, lanes):
        by_feature = jnp.concatenate(
            [kept[f : f + 1] * grad[32 * f : 32 * f + 32] for f in range(F)], axis=0
        )
        outs = []
        for v in (by_feature, grad):
            total = v[:, :128]
            for k in range(1, lanes // 128):
                total = total + v[:, 128 * k : 128 * k + 128]
            outs.append(total)
        return outs

    def post_block(j, carry):
        at = pl.ds(pl.multiple_of(j * 256, 256), 256)
        kept = xs[:, at] * (1.0 - fs[:, at])
        hidden = embed_t(kept, emb_w(256), emb_b(256))
        normed, inverse = norm_t(hidden)
        dq = dq_s[:, at]
        gq = (dq * coef2).astype(bf16)
        prod = fold(dq * q_s[:, at].astype(f32))
        for h in range(H):
            acc_gain[4 * D + h : 4 * D + h + 1, :] += jnp.sum(
                prod[32 * h : 32 * h + 32], axis=0, keepdims=True
            )
        gqkv[:, 0:D] += nt(qn_s[:, at], gq)
        gqn = nn(w_s[:, 0:D], gq)
        acc_gain[0:D, :] += fold(gqn * normed)
        gh = gres[:, at] + norm_back_t(gqn, normed, inverse, gain_in(256))
        by_f, plain = sum_in(gh, normed, kept, 256)
        acc_gain[2 * D : 3 * D, :] += by_f
        acc_gain[3 * D : 4 * D, :] += plain
        return carry

    gqkv[...] = jnp.zeros_like(gqkv)
    lax.fori_loop(0, qs // 256, post_block, 0)
    gout[...] = nt(att[...], gb_s[...])
    ghead[...] = nt(fn_s[...], gho_s[...])

    def mem_back(c, carry):
        at = pl.ds(pl.multiple_of(c * KC, KC), KC)
        live = ((iota((KC, 1), 0) + c * KC) < ch_end[c]).astype(f32)
        coef_lane = carry
        gk_c = (gk[at, :] * coef_lane * live).astype(bf16)
        gv_c = (gv[at, :] * live).astype(bf16)
        mn = mnt[:, at]
        gqkv[:, D : 2 * D] += nn(mn, gk_c)
        gqkv[:, 2 * D : 3 * D] += nn(mn, gv_c)
        gmn = nt(w_s[:, D : 2 * D], gk_c) + nt(w_s[:, 2 * D : 3 * D], gv_c)
        feats_c = mfeat[:, at]
        hidden = embed_t(feats_c, emb_w(KC), emb_b(KC))
        normed, inverse = norm_t(hidden)
        dgain = gmn * normed
        acc_gain[0:D, :] += dgain[:, :128] + dgain[:, 128:256] + dgain[:, 256:384]
        gm = norm_back_t(gmn, normed, inverse, gain_in(KC))
        by_f, plain = sum_in(gm, normed, feats_c, KC)
        acc_gain[2 * D : 3 * D, :] += by_f
        acc_gain[3 * D : 4 * D, :] += plain
        return carry

    coef_lane = jnp.concatenate([coefb[0:128, :].T[0:1], coefb[128:256, :].T[0:1]], axis=1)
    lax.fori_loop(0, num_chunks, mem_back, coef_lane)

    out_sums[...] = jnp.broadcast_to(
        jnp.sum(acc_gain[...], axis=1, keepdims=True), (4 * D + H, 128)
    )


def step_call(n, num_mem, small_size, xs, fs, ct, posm, units, an, gw):
    num_q = xs.shape[1]
    q_blocks, k_chunks = xs.shape[1] // QB, (num_mem + TASKS * (KC - 1)) // KC
    qs, ks = q_blocks * QB, k_chunks * KC
    V = pltpu.VMEM
    S = pltpu.SMEM
    vm = pl.BlockSpec(memory_space=pltpu.VMEM)
    sm = pl.BlockSpec(memory_space=pltpu.SMEM)
    scratch = [
        V((D, 4 * D), bf16), V((4 * D, D), bf16), V((D, 128), bf16), V((32, D), bf16),
        V((D, 512), bf16), V((D, 512), bf16),
        V((4 * D, 128), f32), V((D, 128), f32),
        V((16, num_mem), bf16), V((8, ks), f32),
        V((ks, 512), bf16), V((ks, 512), bf16), V((D, ks), bf16), V((4 * VROWS, ks), bf16),
        V((D, ks), bf16), V((ks, D), f32), V((ks, D), f32),
        V((D, qs), bf16), V((D, qs), bf16), V((D, qs), bf16), V((D, qs), bf16), V((D, qs), bf16),
        V((H, qs), f32), V((D, qs), f32), V((D, qs), bf16), V((32, qs), bf16), V((D, qs), bf16),
        V((D, qs), bf16), V((H, qs), f32), V((D, qs), f32), V((8, qs), f32),
        V((E_CAP + 1, KC, 1024), bf16), V((8, 128), f32), V((KC, 1024), bf16),
        V((4 * VROWS, 256), f32), V((q_blocks, 1, 1024), f32),
        V((4 * D + H, 128), f32),
        S((q_blocks,), jnp.int32), S((q_blocks,), jnp.int32), S((q_blocks,), jnp.int32),
        S((k_chunks,), jnp.int32), S((k_chunks,), jnp.int32),
    ]
    return pl.pallas_call(
        functools.partial(step_kernel, n, qs, num_mem, small_size),
        out_shape=(
            jax.ShapeDtypeStruct((D, 3 * D), f32),
            jax.ShapeDtypeStruct((D, D), f32),
            jax.ShapeDtypeStruct((D, 32), f32),
            jax.ShapeDtypeStruct((4 * D + H, 128), f32),
            jax.ShapeDtypeStruct((8, 128), f32),
        ),
        in_specs=[vm] * 4 + [sm] * 2 + [vm],
        out_specs=(vm,) * 5,
        scratch_shapes=scratch,
        compiler_params=pltpu.CompilerParams(vmem_limit_bytes=58 * 1024 * 1024),
    )(xs, fs, ct, posm, units, an, gw)


MESH = pl.DeviceIdType.MESH


def greet(targets):
    barrier = pltpu.get_barrier_semaphore()
    for target in targets:
        pl.semaphore_signal(barrier, inc=1, device_id=(target,), device_id_type=MESH)
    return barrier


def send(src, dst, send_sem, recv_sem, target):
    copy = pltpu.make_async_remote_copy(
        src_ref=src,
        dst_ref=dst,
        send_sem=send_sem,
        recv_sem=recv_sem,
        device_id=(target,),
        device_id_type=MESH,
    )
    copy.start()
    return copy


def where_am_i(planes):
    me = lax.axis_index("mem")
    core = lax.rem(me, 2)
    square = lax.rem(lax.div(me, 2), 4)
    plane = lax.div(me, 8)
    return me, core, square, plane


def gather_kernel(
    n, num_q, num_mem, w_qkv, w_out, w_heads, w_small, mfeat, qf, fm, qt, tc, tm, mt, mm,
    gw, xs, fs, ct, posm, units_out,
    send_z, recv_z, send_s, recv_s, send_c, recv_c,
):
    planes = n // 8
    me, core, square, plane = where_am_i(planes)
    in_plane = core + 2 * square
    z_of = [lax.rem(plane + k, planes) * 8 + in_plane for k in range(1, planes)]
    s_of = [plane * 8 + lax.rem(square + k, 4) * 2 + core for k in range(1, 4)]
    c_of = plane * 8 + square * 2 + (1 - core)
    barrier = greet(z_of + s_of + [c_of])

    rows = []
    for c in range(6):
        rows.append(w_qkv[pl.ds(c, 8, stride=6), :])
    for c in range(2):
        rows.append(w_out[pl.ds(c, 8, stride=2), :])
    per_head = w_heads.shape[1]
    lane = iota((8, 256), 1)
    head_row = jnp.concatenate([w_heads[...], jnp.zeros((1, 256 - per_head), f32)], axis=1)
    owner = jnp.floor((lane.astype(f32) + 0.5) * (1.0 / (C + F))).astype(jnp.int32)
    kept_heads = jnp.where(owner == iota((8, 256), 0), head_row, 0.0).astype(bf16)
    fold_r = iota((256, 128), 0)
    fold_row = jnp.floor((fold_r.astype(f32) + 0.5) * (1.0 / (C + F))).astype(jnp.int32)
    fold_m = (fold_r - (C + F) * fold_row == iota((256, 128), 1) - 64).astype(f32).astype(bf16)
    heads = nn(kept_heads, fold_m)
    per_small = w_small.shape[1]
    small = jnp.concatenate([w_small[...], jnp.zeros((1, 128 - per_small), f32)], axis=1)
    small = pltpu.roll(jnp.broadcast_to(small, (8, 128)), SMALL_LANE, 1)
    feats = jnp.concatenate([mfeat[...], jnp.zeros((8, 64), f32)], axis=1)
    lane8 = iota((8, 128), 1)
    row8 = iota((8, 128), 0)
    num_t = jnp.sum(tm[...].astype(f32), axis=1, keepdims=True)
    num_r = jnp.sum(jnp.sum(fm[...].astype(f32), axis=0, keepdims=True), axis=1, keepdims=True)
    block = feats + heads
    first = (row8 == 0) & (lane8 >= SMALL_LANE) & (lane8 < SMALL_LANE + per_small)
    block = jnp.where(first, small, block)
    block = jnp.where((row8 == 0) & (lane8 == COUNT_LANE), num_t, block)
    block = jnp.where((row8 == 0) & (lane8 == COUNT_LANE + 1), num_r, block)

    def slot_of(k, j, c):
        back = lax.rem(plane + planes - k, planes)
        return c * (4 * planes) + lax.rem(square + 4 - j, 4) * planes + back

    gw[slot_of(0, 0, core)] = jnp.concatenate(rows + list(split2(block)), axis=0).astype(bf16)

    pl.semaphore_wait(barrier, planes - 1 + 4)

    def spread(k, done):
        at = gw.at[slot_of(k, 0, core)]
        for j in range(1, 4):
            done[k, j] = send(at, at, send_s.at[k, j - 1], recv_s.at[k, j - 1], s_of[j - 1])
        done[k, 0, "c"] = send(at, at, send_c.at[k, 0], recv_c.at[k, 0], c_of)

    at = gw.at[slot_of(0, 0, core)]
    done = {}
    for k in range(1, planes):
        done[k] = send(at, at, send_z.at[k - 1], recv_z.at[k - 1], z_of[k - 1])
    spread(0, done)

    task_row = iota((8, 256), 0)
    marks = []
    for b in range(num_q // 256):
        marks.append((qt[:, 256 * b : 256 * b + 256] == task_row).astype(f32))
    for b in range(num_mem // 256):
        cut = slice(256 * b, 256 * b + 256)
        marks.append(((mt[:, cut] == task_row) & (mm[:, cut] > 0)).astype(f32))
    marks_all = jnp.concatenate(marks, axis=0)
    tri = (iota((256, 256), 0) < iota((256, 256), 1)).astype(f32).astype(bf16)
    ranks = nn(marks_all.astype(bf16), tri)
    totals = jnp.sum(marks_all, axis=1, keepdims=True)
    task_col = iota((8, 1), 0)

    def lay_out(first, count, unit):
        carry = jnp.zeros((8, 1), f32)
        before = []
        for b in range(count):
            before.append(carry)
            at = 8 * (first + b)
            carry = carry + totals[at : at + 8]
        base = jnp.int32(0)
        bases, counts, units = [], [], []
        base_vec = jnp.zeros((8, 1), f32)
        for t in range(TASKS):
            num = jnp.sum(jnp.where(task_col == t, carry, 0.0)).astype(jnp.int32)
            bases.append(base)
            counts.append(num)
            used_units = lax.div(num + (unit - 1), jnp.int32(unit))
            units.append(used_units)
            base_vec = base_vec + jnp.where(task_col == t, base.astype(f32), 0.0)
            base = base + used_units * unit
        places = []
        for b in range(count):
            at = 8 * (first + b)
            places.append(
                jnp.sum(
                    marks[first + b] * (base_vec + before[b] + ranks[at : at + 8]),
                    axis=0,
                    keepdims=True,
                )
                - (1.0 - jnp.sum(marks[first + b], axis=0, keepdims=True))
            )
        return jnp.concatenate(places, axis=1), bases, counts, units

    place_q, q_base, q_count, q_units = lay_out(0, num_q // 256, QB)
    place_m, m_base, m_count, m_units = lay_out(num_q // 256, num_mem // 256, KC)

    posm[...] = place_m
    for t in range(TASKS):
        units_out[t] = m_base[t]
        units_out[TASKS + t] = m_count[t]
        units_out[2 * TASKS + t] = m_units[t]
        units_out[3 * TASKS + t] = q_base[t]
        units_out[4 * TASKS + t] = q_units[t]
    qs = xs.shape[1]
    xq = qf[...]
    fmq = fm[...].astype(f32)
    row8 = iota((8, num_q), 0)
    label_rows = jnp.where(
        row8 == 0, tc[...].astype(f32), jnp.where(row8 == 1, tm[...].astype(f32), 0.0)
    )
    q_rows = jnp.concatenate(
        list(split3(xq)) + [fmq, label_rows, jnp.zeros((8, num_q), f32)], axis=0
    ).astype(bf16)
    for b in range(qs // 256):
        chosen = (
            (place_q == (iota((256, 1), 0) + 256 * b).astype(f32)).astype(f32).astype(bf16)
        )
        got = nt(q_rows, chosen)
        cut = slice(256 * b, 256 * b + 256)
        xs[:, cut] = got[0:8] + got[8:16] + got[16:24]
        fs[:, cut] = got[24:32]
        ct[:, cut] = got[32:40]


    for k in range(1, planes):
        done[k].wait_recv()
        spread(k, done)
    for k in range(planes):
        for j in range(1, 4):
            done[k, j].wait_recv()
            at = gw.at[slot_of(k, j, core)]
            done[k, j, "c"] = send(at, at, send_c.at[k, j], recv_c.at[k, j], c_of)
    for k in range(planes):
        for j in range(4):
            done[k, j, "c"].wait_recv()
    for copy in done.values():
        copy.wait_send()


def gather_call(n, w_qkv, w_out, w_heads, w_small, mfeat, qf, fm, qt, tc, tm, mt, mm):
    planes = n // 8
    num_q, num_mem = qf.shape[1], mt.shape[1]
    qs = sizes(n, num_q, num_mem)[0] * QB
    vm = pl.BlockSpec(memory_space=pltpu.VMEM)
    dma = pltpu.SemaphoreType.DMA
    return pl.pallas_call(
        functools.partial(gather_kernel, n, num_q, num_mem),
        out_shape=(
            jax.ShapeDtypeStruct((n, 80, 128), bf16),
            jax.ShapeDtypeStruct((8, qs), f32),
            jax.ShapeDtypeStruct((8, qs), f32),
            jax.ShapeDtypeStruct((8, qs), f32),
            jax.ShapeDtypeStruct((1, num_mem), f32),
            jax.ShapeDtypeStruct((5 * TASKS,), jnp.int32),
        ),
        in_specs=[vm] * 12,
        out_specs=(vm,) * 5 + (pl.BlockSpec(memory_space=pltpu.SMEM),),
        scratch_shapes=[
            dma((planes - 1,)), dma((planes - 1,)), dma((planes, 3)), dma((planes, 3)),
            dma((planes, 4)), dma((planes, 4)),
        ],
        compiler_params=pltpu.CompilerParams(collective_id=0, has_side_effects=True),
    )(w_qkv, w_out, w_heads, w_small, mfeat, qf, fm, qt, tc, tm, mt, mm)


def reduce_kernel(
    n, per_small, gqkv, gout, ghead, sums_in, l_in, g_out, t_out,
    s_s, r_core, t_square, r_square, t_plane, r_plane, own, n_mine, n_all,
    send_c, recv_c, send_s, recv_s, send_z, recv_z, send_n, recv_n,
):
    planes = n // 8
    rows_dev = D // n
    me, core, square, plane = where_am_i(planes)
    in_plane = core + 2 * square
    a_of = [lax.rem(me + k, n) for k in range(1, n)]
    z_of = [lax.rem(plane + k, planes) * 8 + in_plane for k in range(1, planes)]
    s_of = [plane * 8 + lax.rem(square + k, 4) * 2 + core for k in range(1, 4)]
    c_of = plane * 8 + square * 2 + (1 - core)
    barrier = greet(a_of)

    used = 4 * D + 2 * H
    row = iota((used, 128), 0)
    lan = iota((used, 128), 1)
    row_dev = jnp.floor((row.astype(f32) + 0.5) * (1.0 / per_small)).astype(jnp.int32)
    sums = sums_in[...]
    small = jnp.concatenate(
        [
            sums[2 * D : 3 * D],
            sums[3 * D : 4 * D],
            sums[0:D],
            sums[D : 2 * D],
            sums[4 * D : 4 * D + H] * (32 ** (-0.5)),
            jnp.zeros((H, 128), f32),
        ],
        axis=0,
    )
    placed = jnp.where(lan == (row - per_small * row_dev), small, 0.0).astype(bf16)
    r_dev = iota((n, used), 0)
    r_row = iota((n, used), 1)
    mine = (r_row >= per_small * r_dev) & (r_row < per_small * r_dev + per_small)
    small_rows_out = nn(mine.astype(f32).astype(bf16), placed)
    to_flat_r = iota((32, 256), 0)
    to_flat_l = iota((32, 256), 1)
    lane_row = jnp.floor((to_flat_l.astype(f32) + 0.5) * (1.0 / (C + F))).astype(jnp.int32)
    to_flat = ((to_flat_l - (C + F) * lane_row == to_flat_r) & (to_flat_r < C + F)).astype(f32)
    spread_h = nn(ghead[...].astype(bf16), to_flat.astype(bf16))
    lr = iota((D, 256), 1)
    lr_row = jnp.floor((lr.astype(f32) + 0.5) * (1.0 / (C + F))).astype(jnp.int32)
    spread_h = jnp.where(lr_row == (iota((D, 256), 0) & (rows_dev - 1)), spread_h, 0.0)
    r8 = iota((8, 128), 0)
    for d in range(n):
        rows = slice(rows_dev * d, rows_dev * d + rows_dev)
        head_flat = jnp.sum(spread_h[rows], axis=0, keepdims=True)
        extra = jnp.where(
            r8 == 0,
            head_flat[:, :128],
            jnp.where(r8 == 1, head_flat[:, 128:], jnp.where(r8 == 2, small_rows_out[d : d + 1], 0.0)),
        )
        block = [gqkv[rows, 128 * k : 128 * k + 128] for k in range(6)]
        block += [gout[rows, 128 * k : 128 * k + 128] for k in range(2)]
        block += [extra, jnp.zeros((8, 128), f32)]
        s_s[place_of(d, planes)] = jnp.concatenate(block, axis=0).astype(bf16)

    pl.semaphore_wait(barrier, n - 1)

    def part(c, j, k):
        z = lax.rem(plane + k, planes)
        return c * (4 * planes) + lax.rem(square + j, 4) * planes + z

    done = []
    pieces = {}
    for j in (1, 2, 3, 0):
        line = pl.ds((1 - core) * (4 * planes) + lax.rem(square + j, 4) * planes, planes)
        pieces[j] = send(s_s.at[line], r_core.at[j], send_c.at[j], recv_c.at[j], c_of)
    for j in (1, 2, 3):
        pieces[j].wait_recv()
    order = [2, 1, 3, 0] if planes == 4 else list(range(1, planes)) + [0]
    crossing = {}
    for k in order:
        z = lax.rem(plane + k, planes)
        for j in range(1, 4):
            t_square[j - 1, k] = (
                s_s[part(core, j, k)].astype(f32) + r_core[j, z].astype(f32)
            ).astype(bf16)
            crossing[k, j] = send(
                t_square.at[j - 1, k], r_square.at[j - 1, k],
                send_s.at[j - 1, k], recv_s.at[j - 1, k], s_of[j - 1],
            )
    pieces[0].wait_recv()
    for k in order:
        z = lax.rem(plane + k, planes)
        own[k] = s_s[part(core, 0, k)].astype(f32) + r_core[0, z].astype(f32)
    along = {}
    for k in order:
        total = own[k]
        for j in range(1, 4):
            crossing[k, j].wait_recv()
            total = total + r_square[j - 1, k].astype(f32)
        if k:
            t_plane[k - 1] = total.astype(bf16)
            along[k] = send(
                t_plane.at[k - 1], r_plane.at[k - 1], send_z.at[k - 1], recv_z.at[k - 1], z_of[k - 1]
            )
    for k in range(1, planes):
        along[k].wait_recv()
        total = total + r_plane[k - 1].astype(f32)
    g_out[...] = total
    squares = jnp.sum(total * total, axis=0, keepdims=True)
    squares = squares + pltpu.roll(squares, 64, 1)
    losses = l_in[0:1, :]
    losses = losses + pltpu.roll(losses, 64, 1)
    n_mine[...] = jnp.where(iota((1, 128), 1) < 64, squares, losses)
    last = []
    for k in range(1, n):
        last.append(send(n_mine, n_all.at[k - 1], send_n.at[k - 1], recv_n.at[k - 1], a_of[k - 1]))
    total = n_mine[...]
    for k in range(1, n):
        last[k - 1].wait_recv()
        total = total + n_all[k - 1]
    t_out[...] = total
    for copies in (pieces, crossing, along):
        for copy in copies.values():
            copy.wait_send()
    for copy in last:
        copy.wait_send()


def reduce_call(n, per_small, *grads):
    planes = n // 8
    rows = 80
    vm = pl.BlockSpec(memory_space=pltpu.VMEM)
    dma = pltpu.SemaphoreType.DMA
    V = pltpu.VMEM
    z = planes - 1
    return pl.pallas_call(
        functools.partial(reduce_kernel, n, per_small),
        out_shape=(
            jax.ShapeDtypeStruct((rows, 128), f32),
            jax.ShapeDtypeStruct((1, 128), f32),
        ),
        in_specs=[vm] * 5,
        out_specs=(vm, vm),
        scratch_shapes=[
            V((n, rows, 128), bf16), V((4, planes, rows, 128), bf16), V((3, planes, rows, 128), bf16),
            V((3, planes, rows, 128), bf16), V((z, rows, 128), bf16), V((z, rows, 128), bf16),
            V((planes, rows, 128), f32), V((1, 128), f32), V((n - 1, 1, 128), f32),
            dma((4,)), dma((4,)), dma((3, planes)), dma((3, planes)), dma((z,)), dma((z,)),
            dma((n - 1,)), dma((n - 1,)),
        ],
        compiler_params=pltpu.CompilerParams(collective_id=1, has_side_effects=True),
    )(*grads)


def update_kernel(g, tot, *refs):
    weights, firsts, seconds = refs[0:4], refs[4:8], refs[8:12]
    new, first_o, second_o, copy_o = refs[12:16], refs[16:20], refs[20:24], refs[24:28]
    loss_o, norm_o, gq_s, go_s = refs[28:32]
    for c in range(6):
        gq_s[pl.ds(c, 8, stride=6), :] = g[8 * c : 8 * c + 8, :]
    for c in range(2):
        go_s[pl.ds(c, 8, stride=2), :] = g[48 + 8 * c : 56 + 8 * c, :]
    first_half = iota((1, 128), 1) < 64
    norm = jnp.sqrt(jnp.sum(jnp.where(first_half, tot[...], 0.0), axis=1, keepdims=True))
    loss_o[...] = jnp.sum(jnp.where(first_half, 0.0, tot[...]), axis=1, keepdims=True)
    norm_o[...] = norm
    factor = jnp.minimum(1.0, max_norm / (norm + 1e-06))
    per_head, per_small = weights[2].shape[1], weights[3].shape[1]
    grads = (
        gq_s[...],
        go_s[...],
        jnp.concatenate([g[64:65, :], g[65:66, : per_head - 128]], axis=1),
        g[66:67, :per_small],
    )
    for i in range(4):
        first_new, second_new, weight_new = adamw(
            weights[i][...], firsts[i][...], seconds[i][...], grads[i], factor, float(STEP), learn_rates[i]
        )
        new[i][...] = weight_new
        first_o[i][...] = first_new
        second_o[i][...] = second_new
        copy_o[i][...] = weight_new.astype(bf16)


def update_call(g, tot, weights, firsts, seconds):
    vm = pl.BlockSpec(memory_space=pltpu.VMEM)
    shapes = [w.shape for w in weights]
    outs = [jax.ShapeDtypeStruct(s, f32) for s in shapes] * 3
    outs += [jax.ShapeDtypeStruct(s, bf16) for s in shapes]
    outs += [jax.ShapeDtypeStruct((1, 1), f32)] * 2
    return pl.pallas_call(
        update_kernel,
        out_shape=tuple(outs),
        in_specs=[vm] * 14,
        out_specs=(vm,) * 18,
        scratch_shapes=[pltpu.VMEM((48, 128), f32), pltpu.VMEM((16, 128), f32)],
    )(g, tot, *weights, *firsts, *seconds)


def local_fast(
    n, query_feats, feature_mask, query_task, target_class, target_mask, memory_feats, memory_task,
    memory_mask, anneal, w_qkv, w_out, w_heads, w_small, m_qkv, m_out, m_heads, m_small,
    v_qkv, v_out, v_heads, v_small,
):
    def row(v):
        return v.reshape(1, -1)

    def tiles(v):
        return v.reshape(-1, 128)

    weights = (tiles(w_qkv), tiles(w_out), row(w_heads), row(w_small))
    firsts = (tiles(m_qkv), tiles(m_out), row(m_heads), row(m_small))
    seconds = (tiles(v_qkv), tiles(v_out), row(v_heads), row(v_small))
    tm, mt = row(target_mask), row(memory_task)
    gw, xs, fs, ct, posm, units = gather_call(
        n, *weights, memory_feats.T, query_feats.T, feature_mask.T, row(query_task),
        row(target_class), tm, mt, row(memory_mask),
    )
    found = step_call(n, mt.shape[1], w_small.shape[0] * n, xs, fs, ct, posm, units, anneal, gw)
    grads, totals = reduce_call(n, w_small.shape[0], *found)
    outs = update_call(grads, totals, weights, firsts, seconds)
    return tuple(out.reshape(-1) for out in outs)


def solution(mesh):
    placed = (
        P("mem", None),
        P("mem", None),
        P("mem"),
        P("mem"),
        P("mem"),
        P("mem", None),
        P(),
        P(),
        P(),
        P("mem"),
        P("mem"),
        P("mem"),
        P("mem"),
        P("mem"),
        P("mem"),
        P("mem"),
        P("mem"),
        P("mem"),
        P("mem"),
        P("mem"),
        P("mem"),
    )
    n = mesh.shape["mem"]

    def choose(*args):
        if D // n == 8 and args[6].shape[0] <= 4096:
            return local_fast(n, *args)
        return local(*args)

    return jax.shard_map(
        choose,
        mesh=mesh,
        in_specs=placed,
        out_specs=(
            P("mem"),
            P("mem"),
            P("mem"),
            P("mem"),
            P("mem"),
            P("mem"),
            P("mem"),
            P("mem"),
            P("mem"),
            P("mem"),
            P("mem"),
            P("mem"),
            P("mem"),
            P("mem"),
            P("mem"),
            P("mem"),
            P(),
            P(),
        ),
        check_vma=False,
    )
```

time: 101 us -> 82.5 us (0.82)
  Pallas kernels: 97.7 us -> 79.4 us
    pallas_call x3, Pallas kernels: 95.9 us -> 77.6 us  [the longest x1 39.8 us: step_call(): pl.pallas_call(functools.partial(step_kernel, n, qs, num_mem, small_size)...]
where the time goes in v2:
time: 82.5 us; the launch traced here: 81.9 us
  Pallas kernels  79.4 us (96%)
  between operations  1.34 us (2%)
    pallas_call x1, Pallas kernels, step_call(): pl.pallas_call(functools.partial(step_kernel, n, qs, num_mem, small_size)...  39.8 us
    pallas_call x1, Pallas kernels, reduce_call(): pl.pallas_call(functools.partial(reduce_kernel, n, per_small), out_shape=...  21.8 us
    pallas_call x1, Pallas kernels, gather_call(): pl.pallas_call(functools.partial(gather_kernel, n, num_q, num_mem), out_s...  15.9 us
    pallas_call x1, Pallas kernels, update_call(): pl.pallas_call(update_kernel, out_shape=tuple(outs), in_specs=[vm] * 14,...  1.77 us

profile of v2, /device:TPU:0, one launch (start us, length us, event | category | flops | bytes accessed | tf_op | source)
XLA Modules:
  0.0 81.9 jit_solution(7535646148185863748)
XLA Ops:
  1.3 15.9 %shard_map.340 = (bf16[32,80,128]{2,1,0:T(8,128)(2,1)}, f32[8,1536]{1,0:T(8,128)}, f32[8,1536]{1,0:T(8,128)}, f32[8,1536]{1,0:T(8,128)}, f32[1,2048]{1,0:T(1,128)}, /*index=5*/s32[20]{0:T(128)}) custom-call(f32[48,128]{1,0:T(8,128)} %bitcast.37, f32[16,128]{1,0:T(8,128)} %bitcast.39, f32[1,192]{1,0:T(1,128)} %bitcast.49, f32[1,33]{1,0:T(1,128)} %bitcast.55, ...), custom_call_target="tpu_custom_call" | custom-call | tf_op jit(solution)/shard_map/pallas_call | solution.py:1058
  17.2 39.8 %shard_map.341 = (f32[256,768]{1,0:T(8,128)}, f32[256,256]{1,0:T(8,128)}, f32[256,32]{1,0:T(8,128)}, f32[1032,128]{1,0:T(8,128)}, f32[8,128]{1,0:T(8,128)}) custom-call(f32[8,1536]{1,0:T(8,128)} %get-tuple-element.49.xs, f32[8,1536]{1,0:T(8,128)} %get-tuple-element.50.fs, f32[8,1536]{1,0:T(8,128)} %get-tuple-element.51.ct, ...), custom_call_target="tpu_custom_call" | custom-call | tf_op jit(solution)/shard_map/pallas_call | solution.py:854
  57.1 21.8 %shard_map.342 = (f32[80,128]{1,0:T(8,128)}, f32[1,128]{1,0:T(1,128)}) custom-call(f32[256,768]{1,0:T(8,128)} %get-tuple-element.55.gqkv, f32[256,256]{1,0:T(8,128)} %get-tuple-element.56.gout, f32[256,32]{1,0:T(8,128)} %get-tuple-element.57.ghead, f32[1032,128]{1,0:T(8,128)} %get-tuple-element.58.sums_in, f32[8,128]{1,0:T(8,128)} %get-tuple-element.59.l_in), custom_call_target="tpu_custom_call" | custom-call | tf_op jit(solution)/shard_map/pallas_call | solution.py:1207
  78.9 1.8 %shard_map.343 = (f32[48,128]{1,0:T(8,128)}, f32[16,128]{1,0:T(8,128)}, f32[1,192]{1,0:T(1,128)}, f32[1,33]{1,0:T(1,128)}, f32[48,128]{1,0:T(8,128)}, /*index=5*...) custom-call(f32[80,128]{1,0:T(8,128)} %get-tuple-element.60.g, ...), custom_call_target="tpu_custom_call" | custom-call | tf_op jit(solution)/shard_map/pallas_call | solution.py:1262
  80.7 0.0 copy-start
  80.7 0.7 copy-done
  81.4 0.5 reduce
Async XLA Ops:
  80.7 0.7 copy-start

commit v3 on v2

--- a/solution.py
+++ b/solution.py
@@ -334,6 +334,7 @@
 LOG2E = math.log2(math.e)
 QB = 128
 KC = 384
+KC_LOW = 320
 VROWS = 80
 E_CAP = 16
 SMALL_LANE = 88
@@ -398,30 +399,61 @@
     )
 
 
-def sizes(n, num_q, num_mem):
-    q_blocks = (num_q + TASKS * (QB - 1)) // QB
-    q_blocks += q_blocks % 2
-    k_chunks = (num_mem + TASKS * (KC - 1)) // KC
-    return q_blocks, k_chunks
+def blocks_of(num_q):
+    blocks = (num_q + TASKS * (QB - 1)) // QB
+    return -(-blocks // 4) * 4
+
+
+def chunks_of(num_mem):
+    chunks = (num_mem + TASKS * (KC - 1)) // KC
+    return chunks + chunks % 2
 
 
 def step_kernel(
-    n, num_q, num_mem, small_size,
-    xs, fs, ct, posm, units, an, gw,
+    n, qs, num_mem, small_size,
+    xs, fs, ct, posb, table, units, an, gw,
     gqkv, gout, ghead, out_sums, out_l,
-    w_s, wt_s, wh_s, wht_s, kdup_s, vaug_w,
+    w_s, wt_s, wh_s, wht_s,
     cols, coefb,
-    f2_s, mfeat,
-    kaug, vaug, kt_s, vt_s, mnt, gk, gv,
-    qn_s, q_s, qhi, qlo, att, il_s, gres, fn_s, gho_s, gb_s, dap, dneg, dq_s, stat_q,
-    ebuf, sbuf, ecur, acc, m_s,
-    acc_gain,
-    blk_c0, blk_nc, blk_tile, ch_base, ch_end,
+    mfeat, kn, vn, kt_s, vt_s, mnt, gk, gv,
+    qn_s, q_s, att, il_s, gres, fn_s, gho_s, gb_s, dap, delta, dq_s,
+    ebuf, ecur, acc, m_s, acc_gain,
+    blk_c0, blk_nc, blk_tile, blk_rows, ch_base, ch_end,
 ):
     planes = n // 8
-    rows_dev = D // n
     per_small = small_size // n
-    qs = num_q
+    k_chunks = ch_base.shape[0]
+
+    m_base = [units[t] for t in range(TASKS)]
+    m_count = [units[TASKS + t] for t in range(TASKS)]
+    m_units = [units[2 * TASKS + t] for t in range(TASKS)]
+    q_base = [units[3 * TASKS + t] for t in range(TASKS)]
+    q_units = [units[4 * TASKS + t] for t in range(TASKS)]
+    num_blocks = q_units[0] + q_units[1] + q_units[2] + q_units[3]
+    num_chunks = m_units[0] + m_units[1] + m_units[2] + m_units[3]
+    for c in range(k_chunks):
+        ch_base[c] = jnp.int32(c * KC)
+        ch_end[c] = jnp.int32(c * KC)
+    tile = jnp.int32(0)
+    for t in range(TASKS):
+        first_chunk = lax.div(m_base[t], jnp.int32(KC))
+        first_block = lax.div(q_base[t], jnp.int32(QB))
+
+        def fill_chunk(i, carry, t=t, first_chunk=first_chunk):
+            ch_base[first_chunk + i] = m_base[t]
+            ch_end[first_chunk + i] = m_base[t] + m_count[t]
+            return carry
+
+        lax.fori_loop(0, m_units[t], fill_chunk, 0)
+
+        def fill_block(i, tile_in, t=t, first_chunk=first_chunk, first_block=first_block):
+            blk_c0[first_block + i] = first_chunk
+            blk_nc[first_block + i] = m_units[t]
+            blk_rows[first_block + i] = m_count[t]
+            blk_tile[first_block + i] = tile_in
+            return tile_in + m_units[t]
+
+        tile = lax.fori_loop(0, q_units[t], fill_block, tile)
 
     pieces = [gw[place_of(d, planes)].astype(f32) for d in range(n)]
     for col in range(8):
@@ -435,18 +467,6 @@
     heads = jnp.where(lane_w < C + F, heads, 0.0)
     wh_s[...] = heads.astype(bf16)
     wht_s[...] = heads.T[:32].astype(bf16)
-    feats = []
-    for b in range(n // 2):
-        feats.append(jnp.where(lane < 64, tiles[2 * b], pltpu.roll(tiles[2 * b + 1], 64, 1)))
-    feats = jnp.concatenate(feats, axis=1)
-    f2_s[...] = jnp.concatenate(split2(feats), axis=0).astype(bf16)
-    dup_r = iota((D, 4 * 128), 0)
-    dup_l = iota((D, 4 * 128), 1)
-    low6 = dup_l & 127
-    dup = (dup_r == 64 * (dup_l >> 7) + (low6 & 63)).astype(f32).astype(bf16)
-    once = ((dup_r == 64 * (dup_l >> 7) + low6) & (low6 < 64)).astype(f32).astype(bf16)
-    kdup_s[...] = nn(w_s[:, D : 2 * D], dup).astype(bf16)
-    vaug_w[...] = nn(w_s[:, 2 * D : 3 * D], once).astype(bf16)
 
     small_rows = jnp.concatenate([tile[0:1] for tile in tiles], axis=0)
     lane_n = iota((n, 128), 1)
@@ -470,101 +490,106 @@
             column[4 * D + h : 4 * D + h + 1] * (32 ** (-0.5)), (32, 128)
         )
 
-    m_base = [units[t] for t in range(TASKS)]
-    m_count = [units[TASKS + t] for t in range(TASKS)]
-    m_units = [units[2 * TASKS + t] for t in range(TASKS)]
-    q_base = [units[3 * TASKS + t] for t in range(TASKS)]
-    q_units = [units[4 * TASKS + t] for t in range(TASKS)]
-    tile = jnp.int32(0)
-    for t in range(TASKS):
-        first_chunk = lax.div(m_base[t], jnp.int32(KC))
-        first_block = lax.div(q_base[t], jnp.int32(QB))
-
-        def fill_chunk(i, carry, t=t, first_chunk=first_chunk):
-            ch_base[first_chunk + i] = m_base[t]
-            ch_end[first_chunk + i] = m_base[t] + m_count[t]
-            return carry
-
-        lax.fori_loop(0, m_units[t], fill_chunk, 0)
-
-        def fill_block(i, tile_in, t=t, first_chunk=first_chunk, first_block=first_block):
-            blk_c0[first_block + i] = first_chunk
-            blk_nc[first_block + i] = m_units[t]
-            blk_tile[first_block + i] = tile_in
-            return tile_in + m_units[t]
-
-        tile = lax.fori_loop(0, q_units[t], fill_block, tile)
-    num_blocks = q_units[0] + q_units[1] + q_units[2] + q_units[3]
-    num_chunks = m_units[0] + m_units[1] + m_units[2] + m_units[3]
-
     emb_w = lambda lanes: wide(cols[0:D, :], lanes)
     emb_b = lambda lanes: wide(cols[D : 2 * D, :], lanes)
     gain_in = lambda lanes: wide(cols[2 * D : 3 * D, :], lanes)
     gain_out = lambda lanes: wide(cols[3 * D : 4 * D, :], lanes)
 
-    def mem_chunk(c, carry):
+    for b in range(n // 2):
+        raw = jnp.where(lane < 64, tiles[2 * b], pltpu.roll(tiles[2 * b + 1], 64, 1))
+        chosen = (posb[:, 128 * b : 128 * b + 128] == iota((128, 1), 0).astype(f32)).astype(f32)
+        got = nt(jnp.concatenate(split2(raw), axis=0).astype(bf16), chosen.astype(bf16))
+        run = got[0:8] + got[8:16]
+        for t in range(TASKS):
+            i = 8 * b + t
+            start, count, slot = table[0, i], table[1, i], table[2, i]
+            first = slot & 127
+            shift = (first - start) & 127
+            moved = pltpu.roll(run, shift, 1)
+            at = pl.multiple_of(slot - first, 128)
+            pltpu.store(
+                mfeat.at[:, pl.ds(at, 128)], moved, mask=(lane >= first) & (lane < first + count)
+            )
+            pltpu.store(mfeat.at[:, pl.ds(at + 128, 128)], moved, mask=lane < first + count - 128)
+
+    def mem_feats(c):
+        base, end = ch_base[c], ch_end[c]
         at = pl.ds(pl.multiple_of(c * KC, KC), KC)
-        base, end = ch_base[c], ch_end[c]
-        s_col = iota((KC, 1), 0) + c * KC
-        source = jnp.where(s_col < end, s_col, base).astype(f32)
-        chosen = (posm[...] == source).astype(f32).astype(bf16)
-        got = nt(f2_s[...], chosen)
-        feats_c = got[0:8] + got[8:16]
-        mfeat[:, at] = feats_c
-        hidden = embed_t(feats_c, emb_w(KC), emb_b(KC))
-        normed, unused = norm_t(hidden)
-        mn = (normed * gain_in(KC)).astype(bf16)
-        mnt[:, at] = mn
-        kt_s[:, at] = nn(wt_s[D : 2 * D, :], mn).astype(bf16)
-        live_row = ((iota((1, KC), 1) + c * KC) < end).astype(f32)
-        vt = nn(wt_s[2 * D : 3 * D, :], mn) * live_row
-        tail = jnp.where(iota((16, KC), 0) == 0, live_row, 0.0)
-        vt_s[:, at] = jnp.concatenate(
-            [part for p in range(4) for part in (vt[64 * p : 64 * p + 64], tail)], axis=0
-        ).astype(bf16)
-        kaug[at, :] = tn(mn, kdup_s[...]).astype(bf16)
-        live_col = (s_col < end).astype(f32)
-        low = iota((KC, 512), 1) & 127
-        vn = jnp.where((low == 64) | (low == 65), 1.0, tn(mn, vaug_w[...]))
-        vaug[at, :] = (vn * live_col).astype(bf16)
-        gk[at, :] = jnp.zeros((KC, D), f32)
-        gv[at, :] = jnp.zeros((KC, D), f32)
+        slot = iota((8, KC), 1) + c * KC
+        head = mfeat[:, pl.ds(pl.multiple_of(base, KC), 128)][:, 0:1]
+        live = (slot < end).astype(f32)[0:1]
+        return jnp.where(slot < end, mfeat[:, at], jnp.where(end > base, head, 0.0)), live
+
+    def mem_pair(i, carry):
+        found = []
+        for k in range(2):
+            c = 2 * i + k
+            feats_c, live = mem_feats(c)
+            normed, unused = norm_t(embed_t(feats_c, emb_w(KC), emb_b(KC)))
+            mnf = normed * gain_in(KC)
+            mn = mnf.astype(bf16)
+            keys_t = (nn(wt_s[D : 2 * D, :], mn) * live).astype(bf16)
+            vals_t = nn(wt_s[2 * D : 3 * D, :], mn) * live
+            tail = jnp.where(iota((16, KC), 0) == 0, live, 0.0)
+            vals_t = jnp.concatenate(
+                [part for p in range(4) for part in (vals_t[64 * p : 64 * p + 64], tail)], axis=0
+            ).astype(bf16)
+            both = nn(mnf.T.astype(bf16), w_s[:, D : 3 * D])
+            live_col = ((iota((KC, 1), 0) + c * KC) < ch_end[c]).astype(f32)
+            found.append((mn, keys_t, vals_t, both[:, :D], both[:, D:] * live_col))
+        for k in range(2):
+            at = pl.ds(pl.multiple_of((2 * i + k) * KC, KC), KC)
+            mnt[:, at], kt_s[:, at], vt_s[:, at] = found[k][0:3]
+            kn[at, :] = found[k][3].astype(bf16)
+            vn[at, :] = found[k][4].astype(bf16)
+            gk[at, :] = jnp.zeros((KC, D), f32)
+            gv[at, :] = jnp.zeros((KC, D), f32)
         return carry
 
-    lax.fori_loop(0, num_chunks, mem_chunk, 0)
-
-    coef2 = wide(coefb[...], 256)
+    lax.fori_loop(0, lax.div(num_chunks + 1, jnp.int32(2)), mem_pair, 0)
+
+    def spots(j):
+        return [pl.ds(pl.multiple_of(j * 512 + 256 * k, 256), 256) for k in range(2)]
 
     def pre_block(j, carry):
-        at = pl.ds(pl.multiple_of(j * 256, 256), 256)
-        kept = xs[:, at] * (1.0 - fs[:, at])
-        hidden = embed_t(kept, emb_w(256), emb_b(256))
-        normed, unused = norm_t(hidden)
-        qn = (normed * gain_in(256)).astype(bf16)
-        qn_s[:, at] = qn
-        q = nn(wt_s[0:D, :], qn).astype(bf16)
-        q_s[:, at] = q
-        scaled = q.astype(f32) * (coef2 * LOG2E)
-        upper = scaled.astype(bf16)
-        qhi[:, at] = upper
-        qlo[:, at] = (scaled - upper.astype(f32)).astype(bf16)
-        att[:, at] = jnp.zeros((D, 256), bf16)
-        il_s[:, at] = jnp.zeros((H, 256), f32)
-        dq_s[:, at] = jnp.zeros((D, 256), f32)
+        found = []
+        for at in spots(j):
+            kept = xs[:, at] * (1.0 - fs[:, at])
+            normed, unused = norm_t(embed_t(kept, emb_w(256), emb_b(256)))
+            qn = (normed * gain_in(256)).astype(bf16)
+            found.append((qn, nn(wt_s[0:D, :], qn).astype(bf16)))
+        for k, at in enumerate(spots(j)):
+            qn_s[:, at], q_s[:, at] = found[k]
+            att[:, at] = jnp.zeros((D, 256), bf16)
+            il_s[:, at] = jnp.zeros((H, 256), f32)
+            dq_s[:, at] = jnp.zeros((D, 256), f32)
         return carry
 
-    lax.fori_loop(0, qs // 256, pre_block, 0)
+    lax.fori_loop(0, qs // 512, pre_block, 0)
 
     zero_h = jnp.zeros((32, 128), bf16)
-
-    def diagonal(ref, at, p):
-        return [
-            jnp.concatenate([ref[64 * p : 64 * p + 32, at], zero_h], axis=1),
-            jnp.concatenate([zero_h, ref[64 * p + 32 : 64 * p + 64, at]], axis=1),
-        ]
-
-    def score_operand(at, p):
-        return jnp.concatenate(diagonal(qhi, at, p) + diagonal(qlo, at, p), axis=0)
+    zero_p = jnp.zeros((64, 256), bf16)
+
+    def pair(p, width):
+        return slice(width * p, width * p + width)
+
+    def half(p):
+        return slice(128 * (p // 2), 128 * (p // 2) + 128)
+
+    def two_heads(ref, at, p):
+        diag = jnp.concatenate(
+            [
+                jnp.concatenate([ref[64 * p : 64 * p + 32, at], zero_h], axis=1),
+                jnp.concatenate([zero_h, ref[64 * p + 32 : 64 * p + 64, at]], axis=1),
+            ],
+            axis=0,
+        )
+        return jnp.concatenate([zero_p, diag] if p % 2 else [diag, zero_p], axis=0)
+
+    def coef_row(p):
+        return LOG2E * jnp.concatenate(
+            [coefb[64 * p : 64 * p + 1, :], coefb[64 * p + 32 : 64 * p + 33, :]], axis=1
+        )
 
     def finish_forward(at, p, got):
         inverse = 1.0 / got[64:65, :]
@@ -573,27 +598,31 @@
         att[64 * p : 64 * p + 32, at] = (got[0:32, :128] * inverse[:, :128]).astype(bf16)
         att[64 * p + 32 : 64 * p + 64, at] = (got[32:64, 128:] * inverse[:, 128:]).astype(bf16)
 
-    def pair(p, width):
-        return slice(width * p, width * p + width)
-
     def forward_block(i, carry):
         at = pl.ds(pl.multiple_of(i * QB, QB), QB)
-        c0, nc, tile0 = blk_c0[i], blk_nc[i], blk_tile[i]
-
-        @pl.when(nc == 1)
-        def one():
-            keys = pl.ds(pl.multiple_of(c0 * KC, KC), KC)
+        c0, nc, tile0, count = blk_c0[i], blk_nc[i], blk_tile[i], blk_rows[i]
+
+        def one(rows):
+            keys = pl.ds(pl.multiple_of(c0 * KC, KC), rows)
             keep = jnp.minimum(tile0, E_CAP)
-            operands = [score_operand(at, p) for p in range(4)]
-            values = [vt_s[pair(p, VROWS), keys] for p in range(4)]
-            scores = [nn(kaug[keys, pair(p, 128)], operands[p]) for p in range(4)]
+            operands = [two_heads(q_s, at, p) for p in range(4)]
+            values = [vt_s[pair(p, VROWS), pl.ds(pl.multiple_of(c0 * KC, KC), KC)][:, :rows] for p in range(4)]
+            scores = [nn(kn[keys, half(p)], operands[p]) * coef_row(p) for p in range(4)]
             tops = [jnp.max(s, axis=0, keepdims=True) for s in scores]
             es = [jnp.exp2(scores[p] - tops[p]).astype(bf16) for p in range(4)]
             sums = [nn(values[p], es[p]) for p in range(4)]
             for p in range(4):
                 m_s[i, :, pair(p, 256)] = tops[p]
-                ebuf[keep, :, pair(p, 256)] = es[p]
+                ebuf[keep, :rows, pair(p, 256)] = es[p]
                 finish_forward(at, p, sums[p])
+
+        @pl.when(count <= KC_LOW)
+        def few():
+            one(KC_LOW)
+
+        @pl.when((count > KC_LOW) & (nc == 1))
+        def full():
+            one(KC)
 
         @pl.when(nc > 1)
         def many():
@@ -603,7 +632,7 @@
             def tops(c, inner):
                 keys = pl.ds(pl.multiple_of((c0 + c) * KC, KC), KC)
                 for p in range(4):
-                    s = nn(kaug[keys, pair(p, 128)], score_operand(at, p))
+                    s = nn(kn[keys, half(p)], two_heads(q_s, at, p)) * coef_row(p)
                     m_s[i, :, pair(p, 256)] = jnp.maximum(
                         m_s[i, :, pair(p, 256)], jnp.max(s, axis=0, keepdims=True)
                     )
@@ -615,7 +644,7 @@
                 keys = pl.ds(pl.multiple_of((c0 + c) * KC, KC), KC)
                 keep = jnp.minimum(tile0 + c, E_CAP)
                 for p in range(4):
-                    s = nn(kaug[keys, pair(p, 128)], score_operand(at, p))
+                    s = nn(kn[keys, half(p)], two_heads(q_s, at, p)) * coef_row(p)
                     e = jnp.exp2(s - m_s[i, :, pair(p, 256)]).astype(bf16)
                     ebuf[keep, :, pair(p, 256)] = e
                     acc[pair(p, VROWS), :] += nn(vt_s[pair(p, VROWS), keys], e)
@@ -636,19 +665,19 @@
     out_l[...] = jnp.zeros_like(out_l)
 
     def fold(v):
-        return v[:, :128] + v[:, 128:256]
-
-    def mid_block(j, carry):
-        at = pl.ds(pl.multiple_of(j * 256, 256), 256)
+        total = v[:, :128]
+        for k in range(1, v.shape[1] // 128):
+            total = total + v[:, 128 * k : 128 * k + 128]
+        return total
+
+    def mid_values(at):
         x = xs[:, at]
         fmask = fs[:, at]
-        kept = x * (1.0 - fmask)
-        hidden = embed_t(kept, emb_w(256), emb_b(256))
+        hidden = embed_t(x * (1.0 - fmask), emb_w(256), emb_b(256))
         attended = att[:, at]
         residual = hidden + nn(wt_s[3 * D : 4 * D, :], attended)
         normed, inverse = norm_t(residual)
         fn = (normed * gain_out(256)).astype(bf16)
-        fn_s[:, at] = fn
         head = nn(wht_s[...], fn)
         logits = head[0:C]
         err = head[C : C + F] - x
@@ -658,64 +687,68 @@
         e = jnp.exp(logits - top)
         total = jnp.sum(e, axis=0, keepdims=True)
         picked = jnp.sum(logits * hot, axis=0, keepdims=True)
-        out_l[0:1, :] += fold(
-            scale_t * label * (jnp.log(total) + top - picked)
-            + scale_r * jnp.sum(fmask * err * err, axis=0, keepdims=True)
+        loss = scale_t * label * (jnp.log(total) + top - picked) + scale_r * jnp.sum(
+            fmask * err * err, axis=0, keepdims=True
         )
         g_log = scale_t * label * (e / total - hot)
         g_rec = scale_r * fmask * 2.0 * err
         gho = jnp.concatenate([g_log, g_rec, jnp.zeros((8, 256), f32)], axis=0).astype(bf16)
-        gho_s[:, at] = gho
         g_final = nn(wh_s[:, :32], gho)
-        acc_gain[D : 2 * D, :] += fold(g_final * normed)
         g_res = norm_back_t(g_final, normed, inverse, gain_out(256))
-        gres[:, at] = g_res
         gb = g_res.astype(bf16)
-        gb_s[:, at] = gb
         ga = nn(w_s[:, 3 * D : 4 * D], gb).astype(bf16).astype(f32)
         attf = attended.astype(f32)
+        das, deltas = [], []
         for h in range(H):
             rows = slice(32 * h, 32 * h + 32)
             da = (ga[rows] * il_s[h : h + 1, at]).astype(bf16)
-            dap[rows, at] = da
-            dneg[h : h + 1, at] = -jnp.sum(da.astype(f32) * attf[rows], axis=0, keepdims=True)
+            das.append(da)
+            deltas.append(jnp.sum(da.astype(f32) * attf[rows], axis=0, keepdims=True))
+        return (
+            fold(loss), fold(g_final * normed),
+            fn, gho, g_res, gb, jnp.concatenate(das, axis=0), jnp.concatenate(deltas, axis=0),
+        )
+
+    def mid_block(j, carry):
+        found = [mid_values(at) for at in spots(j)]
+        out_l[0:1, :] += found[0][0] + found[1][0]
+        acc_gain[D : 2 * D, :] += found[0][1] + found[1][1]
+        for k, at in enumerate(spots(j)):
+            for ref, value in zip((fn_s, gho_s, gres, gb_s, dap, delta), found[k][2:]):
+                ref[:, at] = value
         return carry
 
-    lax.fori_loop(0, qs // 256, mid_block, 0)
-
-    zero_p = jnp.zeros((64, 256), bf16)
-    zero_t = jnp.zeros((48, 256), bf16)
-    r16 = iota((16, 256), 0)
-
-    def backward_chunk(at, c, e_of):
-        keys = pl.ds(pl.multiple_of(c * KC, KC), KC)
+    lax.fori_loop(0, qs // 512, mid_block, 0)
+
+    def backward_chunk(at, c, rows, e_of):
+        keys = pl.ds(pl.multiple_of(c * KC, KC), rows)
+        lanes = pl.ds(pl.multiple_of(c * KC, KC), KC)
         es = [e_of(p) for p in range(4)]
-        das = [jnp.concatenate(diagonal(dap, at, p), axis=0) for p in range(4)]
-        qds = [jnp.concatenate(diagonal(q_s, at, p), axis=0) for p in range(4)]
-        negs = dneg[:, at]
-        vals = [vaug[keys, pair(p, 128)] for p in range(4)]
-        kts = [kt_s[64 * p : 64 * p + 64, keys] for p in range(4)]
+        das = [two_heads(dap, at, p) for p in range(4)]
+        qds = [two_heads(q_s, at, p) for p in range(4)]
+        deltas = delta[:, at]
+        kts = [kt_s[64 * p : 64 * p + 64, lanes][:, :rows] for p in range(4)]
         old_dq = dq_s[:, at]
         old_gk = gk[keys, :]
         old_gv = gv[keys, :]
-        operands = []
+        dps = [nn(vn[keys, half(p)], das[p]) for p in range(4)]
+        dss = []
         for p in range(4):
-            neg = jnp.concatenate([negs[2 * p : 2 * p + 1], negs[2 * p + 1 : 2 * p + 2]], axis=1)
-            neg_hi = neg.astype(bf16).astype(f32)
-            tail = jnp.where(r16 == 0, neg_hi, jnp.where(r16 == 1, neg - neg_hi, 0.0)).astype(bf16)
-            operands.append(jnp.concatenate([das[p], tail, zero_t], axis=0))
-        dps = [nn(vals[p], operands[p]) for p in range(4)]
-        dss = [(es[p].astype(f32) * dps[p]).astype(bf16) for p in range(4)]
+            take = jnp.concatenate([deltas[2 * p : 2 * p + 1], deltas[2 * p + 1 : 2 * p + 2]], axis=1)
+            dss.append((es[p].astype(f32) * (dps[p] - take)).astype(bf16))
         dqs = [nn(kts[p], dss[p]) for p in range(4)]
 
         def by_key(grads, others):
-            halves = []
-            for a in (0, 2):
-                left = jnp.concatenate([grads[a], grads[a + 1]], axis=1)
-                upper = jnp.concatenate([others[a], zero_p], axis=1)
-                lower = jnp.concatenate([zero_p, others[a + 1]], axis=1)
-                halves.append(nt(left, jnp.concatenate([upper, lower], axis=0)))
-            return jnp.concatenate(halves, axis=1)
+            return jnp.concatenate(
+                [
+                    nt(
+                        jnp.concatenate([grads[a], grads[a + 1]], axis=1),
+                        jnp.concatenate([others[a], others[a + 1]], axis=1),
+                    )
+                    for a in (0, 2)
+                ],
+                axis=1,
+            )
 
         new_gv = old_gv + by_key(es, das)
         new_gk = old_gk + by_key(dss, qds)
@@ -728,30 +761,35 @@
 
     def backward_block(i, carry):
         at = pl.ds(pl.multiple_of(i * QB, QB), QB)
-        c0, nc, tile0 = blk_c0[i], blk_nc[i], blk_tile[i]
+        c0, nc, tile0, count = blk_c0[i], blk_nc[i], blk_tile[i], blk_rows[i]
         simple = (nc == 1) & (tile0 < E_CAP)
 
-        @pl.when(simple)
-        def one():
-            backward_chunk(at, c0, lambda p: ebuf[tile0, :, pair(p, 256)])
+        @pl.when(simple & (count <= KC_LOW))
+        def few():
+            backward_chunk(at, c0, KC_LOW, lambda p: ebuf[tile0, :KC_LOW, pair(p, 256)])
+
+        @pl.when(simple & (count > KC_LOW))
+        def full():
+            backward_chunk(at, c0, KC, lambda p: ebuf[tile0, :, pair(p, 256)])
 
         @pl.when(jnp.logical_not(simple))
         def many():
             def one_chunk(c, inner):
-                @pl.when(tile0 + c < E_CAP)
+                keys = pl.ds(pl.multiple_of((c0 + c) * KC, KC), KC)
+
+                @pl.when((tile0 + c < E_CAP) & (nc > 1))
                 def kept():
                     ecur[...] = ebuf[tile0 + c]
 
-                @pl.when(tile0 + c >= E_CAP)
+                @pl.when((tile0 + c >= E_CAP) | (nc == 1))
                 def again():
-                    keys = pl.ds(pl.multiple_of((c0 + c) * KC, KC), KC)
                     for p in range(4):
-                        s = nn(kaug[keys, pair(p, 128)], score_operand(at, p))
+                        s = nn(kn[keys, half(p)], two_heads(q_s, at, p)) * coef_row(p)
                         ecur[:, pair(p, 256)] = jnp.exp2(
                             s - m_s[i, :, pair(p, 256)]
                         ).astype(bf16)
 
-                backward_chunk(at, c0 + c, lambda p: ecur[:, pair(p, 256)])
+                backward_chunk(at, c0 + c, KC, lambda p: ecur[:, pair(p, 256)])
                 return inner
 
             lax.fori_loop(0, nc, one_chunk, 0)
@@ -760,96 +798,89 @@
 
     lax.fori_loop(0, num_blocks, backward_block, 0)
 
-    def sum_in(grad, normed, kept, lanes):
-        by_feature = jnp.concatenate(
+    def by_feature(grad, kept):
+        return jnp.concatenate(
             [kept[f : f + 1] * grad[32 * f : 32 * f + 32] for f in range(F)], axis=0
         )
-        outs = []
-        for v in (by_feature, grad):
-            total = v[:, :128]
-            for k in range(1, lanes // 128):
-                total = total + v[:, 128 * k : 128 * k + 128]
-            outs.append(total)
-        return outs
-
-    def post_block(j, carry):
-        at = pl.ds(pl.multiple_of(j * 256, 256), 256)
+
+    coef2 = wide(coefb[...], 256)
+
+    def post_values(at):
         kept = xs[:, at] * (1.0 - fs[:, at])
-        hidden = embed_t(kept, emb_w(256), emb_b(256))
-        normed, inverse = norm_t(hidden)
+        normed, inverse = norm_t(embed_t(kept, emb_w(256), emb_b(256)))
         dq = dq_s[:, at]
         gq = (dq * coef2).astype(bf16)
         prod = fold(dq * q_s[:, at].astype(f32))
-        for h in range(H):
-            acc_gain[4 * D + h : 4 * D + h + 1, :] += jnp.sum(
-                prod[32 * h : 32 * h + 32], axis=0, keepdims=True
-            )
-        gqkv[:, 0:D] += nt(qn_s[:, at], gq)
+        betas = jnp.concatenate(
+            [jnp.sum(prod[32 * h : 32 * h + 32], axis=0, keepdims=True) for h in range(H)], axis=0
+        )
         gqn = nn(w_s[:, 0:D], gq)
-        acc_gain[0:D, :] += fold(gqn * normed)
         gh = gres[:, at] + norm_back_t(gqn, normed, inverse, gain_in(256))
-        by_f, plain = sum_in(gh, normed, kept, 256)
-        acc_gain[2 * D : 3 * D, :] += by_f
-        acc_gain[3 * D : 4 * D, :] += plain
+        return gq, betas, fold(gqn * normed), fold(by_feature(gh, kept)), fold(gh)
+
+    def post_block(j, carry):
+        cuts = spots(j)
+        found = [post_values(at) for at in cuts]
+        qn = jnp.concatenate([qn_s[:, at] for at in cuts], axis=1)
+        gq = jnp.concatenate([found[0][0], found[1][0]], axis=1)
+        gqkv[:, 0:D] += nt(qn, gq)
+        for k, rows in ((1, slice(4 * D, 4 * D + H)), (2, slice(0, D)), (3, slice(2 * D, 3 * D)), (4, slice(3 * D, 4 * D))):
+            acc_gain[rows, :] += found[0][k] + found[1][k]
         return carry
 
     gqkv[...] = jnp.zeros_like(gqkv)
-    lax.fori_loop(0, qs // 256, post_block, 0)
+    lax.fori_loop(0, qs // 512, post_block, 0)
     gout[...] = nt(att[...], gb_s[...])
     ghead[...] = nt(fn_s[...], gho_s[...])
 
-    def mem_back(c, carry):
-        at = pl.ds(pl.multiple_of(c * KC, KC), KC)
-        live = ((iota((KC, 1), 0) + c * KC) < ch_end[c]).astype(f32)
-        coef_lane = carry
-        gk_c = (gk[at, :] * coef_lane * live).astype(bf16)
-        gv_c = (gv[at, :] * live).astype(bf16)
-        mn = mnt[:, at]
-        gqkv[:, D : 2 * D] += nn(mn, gk_c)
-        gqkv[:, 2 * D : 3 * D] += nn(mn, gv_c)
-        gmn = nt(w_s[:, D : 2 * D], gk_c) + nt(w_s[:, 2 * D : 3 * D], gv_c)
-        feats_c = mfeat[:, at]
-        hidden = embed_t(feats_c, emb_w(KC), emb_b(KC))
-        normed, inverse = norm_t(hidden)
-        dgain = gmn * normed
-        acc_gain[0:D, :] += dgain[:, :128] + dgain[:, 128:256] + dgain[:, 256:384]
-        gm = norm_back_t(gmn, normed, inverse, gain_in(KC))
-        by_f, plain = sum_in(gm, normed, feats_c, KC)
-        acc_gain[2 * D : 3 * D, :] += by_f
-        acc_gain[3 * D : 4 * D, :] += plain
-        return carry
+    def mem_back(i, coef_lane):
+        found = []
+        for k in range(2):
+            c = 2 * i + k
+            at = pl.ds(pl.multiple_of(c * KC, KC), KC)
+            feats_c, unused = mem_feats(c)
+            live = ((iota((KC, 1), 0) + c * KC) < ch_end[c]).astype(f32)
+            gk_c = (gk[at, :] * coef_lane * live).astype(bf16)
+            gv_c = (gv[at, :] * live).astype(bf16)
+            gmn = nt(w_s[:, D : 2 * D], gk_c) + nt(w_s[:, 2 * D : 3 * D], gv_c)
+            normed, inverse = norm_t(embed_t(feats_c, emb_w(KC), emb_b(KC)))
+            gm = norm_back_t(gmn, normed, inverse, gain_in(KC))
+            found.append((gk_c, gv_c, fold(gmn * normed), fold(by_feature(gm, feats_c)), fold(gm)))
+        mn = mnt[:, pl.ds(pl.multiple_of(2 * i * KC, KC), 2 * KC)]
+        gqkv[:, D : 2 * D] += nn(mn, jnp.concatenate([found[0][0], found[1][0]], axis=0))
+        gqkv[:, 2 * D : 3 * D] += nn(mn, jnp.concatenate([found[0][1], found[1][1]], axis=0))
+        for k, rows in ((2, slice(0, D)), (3, slice(2 * D, 3 * D)), (4, slice(3 * D, 4 * D))):
+            acc_gain[rows, :] += found[0][k] + found[1][k]
+        return coef_lane
 
     coef_lane = jnp.concatenate([coefb[0:128, :].T[0:1], coefb[128:256, :].T[0:1]], axis=1)
-    lax.fori_loop(0, num_chunks, mem_back, coef_lane)
+    lax.fori_loop(0, lax.div(num_chunks + 1, jnp.int32(2)), mem_back, coef_lane)
 
     out_sums[...] = jnp.broadcast_to(
         jnp.sum(acc_gain[...], axis=1, keepdims=True), (4 * D + H, 128)
     )
 
 
-def step_call(n, num_mem, small_size, xs, fs, ct, posm, units, an, gw):
-    num_q = xs.shape[1]
-    q_blocks, k_chunks = xs.shape[1] // QB, (num_mem + TASKS * (KC - 1)) // KC
-    qs, ks = q_blocks * QB, k_chunks * KC
+def step_call(n, num_mem, small_size, xs, fs, ct, posb, table, units, an, gw):
+    qs = xs.shape[1]
+    q_blocks, k_chunks = qs // QB, chunks_of(num_mem)
+    ks = k_chunks * KC
     V = pltpu.VMEM
     S = pltpu.SMEM
     vm = pl.BlockSpec(memory_space=pltpu.VMEM)
     sm = pl.BlockSpec(memory_space=pltpu.SMEM)
     scratch = [
         V((D, 4 * D), bf16), V((4 * D, D), bf16), V((D, 128), bf16), V((32, D), bf16),
-        V((D, 512), bf16), V((D, 512), bf16),
         V((4 * D, 128), f32), V((D, 128), f32),
-        V((16, num_mem), bf16), V((8, ks), f32),
-        V((ks, 512), bf16), V((ks, 512), bf16), V((D, ks), bf16), V((4 * VROWS, ks), bf16),
-        V((D, ks), bf16), V((ks, D), f32), V((ks, D), f32),
-        V((D, qs), bf16), V((D, qs), bf16), V((D, qs), bf16), V((D, qs), bf16), V((D, qs), bf16),
-        V((H, qs), f32), V((D, qs), f32), V((D, qs), bf16), V((32, qs), bf16), V((D, qs), bf16),
-        V((D, qs), bf16), V((H, qs), f32), V((D, qs), f32), V((8, qs), f32),
-        V((E_CAP + 1, KC, 1024), bf16), V((8, 128), f32), V((KC, 1024), bf16),
-        V((4 * VROWS, 256), f32), V((q_blocks, 1, 1024), f32),
-        V((4 * D + H, 128), f32),
+        V((8, ks + 128), f32), V((ks, D), bf16), V((ks, D), bf16), V((D, ks), bf16),
+        V((4 * VROWS, ks), bf16), V((D, ks), bf16), V((ks, D), f32), V((ks, D), f32),
+        V((D, qs), bf16), V((D, qs), bf16), V((D, qs), bf16), V((H, qs), f32), V((D, qs), f32),
+        V((D, qs), bf16), V((32, qs), bf16), V((D, qs), bf16), V((D, qs), bf16), V((H, qs), f32),
+        V((D, qs), f32),
+        V((E_CAP + 1, KC, 1024), bf16), V((KC, 1024), bf16), V((4 * VROWS, 256), f32),
+        V((q_blocks, 1, 1024), f32), V((4 * D + H, 128), f32),
         S((q_blocks,), jnp.int32), S((q_blocks,), jnp.int32), S((q_blocks,), jnp.int32),
-        S((k_chunks,), jnp.int32), S((k_chunks,), jnp.int32),
+        S((q_blocks,), jnp.int32), S((k_chunks,), jnp.int32), S((k_chunks,), jnp.int32),
     ]
     return pl.pallas_call(
         functools.partial(step_kernel, n, qs, num_mem, small_size),
@@ -860,11 +891,11 @@
             jax.ShapeDtypeStruct((4 * D + H, 128), f32),
             jax.ShapeDtypeStruct((8, 128), f32),
         ),
-        in_specs=[vm] * 4 + [sm] * 2 + [vm],
+        in_specs=[vm] * 4 + [sm] * 3 + [vm],
         out_specs=(vm,) * 5,
         scratch_shapes=scratch,
         compiler_params=pltpu.CompilerParams(vmem_limit_bytes=58 * 1024 * 1024),
-    )(xs, fs, ct, posm, units, an, gw)
+    )(xs, fs, ct, posb, table, units, an, gw)
 
 
 MESH = pl.DeviceIdType.MESH
@@ -900,7 +931,7 @@
 
 def gather_kernel(
     n, num_q, num_mem, w_qkv, w_out, w_heads, w_small, mfeat, qf, fm, qt, tc, tm, mt, mm,
-    gw, xs, fs, ct, posm, units_out,
+    gw, xs, fs, ct, posb, table, units_out,
     send_z, recv_z, send_s, recv_s, send_c, recv_c,
 ):
     planes = n // 8
@@ -960,53 +991,76 @@
     spread(0, done)
 
     task_row = iota((8, 256), 0)
-    marks = []
-    for b in range(num_q // 256):
-        marks.append((qt[:, 256 * b : 256 * b + 256] == task_row).astype(f32))
-    for b in range(num_mem // 256):
-        cut = slice(256 * b, 256 * b + 256)
-        marks.append(((mt[:, cut] == task_row) & (mm[:, cut] > 0)).astype(f32))
-    marks_all = jnp.concatenate(marks, axis=0)
-    tri = (iota((256, 256), 0) < iota((256, 256), 1)).astype(f32).astype(bf16)
-    ranks = nn(marks_all.astype(bf16), tri)
-    totals = jnp.sum(marks_all, axis=1, keepdims=True)
+    marks = [(qt[:, 256 * b : 256 * b + 256] == task_row).astype(f32) for b in range(num_q // 256)]
+    marks_q = jnp.concatenate(marks, axis=0)
+    before = (iota((256, 256), 0) < iota((256, 256), 1)).astype(f32).astype(bf16)
+    ranks = nn(marks_q.astype(bf16), before)
+    totals = jnp.sum(marks_q, axis=1, keepdims=True)
     task_col = iota((8, 1), 0)
 
-    def lay_out(first, count, unit):
-        carry = jnp.zeros((8, 1), f32)
-        before = []
-        for b in range(count):
-            before.append(carry)
-            at = 8 * (first + b)
-            carry = carry + totals[at : at + 8]
+    def bases_of(sums, unit):
         base = jnp.int32(0)
-        bases, counts, units = [], [], []
+        bases, counts, used = [], [], []
         base_vec = jnp.zeros((8, 1), f32)
         for t in range(TASKS):
-            num = jnp.sum(jnp.where(task_col == t, carry, 0.0)).astype(jnp.int32)
+            count = jnp.sum(jnp.where(task_col == t, sums, 0.0)).astype(jnp.int32)
             bases.append(base)
-            counts.append(num)
-            used_units = lax.div(num + (unit - 1), jnp.int32(unit))
-            units.append(used_units)
+            counts.append(count)
+            used.append(lax.div(count + (unit - 1), jnp.int32(unit)))
             base_vec = base_vec + jnp.where(task_col == t, base.astype(f32), 0.0)
-            base = base + used_units * unit
-        places = []
-        for b in range(count):
-            at = 8 * (first + b)
-            places.append(
-                jnp.sum(
-                    marks[first + b] * (base_vec + before[b] + ranks[at : at + 8]),
-                    axis=0,
-                    keepdims=True,
-                )
-                - (1.0 - jnp.sum(marks[first + b], axis=0, keepdims=True))
-            )
-        return jnp.concatenate(places, axis=1), bases, counts, units
-
-    place_q, q_base, q_count, q_units = lay_out(0, num_q // 256, QB)
-    place_m, m_base, m_count, m_units = lay_out(num_q // 256, num_mem // 256, KC)
-
-    posm[...] = place_m
+            base = base + used[t] * unit
+        return bases, counts, used, base_vec
+
+    carry = jnp.zeros((8, 1), f32)
+    carries = []
+    for b in range(num_q // 256):
+        carries.append(carry)
+        carry = carry + totals[8 * b : 8 * b + 8]
+    q_base, q_count, q_units, base_vec = bases_of(carry, QB)
+    place_q = jnp.concatenate(
+        [
+            jnp.sum(marks[b] * (base_vec + carries[b] + ranks[8 * b : 8 * b + 8]), axis=0, keepdims=True)
+            for b in range(num_q // 256)
+        ],
+        axis=1,
+    )
+
+    cuts = num_mem // 128
+    task_row = iota((8, 128), 0)
+    marks = []
+    for b in range(cuts):
+        cut = slice(128 * b, 128 * b + 128)
+        marks.append(((mt[:, cut] == task_row) & (mm[:, cut] > 0)).astype(f32))
+    marks_m = jnp.concatenate(marks, axis=0)
+    ranks = nn(marks_m.astype(bf16), before[:128, :128])
+    totals = jnp.broadcast_to(jnp.sum(marks_m, axis=1, keepdims=True), (8 * cuts, 128))
+    r_to = iota((8 * cuts, 8 * cuts), 0)
+    r_from = iota((8 * cuts, 8 * cuts), 1)
+    same_cut = (r_to // 8 == r_from // 8) & (r_from < r_to)
+    same_task = (r_to % 8 == r_from % 8) & (r_from < r_to)
+    low_totals = totals.astype(bf16)
+    starts = nn(same_cut.astype(f32).astype(bf16), low_totals)
+    earlier = nn(same_task.astype(f32).astype(bf16), low_totals)
+    last = slice(8 * cuts - 8, 8 * cuts)
+    m_base, m_count, m_units, base_vec = bases_of((earlier + totals)[last, 0:1], KC)
+    slots = earlier + jnp.concatenate([base_vec] * cuts, axis=0)
+    posb[...] = jnp.concatenate(
+        [
+            jnp.sum(marks[b] * (starts[8 * b : 8 * b + 8] + ranks[8 * b : 8 * b + 8] + 1.0), axis=0, keepdims=True)
+            - 1.0
+            for b in range(cuts)
+        ],
+        axis=1,
+    )
+    eye = r_to == r_from
+
+    def as_row(column):
+        return jnp.sum(jnp.where(eye, wide(column, 8 * cuts), 0.0), axis=0, keepdims=True)
+
+    row_t = iota((8, 8 * cuts), 0)
+    table[...] = jnp.where(
+        row_t == 0, as_row(starts), jnp.where(row_t == 1, as_row(totals), as_row(slots))
+    ).astype(jnp.int32)
     for t in range(TASKS):
         units_out[t] = m_base[t]
         units_out[TASKS + t] = m_count[t]
@@ -1052,7 +1106,7 @@
 def gather_call(n, w_qkv, w_out, w_heads, w_small, mfeat, qf, fm, qt, tc, tm, mt, mm):
     planes = n // 8
     num_q, num_mem = qf.shape[1], mt.shape[1]
-    qs = sizes(n, num_q, num_mem)[0] * QB
+    qs = blocks_of(num_q) * QB
     vm = pl.BlockSpec(memory_space=pltpu.VMEM)
     dma = pltpu.SemaphoreType.DMA
     return pl.pallas_call(
@@ -1063,10 +1117,11 @@
             jax.ShapeDtypeStruct((8, qs), f32),
             jax.ShapeDtypeStruct((8, qs), f32),
             jax.ShapeDtypeStruct((1, num_mem), f32),
+            jax.ShapeDtypeStruct((8, num_mem // 16), jnp.int32),
             jax.ShapeDtypeStruct((5 * TASKS,), jnp.int32),
         ),
         in_specs=[vm] * 12,
-        out_specs=(vm,) * 5 + (pl.BlockSpec(memory_space=pltpu.SMEM),),
+        out_specs=(vm,) * 6 + (pl.BlockSpec(memory_space=pltpu.SMEM),),
         scratch_shapes=[
             dma((planes - 1,)), dma((planes - 1,)), dma((planes, 3)), dma((planes, 3)),
             dma((planes, 4)), dma((planes, 4)),
@@ -1225,8 +1280,9 @@
 
 def update_kernel(g, tot, *refs):
     weights, firsts, seconds = refs[0:4], refs[4:8], refs[8:12]
-    new, first_o, second_o, copy_o = refs[12:16], refs[16:20], refs[20:24], refs[24:28]
-    loss_o, norm_o, gq_s, go_s = refs[28:32]
+    new, first_o, second_o = refs[12:16], refs[16:20], refs[20:24]
+    copy_o = (refs[24], refs[25], None, refs[26])
+    loss_o, norm_o, gq_s, go_s = refs[27:31]
     for c in range(6):
         gq_s[pl.ds(c, 8, stride=6), :] = g[8 * c : 8 * c + 8, :]
     for c in range(2):
@@ -1250,20 +1306,21 @@
         new[i][...] = weight_new
         first_o[i][...] = first_new
         second_o[i][...] = second_new
-        copy_o[i][...] = weight_new.astype(bf16)
+        if copy_o[i] is not None:
+            copy_o[i][...] = weight_new.astype(bf16)
 
 
 def update_call(g, tot, weights, firsts, seconds):
     vm = pl.BlockSpec(memory_space=pltpu.VMEM)
     shapes = [w.shape for w in weights]
     outs = [jax.ShapeDtypeStruct(s, f32) for s in shapes] * 3
-    outs += [jax.ShapeDtypeStruct(s, bf16) for s in shapes]
+    outs += [jax.ShapeDtypeStruct(s, bf16) for s in shapes[:2] + shapes[3:]]
     outs += [jax.ShapeDtypeStruct((1, 1), f32)] * 2
     return pl.pallas_call(
         update_kernel,
         out_shape=tuple(outs),
         in_specs=[vm] * 14,
-        out_specs=(vm,) * 18,
+        out_specs=(vm,) * 17,
         scratch_shapes=[pltpu.VMEM((48, 128), f32), pltpu.VMEM((16, 128), f32)],
     )(g, tot, *weights, *firsts, *seconds)
 
@@ -1283,14 +1340,15 @@
     firsts = (tiles(m_qkv), tiles(m_out), row(m_heads), row(m_small))
     seconds = (tiles(v_qkv), tiles(v_out), row(v_heads), row(v_small))
     tm, mt = row(target_mask), row(memory_task)
-    gw, xs, fs, ct, posm, units = gather_call(
+    gw, xs, fs, ct, posb, table, units = gather_call(
         n, *weights, memory_feats.T, query_feats.T, feature_mask.T, row(query_task),
         row(target_class), tm, mt, row(memory_mask),
     )
-    found = step_call(n, mt.shape[1], w_small.shape[0] * n, xs, fs, ct, posm, units, anneal, gw)
+    found = step_call(n, mt.shape[1], w_small.shape[0] * n, xs, fs, ct, posb, table, units, anneal, gw)
     grads, totals = reduce_call(n, w_small.shape[0], *found)
     outs = update_call(grads, totals, weights, firsts, seconds)
-    return tuple(out.reshape(-1) for out in outs)
+    outs = [out.reshape(-1) for out in outs]
+    return tuple(outs[:14] + [outs[2].astype(bf16)] + outs[14:])
 
 
 def solution(mesh):

time: 82.5 us -> 74.5 us (0.903)
  Pallas kernels: 79.4 us -> 71.9 us
    pallas_call x1, Pallas kernels: 39.8 us -> 32.6 us  [step_call(): pl.pallas_call(functools.partial(step_kernel, n, qs, num_mem, small_size)...]
where the time goes in v3:
time: 74.5 us
  Pallas kernels  71.9 us (97%)
  between operations  1.34 us (2%)
    pallas_call x1, Pallas kernels, step_call(): pl.pallas_call(functools.partial(step_kernel, n, qs, num_mem, small_size)...  32.6 us
    pallas_call x1, Pallas kernels, reduce_call(): pl.pallas_call(functools.partial(reduce_kernel, n, per_small), out_shape=...  21.6 us
    pallas_call x1, Pallas kernels, gather_call(): pl.pallas_call(functools.partial(gather_kernel, n, num_q, num_mem), out_s...  15.9 us
    pallas_call x1, Pallas kernels, update_call(): pl.pallas_call(update_kernel, out_shape=tuple(outs), in_specs=[vm] * 14,...  1.76 us

profile of v3, /device:TPU:0, one launch (start us, length us, event | category | flops | bytes accessed | tf_op | source)
XLA Modules:
  0.0 74.5 jit_solution(13469924763892939530)
XLA Ops:
  1.3 15.9 %shard_map.340 = (bf16[32,80,128]{2,1,0:T(8,128)(2,1)}, f32[8,1536]{1,0:T(8,128)}, f32[8,1536]{1,0:T(8,128)}, f32[8,1536]{1,0:T(8,128)}, f32[1,2048]{1,0:T(1,128)}, /*index=5*/s32[8,128]{1,0:T(8,128)}, s32[20]{0:T(128)}) custom-call(f32[48,128]{1,0:T(8,128)} %bitcast.37, f32[16,128]{1,0:T(8,128)} %bitcast.39, f32[1,192]{1,0:T(1,128)} %bitcast.49, ...), custom_call_target="tpu_custom_call" | custom-call | tf_op jit(solution)/shard_map/pallas_call | solution.py:1112
  17.2 32.6 %shard_map.341 = (f32[256,768]{1,0:T(8,128)}, f32[256,256]{1,0:T(8,128)}, f32[256,32]{1,0:T(8,128)}, f32[1032,128]{1,0:T(8,128)}, f32[8,128]{1,0:T(8,128)}) custom-call(f32[8,1536]{1,0:T(8,128)} %get-tuple-element.49.xs, f32[8,1536]{1,0:T(8,128)} %get-tuple-element.50.fs, f32[8,1536]{1,0:T(8,128)} %get-tuple-element.51.ct, ...), custom_call_target="tpu_custom_call" | custom-call | tf_op jit(solution)/shard_map/pallas_call | solution.py:885
  49.9 21.6 %shard_map.342 = (f32[80,128]{1,0:T(8,128)}, f32[1,128]{1,0:T(1,128)}) custom-call(f32[256,768]{1,0:T(8,128)} %get-tuple-element.56.gqkv, f32[256,256]{1,0:T(8,128)} %get-tuple-element.57.gout, f32[256,32]{1,0:T(8,128)} %get-tuple-element.58.ghead, f32[1032,128]{1,0:T(8,128)} %get-tuple-element.59.sums_in, f32[8,128]{1,0:T(8,128)} %get-tuple-element.60.l_in), custom_call_target="tpu_custom_call" | custom-call | tf_op jit(solution)/shard_map/pallas_call | solution.py:1262
  71.5 1.8 %shard_map.343 = (f32[48,128]{1,0:T(8,128)}, f32[16,128]{1,0:T(8,128)}, f32[1,192]{1,0:T(1,128)}, f32[1,33]{1,0:T(1,128)}, f32[48,128]{1,0:T(8,128)}, /*index=5*...) custom-call(f32[80,128]{1,0:T(8,128)} %get-tuple-element.61.g, ...), custom_call_target="tpu_custom_call" | custom-call | tf_op jit(solution)/shard_map/pallas_call | solution.py:1319
  73.3 0.0 copy-start
  73.3 0.7 copy-done
  73.9 0.5 convert_element_type.3
Async XLA Ops:
  73.3 0.7 copy-start

commit v4 on v3

--- a/solution.py
+++ b/solution.py
@@ -336,7 +336,8 @@
 KC = 384
 KC_LOW = 320
 VROWS = 80
-E_CAP = 16
+E_CAP = 12
+STEP_VMEM = 40 * 1024 * 1024
 SMALL_LANE = 88
 COUNT_LANE = 122
 
@@ -384,6 +385,19 @@
     return jnp.concatenate(parts, axis=0)
 
 
+def fold(v):
+    total = v[:, :128]
+    for k in range(1, v.shape[1] // 128):
+        total = total + v[:, 128 * k : 128 * k + 128]
+    return total
+
+
+def by_feature(grad, kept):
+    return jnp.concatenate(
+        [kept[f : f + 1] * grad[32 * f : 32 * f + 32] for f in range(F)], axis=0
+    )
+
+
 def norm_t(v):
     centred = v - jnp.mean(v, axis=0, keepdims=True)
     inverse = lax.rsqrt(jnp.mean(centred * centred, axis=0, keepdims=True) + eps_norm)
@@ -411,24 +425,20 @@
 
 def step_kernel(
     n, qs, num_mem, small_size,
-    xs, fs, ct, posb, table, units, an, gw,
-    gqkv, gout, ghead, out_sums, out_l,
-    w_s, wt_s, wh_s, wht_s,
-    cols, coefb,
+    table, an, gw,
+    xs, fs, qn_s, q_s, att, gb_s, fn_s, gho_s, gres, dq_s, gkv, w_q, cols, coefb, acc_gain, out_l,
+    ct, w_s, wt_s, wh_s, wht_s,
     mfeat, kn, vn, kt_s, vt_s, mnt, gk, gv,
-    qn_s, q_s, att, il_s, gres, fn_s, gho_s, gb_s, dap, delta, dq_s,
-    ebuf, ecur, acc, m_s, acc_gain,
+    il_s, dap, delta, ebuf, ecur, acc, m_s,
     blk_c0, blk_nc, blk_tile, blk_rows, ch_base, ch_end,
 ):
     planes = n // 8
     per_small = small_size // n
     k_chunks = ch_base.shape[0]
 
-    m_base = [units[t] for t in range(TASKS)]
-    m_count = [units[TASKS + t] for t in range(TASKS)]
-    m_units = [units[2 * TASKS + t] for t in range(TASKS)]
-    q_base = [units[3 * TASKS + t] for t in range(TASKS)]
-    q_units = [units[4 * TASKS + t] for t in range(TASKS)]
+    m_base, m_count, m_units, q_base, q_units = (
+        [table[3, TASKS * k + t] for t in range(TASKS)] for k in range(5)
+    )
     num_blocks = q_units[0] + q_units[1] + q_units[2] + q_units[3]
     num_chunks = m_units[0] + m_units[1] + m_units[2] + m_units[3]
     for c in range(k_chunks):
@@ -467,6 +477,13 @@
     heads = jnp.where(lane_w < C + F, heads, 0.0)
     wh_s[...] = heads.astype(bf16)
     wht_s[...] = heads.T[:32].astype(bf16)
+
+    for b in range(qs // 128):
+        block = gw[n + b, 0:48, :].astype(f32)
+        cut = slice(128 * b, 128 * b + 128)
+        xs[:, cut] = block[0:8] + block[8:16] + block[16:24]
+        fs[:, cut] = block[24:32]
+        ct[:, cut] = block[32:40]
 
     small_rows = jnp.concatenate([tile[0:1] for tile in tiles], axis=0)
     lane_n = iota((n, 128), 1)
@@ -495,9 +512,10 @@
     gain_in = lambda lanes: wide(cols[2 * D : 3 * D, :], lanes)
     gain_out = lambda lanes: wide(cols[3 * D : 4 * D, :], lanes)
 
+    places = gw[n, 48 : 48 + n // 2, :].astype(f32)
     for b in range(n // 2):
         raw = jnp.where(lane < 64, tiles[2 * b], pltpu.roll(tiles[2 * b + 1], 64, 1))
-        chosen = (posb[:, 128 * b : 128 * b + 128] == iota((128, 1), 0).astype(f32)).astype(f32)
+        chosen = (places[b : b + 1] == iota((128, 1), 0).astype(f32)).astype(f32)
         got = nt(jnp.concatenate(split2(raw), axis=0).astype(bf16), chosen.astype(bf16))
         run = got[0:8] + got[8:16]
         for t in range(TASKS):
@@ -664,12 +682,6 @@
     acc_gain[...] = jnp.zeros_like(acc_gain)
     out_l[...] = jnp.zeros_like(out_l)
 
-    def fold(v):
-        total = v[:, :128]
-        for k in range(1, v.shape[1] // 128):
-            total = total + v[:, 128 * k : 128 * k + 128]
-        return total
-
     def mid_values(at):
         x = xs[:, at]
         fmask = fs[:, at]
@@ -798,40 +810,8 @@
 
     lax.fori_loop(0, num_blocks, backward_block, 0)
 
-    def by_feature(grad, kept):
-        return jnp.concatenate(
-            [kept[f : f + 1] * grad[32 * f : 32 * f + 32] for f in range(F)], axis=0
-        )
-
-    coef2 = wide(coefb[...], 256)
-
-    def post_values(at):
-        kept = xs[:, at] * (1.0 - fs[:, at])
-        normed, inverse = norm_t(embed_t(kept, emb_w(256), emb_b(256)))
-        dq = dq_s[:, at]
-        gq = (dq * coef2).astype(bf16)
-        prod = fold(dq * q_s[:, at].astype(f32))
-        betas = jnp.concatenate(
-            [jnp.sum(prod[32 * h : 32 * h + 32], axis=0, keepdims=True) for h in range(H)], axis=0
-        )
-        gqn = nn(w_s[:, 0:D], gq)
-        gh = gres[:, at] + norm_back_t(gqn, normed, inverse, gain_in(256))
-        return gq, betas, fold(gqn * normed), fold(by_feature(gh, kept)), fold(gh)
-
-    def post_block(j, carry):
-        cuts = spots(j)
-        found = [post_values(at) for at in cuts]
-        qn = jnp.concatenate([qn_s[:, at] for at in cuts], axis=1)
-        gq = jnp.concatenate([found[0][0], found[1][0]], axis=1)
-        gqkv[:, 0:D] += nt(qn, gq)
-        for k, rows in ((1, slice(4 * D, 4 * D + H)), (2, slice(0, D)), (3, slice(2 * D, 3 * D)), (4, slice(3 * D, 4 * D))):
-            acc_gain[rows, :] += found[0][k] + found[1][k]
-        return carry
-
-    gqkv[...] = jnp.zeros_like(gqkv)
-    lax.fori_loop(0, qs // 512, post_block, 0)
-    gout[...] = nt(att[...], gb_s[...])
-    ghead[...] = nt(fn_s[...], gho_s[...])
+    gkv[...] = jnp.zeros_like(gkv)
+    w_q[...] = w_s[:, 0:D]
 
     def mem_back(i, coef_lane):
         found = []
@@ -847,8 +827,8 @@
             gm = norm_back_t(gmn, normed, inverse, gain_in(KC))
             found.append((gk_c, gv_c, fold(gmn * normed), fold(by_feature(gm, feats_c)), fold(gm)))
         mn = mnt[:, pl.ds(pl.multiple_of(2 * i * KC, KC), 2 * KC)]
-        gqkv[:, D : 2 * D] += nn(mn, jnp.concatenate([found[0][0], found[1][0]], axis=0))
-        gqkv[:, 2 * D : 3 * D] += nn(mn, jnp.concatenate([found[0][1], found[1][1]], axis=0))
+        gkv[:, 0:D] += nn(mn, jnp.concatenate([found[0][0], found[1][0]], axis=0))
+        gkv[:, D : 2 * D] += nn(mn, jnp.concatenate([found[0][1], found[1][1]], axis=0))
         for k, rows in ((2, slice(0, D)), (3, slice(2 * D, 3 * D)), (4, slice(3 * D, 4 * D))):
             acc_gain[rows, :] += found[0][k] + found[1][k]
         return coef_lane
@@ -856,46 +836,39 @@
     coef_lane = jnp.concatenate([coefb[0:128, :].T[0:1], coefb[128:256, :].T[0:1]], axis=1)
     lax.fori_loop(0, lax.div(num_chunks + 1, jnp.int32(2)), mem_back, coef_lane)
 
-    out_sums[...] = jnp.broadcast_to(
-        jnp.sum(acc_gain[...], axis=1, keepdims=True), (4 * D + H, 128)
-    )
-
-
-def step_call(n, num_mem, small_size, xs, fs, ct, posb, table, units, an, gw):
-    qs = xs.shape[1]
-    q_blocks, k_chunks = qs // QB, chunks_of(num_mem)
-    ks = k_chunks * KC
+
+def step_call(n, num_mem, small_size, table, an, gw):
+    q_blocks, k_chunks = gw.shape[0] - n, chunks_of(num_mem)
+    qs, ks = q_blocks * QB, k_chunks * KC
     V = pltpu.VMEM
     S = pltpu.SMEM
+    A = jax.ShapeDtypeStruct
     vm = pl.BlockSpec(memory_space=pltpu.VMEM)
     sm = pl.BlockSpec(memory_space=pltpu.SMEM)
+    outs = (
+        A((8, qs), f32), A((8, qs), f32), A((D, qs), bf16), A((D, qs), bf16), A((D, qs), bf16),
+        A((D, qs), bf16), A((D, qs), bf16), A((32, qs), bf16), A((D, qs), f32), A((D, qs), f32),
+        A((D, 2 * D), f32), A((D, D), bf16), A((4 * D, 128), f32), A((D, 128), f32),
+        A((4 * D + H, 128), f32), A((8, 128), f32),
+    )
     scratch = [
-        V((D, 4 * D), bf16), V((4 * D, D), bf16), V((D, 128), bf16), V((32, D), bf16),
-        V((4 * D, 128), f32), V((D, 128), f32),
+        V((8, qs), f32), V((D, 4 * D), bf16), V((4 * D, D), bf16), V((D, 128), bf16), V((32, D), bf16),
         V((8, ks + 128), f32), V((ks, D), bf16), V((ks, D), bf16), V((D, ks), bf16),
         V((4 * VROWS, ks), bf16), V((D, ks), bf16), V((ks, D), f32), V((ks, D), f32),
-        V((D, qs), bf16), V((D, qs), bf16), V((D, qs), bf16), V((H, qs), f32), V((D, qs), f32),
-        V((D, qs), bf16), V((32, qs), bf16), V((D, qs), bf16), V((D, qs), bf16), V((H, qs), f32),
-        V((D, qs), f32),
+        V((H, qs), f32), V((D, qs), bf16), V((H, qs), f32),
         V((E_CAP + 1, KC, 1024), bf16), V((KC, 1024), bf16), V((4 * VROWS, 256), f32),
-        V((q_blocks, 1, 1024), f32), V((4 * D + H, 128), f32),
+        V((q_blocks, 1, 1024), f32),
         S((q_blocks,), jnp.int32), S((q_blocks,), jnp.int32), S((q_blocks,), jnp.int32),
         S((q_blocks,), jnp.int32), S((k_chunks,), jnp.int32), S((k_chunks,), jnp.int32),
     ]
     return pl.pallas_call(
         functools.partial(step_kernel, n, qs, num_mem, small_size),
-        out_shape=(
-            jax.ShapeDtypeStruct((D, 3 * D), f32),
-            jax.ShapeDtypeStruct((D, D), f32),
-            jax.ShapeDtypeStruct((D, 32), f32),
-            jax.ShapeDtypeStruct((4 * D + H, 128), f32),
-            jax.ShapeDtypeStruct((8, 128), f32),
-        ),
-        in_specs=[vm] * 4 + [sm] * 3 + [vm],
-        out_specs=(vm,) * 5,
+        out_shape=outs,
+        in_specs=[sm, sm, vm],
+        out_specs=(vm,) * len(outs),
         scratch_shapes=scratch,
-        compiler_params=pltpu.CompilerParams(vmem_limit_bytes=58 * 1024 * 1024),
-    )(xs, fs, ct, posb, table, units, an, gw)
+        compiler_params=pltpu.CompilerParams(vmem_limit_bytes=STEP_VMEM),
+    )(table, an, gw)
 
 
 MESH = pl.DeviceIdType.MESH
@@ -930,10 +903,18 @@
 
 
 def gather_kernel(
-    n, num_q, num_mem, w_qkv, w_out, w_heads, w_small, mfeat, qf, fm, qt, tc, tm, mt, mm,
-    gw, xs, fs, ct, posb, table, units_out,
-    send_z, recv_z, send_s, recv_s, send_c, recv_c,
+    n, num_q, num_mem, *refs,
 ):
+    sources, refs = refs[:12], refs[12:]
+    gw, table, keep = refs[:3]
+    copied, refs = refs[3:15], refs[15:]
+    send_z, recv_z, send_s, recv_s, send_c, recv_c, load = refs
+    loads = [
+        pltpu.make_async_copy(sources[i], copied[i], load.at[i]) for i in range(len(sources))
+    ]
+    for copy in loads:
+        copy.start()
+    w_qkv, w_out, w_heads, w_small, mfeat, qf, fm, qt, tc, tm, mt, mm = copied
     planes = n // 8
     me, core, square, plane = where_am_i(planes)
     in_plane = core + 2 * square
@@ -941,6 +922,8 @@
     s_of = [plane * 8 + lax.rem(square + k, 4) * 2 + core for k in range(1, 4)]
     c_of = plane * 8 + square * 2 + (1 - core)
     barrier = greet(z_of + s_of + [c_of])
+    for copy in loads:
+        copy.wait()
 
     rows = []
     for c in range(6):
@@ -1044,13 +1027,13 @@
     last = slice(8 * cuts - 8, 8 * cuts)
     m_base, m_count, m_units, base_vec = bases_of((earlier + totals)[last, 0:1], KC)
     slots = earlier + jnp.concatenate([base_vec] * cuts, axis=0)
-    posb[...] = jnp.concatenate(
+    places_m = jnp.concatenate(
         [
             jnp.sum(marks[b] * (starts[8 * b : 8 * b + 8] + ranks[8 * b : 8 * b + 8] + 1.0), axis=0, keepdims=True)
             - 1.0
             for b in range(cuts)
         ],
-        axis=1,
+        axis=0,
     )
     eye = r_to == r_from
 
@@ -1058,16 +1041,19 @@
         return jnp.sum(jnp.where(eye, wide(column, 8 * cuts), 0.0), axis=0, keepdims=True)
 
     row_t = iota((8, 8 * cuts), 0)
-    table[...] = jnp.where(
+    lane_t = iota((8, 8 * cuts), 1)
+    numbers = jnp.where(
         row_t == 0, as_row(starts), jnp.where(row_t == 1, as_row(totals), as_row(slots))
     ).astype(jnp.int32)
-    for t in range(TASKS):
-        units_out[t] = m_base[t]
-        units_out[TASKS + t] = m_count[t]
-        units_out[2 * TASKS + t] = m_units[t]
-        units_out[3 * TASKS + t] = q_base[t]
-        units_out[4 * TASKS + t] = q_units[t]
-    qs = xs.shape[1]
+    for i, number in enumerate(m_base + m_count + m_units + q_base + q_units):
+        numbers = jnp.where((row_t == 3) & (lane_t == i), number, numbers)
+    table[...] = numbers
+    gw[n, 48 : 48 + cuts, :] = places_m.astype(bf16)
+    heads_low = jnp.concatenate([w_heads[:, 128:], jnp.zeros((1, 256 - per_head), f32)], axis=1)
+    small_row = jnp.concatenate([w_small[...], jnp.zeros((1, 128 - per_small), f32)], axis=1)
+    keep[...] = jnp.where(
+        row8 == 0, w_heads[:, :128], jnp.where(row8 == 1, heads_low, small_row)
+    )
     xq = qf[...]
     fmq = fm[...].astype(f32)
     row8 = iota((8, num_q), 0)
@@ -1077,15 +1063,13 @@
     q_rows = jnp.concatenate(
         list(split3(xq)) + [fmq, label_rows, jnp.zeros((8, num_q), f32)], axis=0
     ).astype(bf16)
-    for b in range(qs // 256):
+    for b in range((gw.shape[0] - n) // 2):
         chosen = (
             (place_q == (iota((256, 1), 0) + 256 * b).astype(f32)).astype(f32).astype(bf16)
         )
-        got = nt(q_rows, chosen)
-        cut = slice(256 * b, 256 * b + 256)
-        xs[:, cut] = got[0:8] + got[8:16] + got[16:24]
-        fs[:, cut] = got[24:32]
-        ct[:, cut] = got[32:40]
+        got = nt(q_rows, chosen).astype(bf16)
+        gw[n + 2 * b, 0:48, :] = got[:, :128]
+        gw[n + 2 * b + 1, 0:48, :] = got[:, 128:]
 
 
     for k in range(1, planes):
@@ -1105,6 +1089,7 @@
 
 def gather_call(n, w_qkv, w_out, w_heads, w_small, mfeat, qf, fm, qt, tc, tm, mt, mm):
     planes = n // 8
+    operands = (w_qkv, w_out, w_heads, w_small, mfeat, qf, fm, qt, tc, tm, mt, mm)
     num_q, num_mem = qf.shape[1], mt.shape[1]
     qs = blocks_of(num_q) * QB
     vm = pl.BlockSpec(memory_space=pltpu.VMEM)
@@ -1112,27 +1097,25 @@
     return pl.pallas_call(
         functools.partial(gather_kernel, n, num_q, num_mem),
         out_shape=(
-            jax.ShapeDtypeStruct((n, 80, 128), bf16),
-            jax.ShapeDtypeStruct((8, qs), f32),
-            jax.ShapeDtypeStruct((8, qs), f32),
-            jax.ShapeDtypeStruct((8, qs), f32),
-            jax.ShapeDtypeStruct((1, num_mem), f32),
+            jax.ShapeDtypeStruct((n + qs // 128, 80, 128), bf16),
             jax.ShapeDtypeStruct((8, num_mem // 16), jnp.int32),
-            jax.ShapeDtypeStruct((5 * TASKS,), jnp.int32),
+            jax.ShapeDtypeStruct((8, 128), f32),
         ),
-        in_specs=[vm] * 12,
-        out_specs=(vm,) * 6 + (pl.BlockSpec(memory_space=pltpu.SMEM),),
-        scratch_shapes=[
+        in_specs=[pl.BlockSpec(memory_space=pltpu.HBM)] * 12,
+        out_specs=(vm,) * 3,
+        scratch_shapes=[pltpu.VMEM(v.shape, v.dtype) for v in operands]
+        + [
             dma((planes - 1,)), dma((planes - 1,)), dma((planes, 3)), dma((planes, 3)),
-            dma((planes, 4)), dma((planes, 4)),
+            dma((planes, 4)), dma((planes, 4)), dma((12,)),
         ],
         compiler_params=pltpu.CompilerParams(collective_id=0, has_side_effects=True),
-    )(w_qkv, w_out, w_heads, w_small, mfeat, qf, fm, qt, tc, tm, mt, mm)
+    )(*operands)
 
 
 def reduce_kernel(
-    n, per_small, gqkv, gout, ghead, sums_in, l_in, g_out, t_out,
-    s_s, r_core, t_square, r_square, t_plane, r_plane, own, n_mine, n_all,
+    n, per_small,
+    xs, fs, qn_s, q_s, att, gb_s, fn_s, gho_s, gres, dq_s, gkv, w_q, cols, coefb, sums_in, l_in,
+    g_out, t_out, gq, acc_gain, s_s, r_core, t_square, r_square, t_plane, r_plane, own, n_mine, n_all,
     send_c, recv_c, send_s, recv_s, send_z, recv_z, send_n, recv_n,
 ):
     planes = n // 8
@@ -1145,11 +1128,48 @@
     c_of = plane * 8 + square * 2 + (1 - core)
     barrier = greet(a_of)
 
+    def over(rows, lanes):
+        return wide(cols[rows, :], lanes)
+
+    def spots(j):
+        return [pl.ds(pl.multiple_of(j * 512 + 256 * k, 256), 256) for k in range(2)]
+
+    coef2 = wide(coefb[...], 256)
+
+    def post_values(at):
+        kept = xs[:, at] * (1.0 - fs[:, at])
+        normed, inverse = norm_t(embed_t(kept, over(slice(0, D), 256), over(slice(D, 2 * D), 256)))
+        dq = dq_s[:, at]
+        low = (dq * coef2).astype(bf16)
+        prod = fold(dq * q_s[:, at].astype(f32))
+        betas = jnp.concatenate(
+            [jnp.sum(prod[32 * h : 32 * h + 32], axis=0, keepdims=True) for h in range(H)], axis=0
+        )
+        gqn = nn(w_q[...], low)
+        gh = gres[:, at] + norm_back_t(gqn, normed, inverse, over(slice(2 * D, 3 * D), 256))
+        return low, betas, fold(gqn * normed), fold(by_feature(gh, kept)), fold(gh)
+
+    def post_block(j, carry):
+        cuts = spots(j)
+        found = [post_values(at) for at in cuts]
+        qn = jnp.concatenate([qn_s[:, at] for at in cuts], axis=1)
+        gq_c = jnp.concatenate([found[0][0], found[1][0]], axis=1)
+        gq[...] += nt(qn, gq_c)
+        for k, rows in ((1, slice(4 * D, 4 * D + H)), (2, slice(0, D)), (3, slice(2 * D, 3 * D)), (4, slice(3 * D, 4 * D))):
+            acc_gain[rows, :] += found[0][k] + found[1][k]
+        return carry
+
+    gq[...] = jnp.zeros_like(gq)
+    acc_gain[...] = sums_in[...]
+    lax.fori_loop(0, xs.shape[1] // 512, post_block, 0)
+    gout = nt(att[...], gb_s[...])
+    ghead = nt(fn_s[...], gho_s[...])
+
     used = 4 * D + 2 * H
     row = iota((used, 128), 0)
     lan = iota((used, 128), 1)
     row_dev = jnp.floor((row.astype(f32) + 0.5) * (1.0 / per_small)).astype(jnp.int32)
-    sums = sums_in[...]
+    sums = jnp.sum(acc_gain[...], axis=1, keepdims=True)
     small = jnp.concatenate(
         [
             sums[2 * D : 3 * D],
@@ -1157,7 +1177,7 @@
             sums[0:D],
             sums[D : 2 * D],
             sums[4 * D : 4 * D + H] * (32 ** (-0.5)),
-            jnp.zeros((H, 128), f32),
+            jnp.zeros((H, 1), f32),
         ],
         axis=0,
     )
@@ -1170,7 +1190,7 @@
     to_flat_l = iota((32, 256), 1)
     lane_row = jnp.floor((to_flat_l.astype(f32) + 0.5) * (1.0 / (C + F))).astype(jnp.int32)
     to_flat = ((to_flat_l - (C + F) * lane_row == to_flat_r) & (to_flat_r < C + F)).astype(f32)
-    spread_h = nn(ghead[...].astype(bf16), to_flat.astype(bf16))
+    spread_h = nn(ghead.astype(bf16), to_flat.astype(bf16))
     lr = iota((D, 256), 1)
     lr_row = jnp.floor((lr.astype(f32) + 0.5) * (1.0 / (C + F))).astype(jnp.int32)
     spread_h = jnp.where(lr_row == (iota((D, 256), 0) & (rows_dev - 1)), spread_h, 0.0)
@@ -1183,7 +1203,8 @@
             head_flat[:, :128],
             jnp.where(r8 == 1, head_flat[:, 128:], jnp.where(r8 == 2, small_rows_out[d : d + 1], 0.0)),
         )
-        block = [gqkv[rows, 128 * k : 128 * k + 128] for k in range(6)]
+        block = [gq[rows, 128 * k : 128 * k + 128] for k in range(2)]
+        block += [gkv[rows, 128 * k : 128 * k + 128] for k in range(4)]
         block += [gout[rows, 128 * k : 128 * k + 128] for k in range(2)]
         block += [extra, jnp.zeros((8, 128), f32)]
         s_s[place_of(d, planes)] = jnp.concatenate(block, axis=0).astype(bf16)
@@ -1265,24 +1286,35 @@
             jax.ShapeDtypeStruct((rows, 128), f32),
             jax.ShapeDtypeStruct((1, 128), f32),
         ),
-        in_specs=[vm] * 5,
+        in_specs=[vm] * len(grads),
         out_specs=(vm, vm),
         scratch_shapes=[
+            V((D, D), f32), V((4 * D + H, 128), f32),
             V((n, rows, 128), bf16), V((4, planes, rows, 128), bf16), V((3, planes, rows, 128), bf16),
             V((3, planes, rows, 128), bf16), V((z, rows, 128), bf16), V((z, rows, 128), bf16),
             V((planes, rows, 128), f32), V((1, 128), f32), V((n - 1, 1, 128), f32),
             dma((4,)), dma((4,)), dma((3, planes)), dma((3, planes)), dma((z,)), dma((z,)),
             dma((n - 1,)), dma((n - 1,)),
         ],
-        compiler_params=pltpu.CompilerParams(collective_id=1, has_side_effects=True),
+        compiler_params=pltpu.CompilerParams(
+            collective_id=1, has_side_effects=True, vmem_limit_bytes=16 * 1024 * 1024
+        ),
     )(*grads)
 
 
 def update_kernel(g, tot, *refs):
-    weights, firsts, seconds = refs[0:4], refs[4:8], refs[8:12]
-    new, first_o, second_o = refs[12:16], refs[16:20], refs[20:24]
-    copy_o = (refs[24], refs[25], None, refs[26])
-    loss_o, norm_o, gq_s, go_s = refs[27:31]
+    w_qkv, w_out, keep = refs[0:3]
+    firsts, seconds, refs = refs[3:7], refs[7:11], refs[11:]
+    per_head, per_small = firsts[2].shape[1], firsts[3].shape[1]
+    weights = (
+        w_qkv[...],
+        w_out[...],
+        jnp.concatenate([keep[0:1, :], keep[1:2, : per_head - 128]], axis=1),
+        keep[2:3, :per_small],
+    )
+    new, first_o, second_o = refs[0:4], refs[4:8], refs[8:12]
+    copy_o = (refs[12], refs[13], None, refs[14])
+    flat_o, loss_o, norm_o, gq_s, go_s = refs[15:20]
     for c in range(6):
         gq_s[pl.ds(c, 8, stride=6), :] = g[8 * c : 8 * c + 8, :]
     for c in range(2):
@@ -1292,7 +1324,6 @@
     loss_o[...] = jnp.sum(jnp.where(first_half, 0.0, tot[...]), axis=1, keepdims=True)
     norm_o[...] = norm
     factor = jnp.minimum(1.0, max_norm / (norm + 1e-06))
-    per_head, per_small = weights[2].shape[1], weights[3].shape[1]
     grads = (
         gq_s[...],
         go_s[...],
@@ -1301,28 +1332,32 @@
     )
     for i in range(4):
         first_new, second_new, weight_new = adamw(
-            weights[i][...], firsts[i][...], seconds[i][...], grads[i], factor, float(STEP), learn_rates[i]
+            weights[i], firsts[i][...], seconds[i][...], grads[i], factor, float(STEP), learn_rates[i]
         )
         new[i][...] = weight_new
         first_o[i][...] = first_new
         second_o[i][...] = second_new
         if copy_o[i] is not None:
             copy_o[i][...] = weight_new.astype(bf16)
-
-
-def update_call(g, tot, weights, firsts, seconds):
+        else:
+            flat_o[...] = weight_new.astype(bf16).reshape(weight_new.shape[1])
+
+
+def update_call(g, tot, w_qkv, w_out, keep, firsts, seconds):
     vm = pl.BlockSpec(memory_space=pltpu.VMEM)
-    shapes = [w.shape for w in weights]
+    shapes = [v.shape for v in firsts]
     outs = [jax.ShapeDtypeStruct(s, f32) for s in shapes] * 3
     outs += [jax.ShapeDtypeStruct(s, bf16) for s in shapes[:2] + shapes[3:]]
+    outs += [jax.ShapeDtypeStruct((shapes[2][1],), bf16)]
     outs += [jax.ShapeDtypeStruct((1, 1), f32)] * 2
     return pl.pallas_call(
         update_kernel,
         out_shape=tuple(outs),
-        in_specs=[vm] * 14,
-        out_specs=(vm,) * 17,
+        in_specs=[vm] * 13,
+        out_specs=(vm,) * 18,
         scratch_shapes=[pltpu.VMEM((48, 128), f32), pltpu.VMEM((16, 128), f32)],
-    )(g, tot, *weights, *firsts, *seconds)
+        compiler_params=pltpu.CompilerParams(vmem_limit_bytes=4 * 1024 * 1024),
+    )(g, tot, w_qkv, w_out, keep, *firsts, *seconds)
 
 
 def local_fast(
@@ -1340,15 +1375,15 @@
     firsts = (tiles(m_qkv), tiles(m_out), row(m_heads), row(m_small))
     seconds = (tiles(v_qkv), tiles(v_out), row(v_heads), row(v_small))
     tm, mt = row(target_mask), row(memory_task)
-    gw, xs, fs, ct, posb, table, units = gather_call(
+    gw, table, keep = gather_call(
         n, *weights, memory_feats.T, query_feats.T, feature_mask.T, row(query_task),
         row(target_class), tm, mt, row(memory_mask),
     )
-    found = step_call(n, mt.shape[1], w_small.shape[0] * n, xs, fs, ct, posb, table, units, anneal, gw)
+    found = step_call(n, mt.shape[1], w_small.shape[0] * n, table, anneal, gw)
     grads, totals = reduce_call(n, w_small.shape[0], *found)
-    outs = update_call(grads, totals, weights, firsts, seconds)
+    outs = update_call(grads, totals, weights[0], weights[1], keep, firsts, seconds)
     outs = [out.reshape(-1) for out in outs]
-    return tuple(outs[:14] + [outs[2].astype(bf16)] + outs[14:])
+    return tuple(outs[:14] + [outs[15]] + [outs[14]] + outs[16:])
 
 
 def solution(mesh):
@@ -1378,7 +1413,7 @@
     n = mesh.shape["mem"]
 
     def choose(*args):
-        if D // n == 8 and args[6].shape[0] <= 4096:
+        if D // n == 8 and args[6].shape[0] in (2048, 4096):
             return local_fast(n, *args)
         return local(*args)
 

time: 74.5 us -> 69.9 us (0.938); the launches traced: 74.5 us -> 69 us
  Pallas kernels: 71.9 us -> 65.4 us
  local copies, waits for them, and re-layouts: 0.67 us -> 1.91 us
    pallas_call x1, Pallas kernels: 32.6 us -> 27.3 us  [step_call(): pl.pallas_call(functools.partial(step_kernel, n, qs, num_mem, small_size)...]
    unnamed x2 -> x26, local copies, waits for them, and re-layouts: 0.67 us -> 1.91 us
    pallas_call x1, Pallas kernels: 1.76 us -> 0.84 us  [update_call(): pl.pallas_call(update_kernel, out_shape=tuple(outs), in_specs=[vm] * 13,...]
where the time goes in v4:
time: 69.9 us; the launch traced here: 69 us
  Pallas kernels  65.4 us (94%)
  local copies, waits for them, and re-layouts  1.91 us (3%)
  between operations  1.67 us (2%)
    pallas_call x1, Pallas kernels, step_call(): pl.pallas_call(functools.partial(step_kernel, n, qs, num_mem, small_size)...  27.3 us
    pallas_call x1, Pallas kernels, reduce_call(): pl.pallas_call(functools.partial(reduce_kernel, n, per_small), out_shape=...  21.9 us
    pallas_call x1, Pallas kernels, gather_call(): pl.pallas_call(functools.partial(gather_kernel, n, num_q, num_mem), out_s...  15.4 us
    unnamed x26, local copies, waits for them, and re-layouts  1.91 us

profile of v4, /device:TPU:0, one launch (start us, length us, event | category | flops | bytes accessed | tf_op | source)
XLA Modules:
  0.0 69.0 jit_solution(11550269540602068601)
XLA Ops:
  1.3 15.4 %shard_map.340 = (bf16[44,80,128]{2,1,0:T(8,128)(2,1)}, s32[8,128]{1,0:T(8,128)}, f32[8,128]{1,0:T(8,128)}) custom-call(f32[48,128]{1,0:T(8,128)} %bitcast.37, f32[16,128]{1,0:T(8,128)} %bitcast.39, f32[1,192]{1,0:T(1,128)} %bitcast.57, f32[1,33]{1,0:T(1,128)} %bitcast.58, f32[8,64]{1,0:T(8,128)} %bitcast.53, f32[8,1024]{1,0:T(8,128)} %bitcast.49, ...), custom_call_target="tpu_custom_call" | custom-call | tf_op jit(solution)/shard_map/pallas_call | solution.py:1097
  16.8 0.0 copy-start
  16.8 1.2 %copy-done = bf16[44,80,128]{2,1,0:T(8,128)(2,1)S(1)} copy-done((bf16[44,80,128]{2,1,0:T(8,128)(2,1)S(1)}, bf16[44,80,128]{2,1,0:T(8,128)(2,1)}, u32[]{:S(2)}) %copy-start) | copy-done | bytes 901144
  17.9 0.0 copy-start.7
  17.9 0.7 copy-done.7
  18.6 27.3 %shard_map.341 = (f32[8,1536]{1,0:T(8,128)S(1)}, f32[8,1536]{1,0:T(8,128)S(1)}, bf16[256,1536]{1,0:T(8,128)(2,1)S(1)}, bf16[256,1536]{1,0:T(8,128)(2,1)S(1)}, bf...) custom-call(s32[8,128]{1,0:T(8,128)S(1)} %copy-done.7, ...), custom_call_target="tpu_custom_call" | custom-call | tf_op jit(solution)/shard_map/pallas_call | solution.py:864
  45.9 0.0 copy-start.1
  45.9 0.0 copy-start.2
  45.9 0.0 copy-start.3
  45.9 0.0 copy-start.4
  45.9 0.0 copy-start.5
  45.9 0.0 copy-start.6
  46.0 0.0 copy-start.8
  46.0 0.0 copy-start.9
  46.0 0.0 copy-start.10
  46.0 0.0 copy-start.11
  46.0 0.0 copy-start.12
  46.0 21.9 %shard_map.342 = (f32[80,128]{1,0:T(8,128)S(1)}, f32[1,128]{1,0:T(1,128)S(1)}) custom-call(f32[8,1536]{1,0:T(8,128)S(1)} %get-tuple-element.59.xs, f32[8,1536]{1,0:T(8,128)S(1)} %get-tuple-element.60.fs, bf16[256,1536]{1,0:T(8,128)(2,1)S(1)} %get-tuple-element.61.qn_s, bf16[256,1536]{1,0:T(8,128)(2,1)S(1)} %get-tuple-element.62.q_s, ...), custom_call_target="tpu_custom_call" | custom-call | tf_op jit(solution)/shard_map/pallas_call | solution.py:1283
  67.9 0.0 copy-done.1
  67.9 0.0 copy-done.2
  67.9 0.0 copy-done.3
  67.9 0.0 copy-done.4
  67.9 0.0 copy-done.5
  67.9 0.0 copy-done.6
  68.0 0.0 copy-done.8
  68.0 0.0 copy-done.9
  68.0 0.0 copy-done.10
  68.0 0.0 copy-done.11
  68.0 0.0 copy-done.12
  68.0 0.8 %shard_map.343 = (f32[48,128]{1,0:T(8,128)}, f32[16,128]{1,0:T(8,128)}, f32[1,192]{1,0:T(1,128)}, f32[1,33]{1,0:T(1,128)}, f32[48,128]{1,0:T(8,128)}, /*index=5*...) custom-call(f32[80,128]{1,0:T(8,128)S(1)} %get-tuple-element.75.g, ...), custom_call_target="tpu_custom_call" | custom-call | tf_op jit(solution)/shard_map/pallas_call | solution.py:1353
Async XLA Ops:
  16.8 1.2 %copy-start = (bf16[44,80,128]{2,1,0:T(8,128)(2,1)S(1)}, bf16[44,80,128]{2,1,0:T(8,128)(2,1)}, u32[]{:S(2)}) copy-start(bf16[44,80,128]{2,1,0:T(8,128)(2,1)} %get-tuple-element.58.gw) | copy-start | bytes 2703364
  17.9 0.7 copy-start.7
  45.9 22.0 %copy-start.1 = (f32[6144]{0:T(1024)S(1)}, f32[6144]{0:T(1024)}, u32[]{:S(2)}) copy-start(f32[6144]{0:T(1024)} %param.30) | copy-start | bytes 73732
  45.9 22.0 %copy-start.2 = (f32[2048]{0:T(1024)S(1)}, f32[2048]{0:T(1024)}, u32[]{:S(2)}) copy-start(f32[2048]{0:T(1024)} %param.31) | copy-start | bytes 24580
  45.9 22.0 %copy-start.3 = (f32[6144]{0:T(1024)S(1)}, f32[6144]{0:T(1024)}, u32[]{:S(2)}) copy-start(f32[6144]{0:T(1024)} %param.34) | copy-start | bytes 73732
  45.9 22.0 %copy-start.4 = (f32[6144]{0:T(1024)S(1)}, f32[6144]{0:T(1024)}, u32[]{:S(2)}) copy-start(f32[6144]{0:T(1024)} %param.38) | copy-start | bytes 73732
  45.9 22.0 %copy-start.5 = (f32[2048]{0:T(1024)S(1)}, f32[2048]{0:T(1024)}, u32[]{:S(2)}) copy-start(f32[2048]{0:T(1024)} %param.35) | copy-start | bytes 24580
  45.9 22.0 %copy-start.6 = (f32[2048]{0:T(1024)S(1)}, f32[2048]{0:T(1024)}, u32[]{:S(2)}) copy-start(f32[2048]{0:T(1024)} %param.39) | copy-start | bytes 24580
  46.0 22.0 %copy-start.8 = (f32[8,128]{1,0:T(8,128)S(1)}, f32[8,128]{1,0:T(8,128)}, u32[]{:S(2)}) copy-start(f32[8,128]{1,0:T(8,128)} %get-tuple-element.77.refs_2_) | copy-start | bytes 12292
  46.0 22.0 %copy-start.9 = (f32[192]{0:T(256)S(1)}, f32[192]{0:T(256)}, u32[]{:S(2)}) copy-start(f32[192]{0:T(256)} %param.36) | copy-start | bytes 2308
  46.0 22.0 %copy-start.10 = (f32[192]{0:T(256)S(1)}, f32[192]{0:T(256)}, u32[]{:S(2)}) copy-start(f32[192]{0:T(256)} %param.40) | copy-start | bytes 2308
  46.0 22.0 %copy-start.11 = (f32[33]{0:T(128)S(1)}, f32[33]{0:T(128)}, u32[]{:S(2)}) copy-start(f32[33]{0:T(128)} %param.37) | copy-start | bytes 400
  46.0 22.0 %copy-start.12 = (f32[33]{0:T(128)S(1)}, f32[33]{0:T(128)}, u32[]{:S(2)}) copy-start(f32[33]{0:T(128)} %param.41) | copy-start | bytes 400

commit v5 on v4

--- a/solution.py
+++ b/solution.py
@@ -337,7 +337,10 @@
 KC_LOW = 320
 VROWS = 80
 E_CAP = 12
-STEP_VMEM = 40 * 1024 * 1024
+STEP_VMEM = 44 * 1024 * 1024
+PRE_SPAN = 3
+MID_SPAN = 6
+MEM_SPAN = 2
 SMALL_LANE = 88
 COUNT_LANE = 122
 
@@ -398,6 +401,13 @@
     )
 
 
+def added(found, k):
+    total = found[0][k]
+    for one in found[1:]:
+        total = total + one[k]
+    return total
+
+
 def norm_t(v):
     centred = v - jnp.mean(v, axis=0, keepdims=True)
     inverse = lax.rsqrt(jnp.mean(centred * centred, axis=0, keepdims=True) + eps_norm)
@@ -420,22 +430,28 @@
 
 def chunks_of(num_mem):
     chunks = (num_mem + TASKS * (KC - 1)) // KC
-    return chunks + chunks % 2
+    return -(-chunks // MEM_SPAN) * MEM_SPAN
 
 
 def step_kernel(
     n, qs, num_mem, small_size,
-    table, an, gw,
+    an, gw,
     xs, fs, qn_s, q_s, att, gb_s, fn_s, gho_s, gres, dq_s, gkv, w_q, cols, coefb, acc_gain, out_l,
     ct, w_s, wt_s, wh_s, wht_s,
     mfeat, kn, vn, kt_s, vt_s, mnt, gk, gv,
     il_s, dap, delta, ebuf, ecur, acc, m_s,
-    blk_c0, blk_nc, blk_tile, blk_rows, ch_base, ch_end,
+    blk_c0, blk_nc, blk_tile, blk_rows, ch_base, ch_end, numbers, table, loaded,
 ):
     planes = n // 8
     per_small = small_size // n
     k_chunks = ch_base.shape[0]
 
+    for i in range(num_mem // 2048):
+        both = gw[n + 1 + i, 48:64, :].astype(f32)
+        numbers[:, 128 * i : 128 * i + 128] = (both[0:8] + both[8:16]).astype(jnp.int32)
+    copy = pltpu.make_async_copy(numbers, table, loaded)
+    copy.start()
+    copy.wait()
     m_base, m_count, m_units, q_base, q_units = (
         [table[3, TASKS * k + t] for t in range(TASKS)] for k in range(5)
     )
@@ -540,8 +556,8 @@
 
     def mem_pair(i, carry):
         found = []
-        for k in range(2):
-            c = 2 * i + k
+        for k in range(MEM_SPAN):
+            c = MEM_SPAN * i + k
             feats_c, live = mem_feats(c)
             normed, unused = norm_t(embed_t(feats_c, emb_w(KC), emb_b(KC)))
             mnf = normed * gain_in(KC)
@@ -555,8 +571,8 @@
             both = nn(mnf.T.astype(bf16), w_s[:, D : 3 * D])
             live_col = ((iota((KC, 1), 0) + c * KC) < ch_end[c]).astype(f32)
             found.append((mn, keys_t, vals_t, both[:, :D], both[:, D:] * live_col))
-        for k in range(2):
-            at = pl.ds(pl.multiple_of((2 * i + k) * KC, KC), KC)
+        for k in range(MEM_SPAN):
+            at = pl.ds(pl.multiple_of((MEM_SPAN * i + k) * KC, KC), KC)
             mnt[:, at], kt_s[:, at], vt_s[:, at] = found[k][0:3]
             kn[at, :] = found[k][3].astype(bf16)
             vn[at, :] = found[k][4].astype(bf16)
@@ -564,26 +580,26 @@
             gv[at, :] = jnp.zeros((KC, D), f32)
         return carry
 
-    lax.fori_loop(0, lax.div(num_chunks + 1, jnp.int32(2)), mem_pair, 0)
-
-    def spots(j):
-        return [pl.ds(pl.multiple_of(j * 512 + 256 * k, 256), 256) for k in range(2)]
+    lax.fori_loop(0, lax.div(num_chunks + MEM_SPAN - 1, jnp.int32(MEM_SPAN)), mem_pair, 0)
+
+    def spots(j, span):
+        return [pl.ds(pl.multiple_of((j * span + k) * 256, 256), 256) for k in range(span)]
 
     def pre_block(j, carry):
         found = []
-        for at in spots(j):
+        for at in spots(j, PRE_SPAN):
             kept = xs[:, at] * (1.0 - fs[:, at])
             normed, unused = norm_t(embed_t(kept, emb_w(256), emb_b(256)))
             qn = (normed * gain_in(256)).astype(bf16)
             found.append((qn, nn(wt_s[0:D, :], qn).astype(bf16)))
-        for k, at in enumerate(spots(j)):
+        for k, at in enumerate(spots(j, PRE_SPAN)):
             qn_s[:, at], q_s[:, at] = found[k]
             att[:, at] = jnp.zeros((D, 256), bf16)
             il_s[:, at] = jnp.zeros((H, 256), f32)
             dq_s[:, at] = jnp.zeros((D, 256), f32)
         return carry
 
-    lax.fori_loop(0, qs // 512, pre_block, 0)
+    lax.fori_loop(0, qs // (256 * PRE_SPAN), pre_block, 0)
 
     zero_h = jnp.zeros((32, 128), bf16)
     zero_p = jnp.zeros((64, 256), bf16)
@@ -616,31 +632,38 @@
         att[64 * p : 64 * p + 32, at] = (got[0:32, :128] * inverse[:, :128]).astype(bf16)
         att[64 * p + 32 : 64 * p + 64, at] = (got[32:64, 128:] * inverse[:, 128:]).astype(bf16)
 
+    def forward_some(blocks, rows):
+        work = []
+        for i in blocks:
+            at = pl.ds(pl.multiple_of(i * QB, QB), QB)
+            first = blk_c0[i] * KC
+            keys = pl.ds(pl.multiple_of(first, KC), rows)
+            operands = [two_heads(q_s, at, p) for p in range(4)]
+            values = [vt_s[pair(p, VROWS), pl.ds(pl.multiple_of(first, KC), KC)][:, :rows] for p in range(4)]
+            work += [(kn[keys, half(p)], operands[p], coef_row(p), values[p]) for p in range(4)]
+        scores = [nn(k, o) * c for k, o, c, unused in work]
+        tops = [jnp.max(s, axis=0, keepdims=True) for s in scores]
+        es = [jnp.exp2(s - top).astype(bf16) for s, top in zip(scores, tops)]
+        sums = [nn(w[3], e) for w, e in zip(work, es)]
+        for n_th, i in enumerate(blocks):
+            at = pl.ds(pl.multiple_of(i * QB, QB), QB)
+            keep = jnp.minimum(blk_tile[i], E_CAP)
+            for p in range(4):
+                m_s[i, :, pair(p, 256)] = tops[4 * n_th + p]
+                ebuf[keep, :rows, pair(p, 256)] = es[4 * n_th + p]
+                finish_forward(at, p, sums[4 * n_th + p])
+
     def forward_block(i, carry):
         at = pl.ds(pl.multiple_of(i * QB, QB), QB)
         c0, nc, tile0, count = blk_c0[i], blk_nc[i], blk_tile[i], blk_rows[i]
 
-        def one(rows):
-            keys = pl.ds(pl.multiple_of(c0 * KC, KC), rows)
-            keep = jnp.minimum(tile0, E_CAP)
-            operands = [two_heads(q_s, at, p) for p in range(4)]
-            values = [vt_s[pair(p, VROWS), pl.ds(pl.multiple_of(c0 * KC, KC), KC)][:, :rows] for p in range(4)]
-            scores = [nn(kn[keys, half(p)], operands[p]) * coef_row(p) for p in range(4)]
-            tops = [jnp.max(s, axis=0, keepdims=True) for s in scores]
-            es = [jnp.exp2(scores[p] - tops[p]).astype(bf16) for p in range(4)]
-            sums = [nn(values[p], es[p]) for p in range(4)]
-            for p in range(4):
-                m_s[i, :, pair(p, 256)] = tops[p]
-                ebuf[keep, :rows, pair(p, 256)] = es[p]
-                finish_forward(at, p, sums[p])
-
         @pl.when(count <= KC_LOW)
         def few():
-            one(KC_LOW)
+            forward_some([i], KC_LOW)
 
         @pl.when((count > KC_LOW) & (nc == 1))
         def full():
-            one(KC)
+            forward_some([i], KC)
 
         @pl.when(nc > 1)
         def many():
@@ -674,7 +697,27 @@
 
         return carry
 
-    lax.fori_loop(0, num_blocks, forward_block, 0)
+    def forward_pair(j, carry):
+        i = 2 * j
+        count = jnp.maximum(blk_rows[i], blk_rows[i + 1])
+
+        @pl.when(count <= KC_LOW)
+        def few():
+            forward_some([i, i + 1], KC_LOW)
+
+        @pl.when((count > KC_LOW) & (count <= KC))
+        def full():
+            forward_some([i, i + 1], KC)
+
+        @pl.when(count > KC)
+        def apart():
+            lax.fori_loop(i, i + 2, forward_block, 0)
+
+        return carry
+
+    pairs = lax.div(num_blocks, jnp.int32(2))
+    lax.fori_loop(0, pairs, forward_pair, 0)
+    lax.fori_loop(2 * pairs, num_blocks, forward_block, 0)
 
     weight_a = an[0]
     scale_t = weight_a / count_t
@@ -722,33 +765,29 @@
         )
 
     def mid_block(j, carry):
-        found = [mid_values(at) for at in spots(j)]
-        out_l[0:1, :] += found[0][0] + found[1][0]
-        acc_gain[D : 2 * D, :] += found[0][1] + found[1][1]
-        for k, at in enumerate(spots(j)):
+        found = [mid_values(at) for at in spots(j, MID_SPAN)]
+        out_l[0:1, :] += added(found, 0)
+        acc_gain[D : 2 * D, :] += added(found, 1)
+        for k, at in enumerate(spots(j, MID_SPAN)):
             for ref, value in zip((fn_s, gho_s, gres, gb_s, dap, delta), found[k][2:]):
                 ref[:, at] = value
         return carry
 
-    lax.fori_loop(0, qs // 512, mid_block, 0)
-
-    def backward_chunk(at, c, rows, e_of):
-        keys = pl.ds(pl.multiple_of(c * KC, KC), rows)
-        lanes = pl.ds(pl.multiple_of(c * KC, KC), KC)
-        es = [e_of(p) for p in range(4)]
-        das = [two_heads(dap, at, p) for p in range(4)]
-        qds = [two_heads(q_s, at, p) for p in range(4)]
-        deltas = delta[:, at]
-        kts = [kt_s[64 * p : 64 * p + 64, lanes][:, :rows] for p in range(4)]
-        old_dq = dq_s[:, at]
-        old_gk = gk[keys, :]
-        old_gv = gv[keys, :]
-        dps = [nn(vn[keys, half(p)], das[p]) for p in range(4)]
-        dss = []
-        for p in range(4):
-            take = jnp.concatenate([deltas[2 * p : 2 * p + 1], deltas[2 * p + 1 : 2 * p + 2]], axis=1)
-            dss.append((es[p].astype(f32) * (dps[p] - take)).astype(bf16))
-        dqs = [nn(kts[p], dss[p]) for p in range(4)]
+    lax.fori_loop(0, qs // (256 * MID_SPAN), mid_block, 0)
+
+    def backward_some(items, rows):
+        work = []
+        for at, c, e_of in items:
+            lanes = pl.ds(pl.multiple_of(c * KC, KC), KC)
+            keys = pl.ds(pl.multiple_of(c * KC, KC), rows)
+            es = [e_of(p) for p in range(4)]
+            das = [two_heads(dap, at, p) for p in range(4)]
+            qds = [two_heads(q_s, at, p) for p in range(4)]
+            kts = [kt_s[64 * p : 64 * p + 64, lanes][:, :rows] for p in range(4)]
+            vals = [vn[keys, half(p)] for p in range(4)]
+            work.append((at, keys, es, das, qds, kts, vals, delta[:, at], dq_s[:, at]))
+        old_gk = gk[work[0][1], :]
+        old_gv = gv[work[0][1], :]
 
         def by_key(grads, others):
             return jnp.concatenate(
@@ -762,14 +801,33 @@
                 axis=1,
             )
 
-        new_gv = old_gv + by_key(es, das)
-        new_gk = old_gk + by_key(dss, qds)
-        parts = []
-        for p in range(4):
-            parts += [dqs[p][0:32, :128], dqs[p][32:64, 128:]]
-        dq_s[:, at] = old_dq + jnp.concatenate(parts, axis=0)
-        gk[keys, :] = new_gk
-        gv[keys, :] = new_gv
+        dps = [[nn(w[6][p], w[3][p]) for p in range(4)] for w in work]
+        dss = []
+        for w, dp in zip(work, dps):
+            takes = [
+                jnp.concatenate([w[7][2 * p : 2 * p + 1], w[7][2 * p + 1 : 2 * p + 2]], axis=1)
+                for p in range(4)
+            ]
+            dss.append([(w[2][p].astype(f32) * (dp[p] - takes[p])).astype(bf16) for p in range(4)])
+        dqs = [[nn(w[5][p], ds[p]) for p in range(4)] for w, ds in zip(work, dss)]
+        new_gvs = [by_key(w[2], w[3]) for w in work]
+        new_gks = [by_key(ds, w[4]) for w, ds in zip(work, dss)]
+        for w, dq in zip(work, dqs):
+            parts = []
+            for p in range(4):
+                parts += [dq[p][0:32, :128], dq[p][32:64, 128:]]
+            dq_s[:, w[0]] = w[8] + jnp.concatenate(parts, axis=0)
+        gk[work[0][1], :] = old_gk + new_gks[0]
+        gv[work[0][1], :] = old_gv + new_gvs[0]
+        for w, new_gk, new_gv in zip(work[1:], new_gks[1:], new_gvs[1:]):
+            gk[w[1], :] += new_gk
+            gv[w[1], :] += new_gv
+
+    def kept_weights(i, rows):
+        return lambda p: ebuf[blk_tile[i], :rows, pair(p, 256)]
+
+    def queries_of(i):
+        return pl.ds(pl.multiple_of(i * QB, QB), QB)
 
     def backward_block(i, carry):
         at = pl.ds(pl.multiple_of(i * QB, QB), QB)
@@ -778,11 +836,11 @@
 
         @pl.when(simple & (count <= KC_LOW))
         def few():
-            backward_chunk(at, c0, KC_LOW, lambda p: ebuf[tile0, :KC_LOW, pair(p, 256)])
+            backward_some([(at, c0, kept_weights(i, KC_LOW))], KC_LOW)
 
         @pl.when(simple & (count > KC_LOW))
         def full():
-            backward_chunk(at, c0, KC, lambda p: ebuf[tile0, :, pair(p, 256)])
+            backward_some([(at, c0, kept_weights(i, KC))], KC)
 
         @pl.when(jnp.logical_not(simple))
         def many():
@@ -801,22 +859,42 @@
                             s - m_s[i, :, pair(p, 256)]
                         ).astype(bf16)
 
-                backward_chunk(at, c0 + c, KC, lambda p: ecur[:, pair(p, 256)])
+                backward_some([(at, c0 + c, lambda p: ecur[:, pair(p, 256)])], KC)
                 return inner
 
             lax.fori_loop(0, nc, one_chunk, 0)
 
         return carry
 
-    lax.fori_loop(0, num_blocks, backward_block, 0)
+    def backward_pair(j, carry):
+        two = (2 * j, 2 * j + 1)
+        count = jnp.maximum(blk_rows[two[0]], blk_rows[two[1]])
+        simple = (count <= KC) & (blk_tile[two[1]] < E_CAP)
+
+        @pl.when(simple & (count <= KC_LOW))
+        def few():
+            backward_some([(queries_of(i), blk_c0[i], kept_weights(i, KC_LOW)) for i in two], KC_LOW)
+
+        @pl.when(simple & (count > KC_LOW))
+        def full():
+            backward_some([(queries_of(i), blk_c0[i], kept_weights(i, KC)) for i in two], KC)
+
+        @pl.when(jnp.logical_not(simple))
+        def apart():
+            lax.fori_loop(two[0], two[0] + 2, backward_block, 0)
+
+        return carry
+
+    lax.fori_loop(0, pairs, backward_pair, 0)
+    lax.fori_loop(2 * pairs, num_blocks, backward_block, 0)
 
     gkv[...] = jnp.zeros_like(gkv)
     w_q[...] = w_s[:, 0:D]
 
     def mem_back(i, coef_lane):
         found = []
-        for k in range(2):
-            c = 2 * i + k
+        for k in range(MEM_SPAN):
+            c = MEM_SPAN * i + k
             at = pl.ds(pl.multiple_of(c * KC, KC), KC)
             feats_c, unused = mem_feats(c)
             live = ((iota((KC, 1), 0) + c * KC) < ch_end[c]).astype(f32)
@@ -826,18 +904,18 @@
             normed, inverse = norm_t(embed_t(feats_c, emb_w(KC), emb_b(KC)))
             gm = norm_back_t(gmn, normed, inverse, gain_in(KC))
             found.append((gk_c, gv_c, fold(gmn * normed), fold(by_feature(gm, feats_c)), fold(gm)))
-        mn = mnt[:, pl.ds(pl.multiple_of(2 * i * KC, KC), 2 * KC)]
-        gkv[:, 0:D] += nn(mn, jnp.concatenate([found[0][0], found[1][0]], axis=0))
-        gkv[:, D : 2 * D] += nn(mn, jnp.concatenate([found[0][1], found[1][1]], axis=0))
+        mn = mnt[:, pl.ds(pl.multiple_of(MEM_SPAN * i * KC, KC), MEM_SPAN * KC)]
+        gkv[:, 0:D] += nn(mn, jnp.concatenate([one[0] for one in found], axis=0))
+        gkv[:, D : 2 * D] += nn(mn, jnp.concatenate([one[1] for one in found], axis=0))
         for k, rows in ((2, slice(0, D)), (3, slice(2 * D, 3 * D)), (4, slice(3 * D, 4 * D))):
-            acc_gain[rows, :] += found[0][k] + found[1][k]
+            acc_gain[rows, :] += added(found, k)
         return coef_lane
 
     coef_lane = jnp.concatenate([coefb[0:128, :].T[0:1], coefb[128:256, :].T[0:1]], axis=1)
-    lax.fori_loop(0, lax.div(num_chunks + 1, jnp.int32(2)), mem_back, coef_lane)
-
-
-def step_call(n, num_mem, small_size, table, an, gw):
+    lax.fori_loop(0, lax.div(num_chunks + MEM_SPAN - 1, jnp.int32(MEM_SPAN)), mem_back, coef_lane)
+
+
+def step_call(n, num_mem, small_size, an, gw):
     q_blocks, k_chunks = gw.shape[0] - n, chunks_of(num_mem)
     qs, ks = q_blocks * QB, k_chunks * KC
     V = pltpu.VMEM
@@ -860,15 +938,16 @@
         V((q_blocks, 1, 1024), f32),
         S((q_blocks,), jnp.int32), S((q_blocks,), jnp.int32), S((q_blocks,), jnp.int32),
         S((q_blocks,), jnp.int32), S((k_chunks,), jnp.int32), S((k_chunks,), jnp.int32),
+        V((8, num_mem // 16), jnp.int32), S((8, num_mem // 16), jnp.int32), pltpu.SemaphoreType.DMA,
     ]
     return pl.pallas_call(
         functools.partial(step_kernel, n, qs, num_mem, small_size),
         out_shape=outs,
-        in_specs=[sm, sm, vm],
+        in_specs=[sm, vm],
         out_specs=(vm,) * len(outs),
         scratch_shapes=scratch,
         compiler_params=pltpu.CompilerParams(vmem_limit_bytes=STEP_VMEM),
-    )(table, an, gw)
+    )(an, gw)
 
 
 MESH = pl.DeviceIdType.MESH
@@ -906,8 +985,8 @@
     n, num_q, num_mem, *refs,
 ):
     sources, refs = refs[:12], refs[12:]
-    gw, table, keep = refs[:3]
-    copied, refs = refs[3:15], refs[15:]
+    gw, keep = refs[:2]
+    copied, refs = refs[2:14], refs[14:]
     send_z, recv_z, send_s, recv_s, send_c, recv_c, load = refs
     loads = [
         pltpu.make_async_copy(sources[i], copied[i], load.at[i]) for i in range(len(sources))
@@ -1044,10 +1123,13 @@
     lane_t = iota((8, 8 * cuts), 1)
     numbers = jnp.where(
         row_t == 0, as_row(starts), jnp.where(row_t == 1, as_row(totals), as_row(slots))
-    ).astype(jnp.int32)
+    )
     for i, number in enumerate(m_base + m_count + m_units + q_base + q_units):
-        numbers = jnp.where((row_t == 3) & (lane_t == i), number, numbers)
-    table[...] = numbers
+        numbers = jnp.where((row_t == 3) & (lane_t == i), number.astype(f32), numbers)
+    for i in range(cuts // 16):
+        gw[n + 1 + i, 48:64, :] = jnp.concatenate(
+            split2(numbers[:, 128 * i : 128 * i + 128]), axis=0
+        ).astype(bf16)
     gw[n, 48 : 48 + cuts, :] = places_m.astype(bf16)
     heads_low = jnp.concatenate([w_heads[:, 128:], jnp.zeros((1, 256 - per_head), f32)], axis=1)
     small_row = jnp.concatenate([w_small[...], jnp.zeros((1, 128 - per_small), f32)], axis=1)
@@ -1098,11 +1180,10 @@
         functools.partial(gather_kernel, n, num_q, num_mem),
         out_shape=(
             jax.ShapeDtypeStruct((n + qs // 128, 80, 128), bf16),
-            jax.ShapeDtypeStruct((8, num_mem // 16), jnp.int32),
             jax.ShapeDtypeStruct((8, 128), f32),
         ),
         in_specs=[pl.BlockSpec(memory_space=pltpu.HBM)] * 12,
-        out_specs=(vm,) * 3,
+        out_specs=(vm,) * 2,
         scratch_shapes=[pltpu.VMEM(v.shape, v.dtype) for v in operands]
         + [
             dma((planes - 1,)), dma((planes - 1,)), dma((planes, 3)), dma((planes, 3)),
@@ -1122,7 +1203,14 @@
     rows_dev = D // n
     me, core, square, plane = where_am_i(planes)
     in_plane = core + 2 * square
-    a_of = [lax.rem(me + k, n) for k in range(1, n)]
+    upper = lax.div(2 * plane, planes)
+    low_plane = plane + upper * (planes - 1 - 2 * plane)
+    a_of = []
+    for i in range(planes):
+        z = planes - 1 - i - lax.div(low_plane + i, max(planes - 1, 1)) if i < planes - 1 else low_plane
+        z = z + upper * (planes - 1 - 2 * z)
+        for k in (6, 7, 4, 5, 2, 3, 1, 0) if i < planes - 1 else (6, 7, 4, 5, 2, 3, 1):
+            a_of.append(z * 8 + lax.rem(in_plane + k, 8))
     z_of = [lax.rem(plane + k, planes) * 8 + in_plane for k in range(1, planes)]
     s_of = [plane * 8 + lax.rem(square + k, 4) * 2 + core for k in range(1, 4)]
     c_of = plane * 8 + square * 2 + (1 - core)
@@ -1258,13 +1346,23 @@
     losses = l_in[0:1, :]
     losses = losses + pltpu.roll(losses, 64, 1)
     n_mine[...] = jnp.where(iota((1, 128), 1) < 64, squares, losses)
-    last = []
+    n_all[me] = n_mine[...]
+    last = [
+        send(n_mine, n_all.at[me], send_n.at[k], recv_n.at[me], a_of[k]) for k in range(n - 1)
+    ]
     for k in range(1, n):
-        last.append(send(n_mine, n_all.at[k - 1], send_n.at[k - 1], recv_n.at[k - 1], a_of[k - 1]))
-    total = n_mine[...]
+        other = lax.rem(me + k, n)
+        pltpu.make_async_remote_copy(
+            src_ref=n_mine,
+            dst_ref=n_all.at[other],
+            send_sem=send_n.at[k - 1],
+            recv_sem=recv_n.at[other],
+            device_id=(other,),
+            device_id_type=MESH,
+        ).wait_recv()
+    total = n_all[0]
     for k in range(1, n):
-        last[k - 1].wait_recv()
-        total = total + n_all[k - 1]
+        total = total + n_all[k]
     t_out[...] = total
     for copies in (pieces, crossing, along):
         for copy in copies.values():
@@ -1292,9 +1390,9 @@
             V((D, D), f32), V((4 * D + H, 128), f32),
             V((n, rows, 128), bf16), V((4, planes, rows, 128), bf16), V((3, planes, rows, 128), bf16),
             V((3, planes, rows, 128), bf16), V((z, rows, 128), bf16), V((z, rows, 128), bf16),
-            V((planes, rows, 128), f32), V((1, 128), f32), V((n - 1, 1, 128), f32),
+            V((planes, rows, 128), f32), V((1, 128), f32), V((n, 1, 128), f32),
             dma((4,)), dma((4,)), dma((3, planes)), dma((3, planes)), dma((z,)), dma((z,)),
-            dma((n - 1,)), dma((n - 1,)),
+            dma((n - 1,)), dma((n,)),
         ],
         compiler_params=pltpu.CompilerParams(
             collective_id=1, has_side_effects=True, vmem_limit_bytes=16 * 1024 * 1024
@@ -1375,11 +1473,11 @@
     firsts = (tiles(m_qkv), tiles(m_out), row(m_heads), row(m_small))
     seconds = (tiles(v_qkv), tiles(v_out), row(v_heads), row(v_small))
     tm, mt = row(target_mask), row(memory_task)
-    gw, table, keep = gather_call(
+    gw, keep = gather_call(
         n, *weights, memory_feats.T, query_feats.T, feature_mask.T, row(query_task),
         row(target_class), tm, mt, row(memory_mask),
     )
-    found = step_call(n, mt.shape[1], w_small.shape[0] * n, table, anneal, gw)
+    found = step_call(n, mt.shape[1], w_small.shape[0] * n, anneal, gw)
     grads, totals = reduce_call(n, w_small.shape[0], *found)
     outs = update_call(grads, totals, weights[0], weights[1], keep, firsts, seconds)
     outs = [out.reshape(-1) for out in outs]

time: 69.9 us -> 65.5 us (0.937)
  Pallas kernels: 65.4 us -> 62.3 us
    pallas_call x1, Pallas kernels: 21.9 us -> 19.9 us  [reduce_call(): pl.pallas_call(functools.partial(reduce_kernel, n, per_small), out_shape=...]
    pallas_call x1, Pallas kernels: 27.3 us -> 26.1 us  [step_call(): pl.pallas_call(functools.partial(step_kernel, n, qs, num_mem, small_size)...]
    unnamed x26 -> x24, local copies, waits for them, and re-layouts: 1.91 us -> 1.23 us
where the time goes in v5:
time: 65.5 us; the launch traced here: 65.2 us
  Pallas kernels  62.3 us (95%)
  between operations  1.69 us (3%)
  local copies, waits for them, and re-layouts  1.23 us (2%)
    pallas_call x1, Pallas kernels, step_call(): pl.pallas_call(functools.partial(step_kernel, n, qs, num_mem, small_size)...  26.1 us
    pallas_call x1, Pallas kernels, reduce_call(): pl.pallas_call(functools.partial(reduce_kernel, n, per_small), out_shape=...  19.9 us
    pallas_call x1, Pallas kernels, gather_call(): pl.pallas_call(functools.partial(gather_kernel, n, num_q, num_mem), out_s...  15.4 us

profile of v5, /device:TPU:0, one launch (start us, length us, event | category | flops | bytes accessed | tf_op | source)
XLA Modules:
  0.0 65.2 jit_solution(7622334125967616323)
XLA Ops:
  1.3 15.4 %shard_map.340 = (bf16[44,80,128]{2,1,0:T(8,128)(2,1)}, f32[8,128]{1,0:T(8,128)}) custom-call(f32[48,128]{1,0:T(8,128)} %bitcast.37, f32[16,128]{1,0:T(8,128)} %bitcast.39, f32[1,192]{1,0:T(1,128)} %bitcast.57, f32[1,33]{1,0:T(1,128)} %bitcast.58, f32[8,64]{1,0:T(8,128)} %bitcast.53, f32[8,1024]{1,0:T(8,128)} %bitcast.49, s32[8,1024]{1,0:T(8,128)} %bitcast.50, ...), custom_call_target="tpu_custom_call" | custom-call | tf_op jit(solution)/shard_map/pallas_call | solution.py:1179
  16.8 0.0 copy-start
  16.8 1.2 %copy-done = bf16[44,80,128]{2,1,0:T(8,128)(2,1)S(1)} copy-done((bf16[44,80,128]{2,1,0:T(8,128)(2,1)S(1)}, bf16[44,80,128]{2,1,0:T(8,128)(2,1)}, u32[]{:S(2)}) %copy-start) | copy-done | bytes 901144
  17.9 26.1 %shard_map.341 = (f32[8,1536]{1,0:T(8,128)S(1)}, f32[8,1536]{1,0:T(8,128)S(1)}, bf16[256,1536]{1,0:T(8,128)(2,1)S(1)}, bf16[256,1536]{1,0:T(8,128)(2,1)S(1)}, bf...) custom-call(f32[1]{0:T(128)S(6)} %copy.39.an, ...), custom_call_target="tpu_custom_call" | custom-call | tf_op jit(solution)/shard_map/pallas_call | solution.py:943
  44.0 0.0 copy-start.1
  44.0 0.0 copy-start.2
  44.1 0.0 copy-start.3
  44.1 0.0 copy-start.4
  44.1 0.0 copy-start.5
  44.1 0.0 copy-start.6
  44.1 0.0 copy-start.7
  44.1 0.0 copy-start.8
  44.1 0.0 copy-start.9
  44.1 0.0 copy-start.10
  44.2 0.0 copy-start.11
  44.2 19.9 %shard_map.342 = (f32[80,128]{1,0:T(8,128)S(1)}, f32[1,128]{1,0:T(1,128)S(1)}) custom-call(f32[8,1536]{1,0:T(8,128)S(1)} %get-tuple-element.57.xs, f32[8,1536]{1,0:T(8,128)S(1)} %get-tuple-element.58.fs, bf16[256,1536]{1,0:T(8,128)(2,1)S(1)} %get-tuple-element.59.qn_s, bf16[256,1536]{1,0:T(8,128)(2,1)S(1)} %get-tuple-element.60.q_s, ...), custom_call_target="tpu_custom_call" | custom-call | tf_op jit(solution)/shard_map/pallas_call | solution.py:1381
  64.1 0.0 copy-done.1
  64.1 0.0 copy-done.2
  64.1 0.0 copy-done.3
  64.1 0.0 copy-done.4
  64.1 0.0 copy-done.5
  64.1 0.0 copy-done.6
  64.2 0.0 copy-done.7
  64.2 0.0 copy-done.8
  64.2 0.0 copy-done.9
  64.2 0.0 copy-done.10
  64.2 0.0 copy-done.11
  64.2 0.8 %shard_map.343 = (f32[48,128]{1,0:T(8,128)}, f32[16,128]{1,0:T(8,128)}, f32[1,192]{1,0:T(1,128)}, f32[1,33]{1,0:T(1,128)}, f32[48,128]{1,0:T(8,128)}, /*index=5*...) custom-call(f32[80,128]{1,0:T(8,128)S(1)} %get-tuple-element.73.g, ...), custom_call_target="tpu_custom_call" | custom-call | tf_op jit(solution)/shard_map/pallas_call | solution.py:1451
Async XLA Ops:
  16.8 1.2 %copy-start = (bf16[44,80,128]{2,1,0:T(8,128)(2,1)S(1)}, bf16[44,80,128]{2,1,0:T(8,128)(2,1)}, u32[]{:S(2)}) copy-start(bf16[44,80,128]{2,1,0:T(8,128)(2,1)} %get-tuple-element.56.gw) | copy-start | bytes 2703364
  44.0 20.1 %copy-start.1 = (f32[6144]{0:T(1024)S(1)}, f32[6144]{0:T(1024)}, u32[]{:S(2)}) copy-start(f32[6144]{0:T(1024)} %param.30) | copy-start | bytes 73732
  44.0 20.1 %copy-start.2 = (f32[2048]{0:T(1024)S(1)}, f32[2048]{0:T(1024)}, u32[]{:S(2)}) copy-start(f32[2048]{0:T(1024)} %param.31) | copy-start | bytes 24580
  44.1 20.1 %copy-start.3 = (f32[6144]{0:T(1024)S(1)}, f32[6144]{0:T(1024)}, u32[]{:S(2)}) copy-start(f32[6144]{0:T(1024)} %param.34) | copy-start | bytes 73732
  44.1 20.1 %copy-start.4 = (f32[6144]{0:T(1024)S(1)}, f32[6144]{0:T(1024)}, u32[]{:S(2)}) copy-start(f32[6144]{0:T(1024)} %param.38) | copy-start | bytes 73732
  44.1 20.1 %copy-start.5 = (f32[2048]{0:T(1024)S(1)}, f32[2048]{0:T(1024)}, u32[]{:S(2)}) copy-start(f32[2048]{0:T(1024)} %param.35) | copy-start | bytes 24580
  44.1 20.0 %copy-start.6 = (f32[2048]{0:T(1024)S(1)}, f32[2048]{0:T(1024)}, u32[]{:S(2)}) copy-start(f32[2048]{0:T(1024)} %param.39) | copy-start | bytes 24580
  44.1 20.0 %copy-start.7 = (f32[8,128]{1,0:T(8,128)S(1)}, f32[8,128]{1,0:T(8,128)}, u32[]{:S(2)}) copy-start(f32[8,128]{1,0:T(8,128)} %get-tuple-element.75.refs_2_) | copy-start | bytes 12292
  44.1 20.0 %copy-start.8 = (f32[192]{0:T(256)S(1)}, f32[192]{0:T(256)}, u32[]{:S(2)}) copy-start(f32[192]{0:T(256)} %param.36) | copy-start | bytes 2308
  44.1 20.0 %copy-start.9 = (f32[192]{0:T(256)S(1)}, f32[192]{0:T(256)}, u32[]{:S(2)}) copy-start(f32[192]{0:T(256)} %param.40) | copy-start | bytes 2308
  44.1 20.0 %copy-start.10 = (f32[33]{0:T(128)S(1)}, f32[33]{0:T(128)}, u32[]{:S(2)}) copy-start(f32[33]{0:T(128)} %param.37) | copy-start | bytes 400
  44.2 20.0 %copy-start.11 = (f32[33]{0:T(128)S(1)}, f32[33]{0:T(128)}, u32[]{:S(2)}) copy-start(f32[33]{0:T(128)} %param.41) | copy-start | bytes 400

commit v6 on v5

--- a/solution.py
+++ b/solution.py
@@ -334,7 +334,7 @@
 LOG2E = math.log2(math.e)
 QB = 128
 KC = 384
-KC_LOW = 320
+ROWS = (320, 352, KC)
 VROWS = 80
 E_CAP = 12
 STEP_VMEM = 44 * 1024 * 1024
@@ -632,6 +632,13 @@
         att[64 * p : 64 * p + 32, at] = (got[0:32, :128] * inverse[:, :128]).astype(bf16)
         att[64 * p + 32 : 64 * p + 64, at] = (got[32:64, 128:] * inverse[:, 128:]).astype(bf16)
 
+    def by_rows(count, work, also=True):
+        for low, rows in zip((0,) + ROWS[:-1], ROWS):
+
+            @pl.when((count > low) & (count <= rows) & also)
+            def some(rows=rows):
+                work(rows)
+
     def forward_some(blocks, rows):
         work = []
         for i in blocks:
@@ -657,13 +664,7 @@
         at = pl.ds(pl.multiple_of(i * QB, QB), QB)
         c0, nc, tile0, count = blk_c0[i], blk_nc[i], blk_tile[i], blk_rows[i]
 
-        @pl.when(count <= KC_LOW)
-        def few():
-            forward_some([i], KC_LOW)
-
-        @pl.when((count > KC_LOW) & (nc == 1))
-        def full():
-            forward_some([i], KC)
+        by_rows(count, lambda rows: forward_some([i], rows))
 
         @pl.when(nc > 1)
         def many():
@@ -701,13 +702,7 @@
         i = 2 * j
         count = jnp.maximum(blk_rows[i], blk_rows[i + 1])
 
-        @pl.when(count <= KC_LOW)
-        def few():
-            forward_some([i, i + 1], KC_LOW)
-
-        @pl.when((count > KC_LOW) & (count <= KC))
-        def full():
-            forward_some([i, i + 1], KC)
+        by_rows(count, lambda rows: forward_some([i, i + 1], rows))
 
         @pl.when(count > KC)
         def apart():
@@ -751,14 +746,14 @@
         g_final = nn(wh_s[:, :32], gho)
         g_res = norm_back_t(g_final, normed, inverse, gain_out(256))
         gb = g_res.astype(bf16)
-        ga = nn(w_s[:, 3 * D : 4 * D], gb).astype(bf16).astype(f32)
+        ga = nn(w_s[:, 3 * D : 4 * D], gb)
         attf = attended.astype(f32)
         das, deltas = [], []
         for h in range(H):
             rows = slice(32 * h, 32 * h + 32)
-            da = (ga[rows] * il_s[h : h + 1, at]).astype(bf16)
-            das.append(da)
-            deltas.append(jnp.sum(da.astype(f32) * attf[rows], axis=0, keepdims=True))
+            inverse_l = il_s[h : h + 1, at]
+            das.append((ga[rows] * inverse_l).astype(bf16))
+            deltas.append(jnp.sum(ga[rows] * attf[rows], axis=0, keepdims=True) * inverse_l)
         return (
             fold(loss), fold(g_final * normed),
             fn, gho, g_res, gb, jnp.concatenate(das, axis=0), jnp.concatenate(deltas, axis=0),
@@ -834,13 +829,9 @@
         c0, nc, tile0, count = blk_c0[i], blk_nc[i], blk_tile[i], blk_rows[i]
         simple = (nc == 1) & (tile0 < E_CAP)
 
-        @pl.when(simple & (count <= KC_LOW))
-        def few():
-            backward_some([(at, c0, kept_weights(i, KC_LOW))], KC_LOW)
-
-        @pl.when(simple & (count > KC_LOW))
-        def full():
-            backward_some([(at, c0, kept_weights(i, KC))], KC)
+        by_rows(
+            count, lambda rows: backward_some([(at, c0, kept_weights(i, rows))], rows), simple
+        )
 
         @pl.when(jnp.logical_not(simple))
         def many():
@@ -871,13 +862,13 @@
         count = jnp.maximum(blk_rows[two[0]], blk_rows[two[1]])
         simple = (count <= KC) & (blk_tile[two[1]] < E_CAP)
 
-        @pl.when(simple & (count <= KC_LOW))
-        def few():
-            backward_some([(queries_of(i), blk_c0[i], kept_weights(i, KC_LOW)) for i in two], KC_LOW)
-
-        @pl.when(simple & (count > KC_LOW))
-        def full():
-            backward_some([(queries_of(i), blk_c0[i], kept_weights(i, KC)) for i in two], KC)
+        by_rows(
+            count,
+            lambda rows: backward_some(
+                [(queries_of(i), blk_c0[i], kept_weights(i, rows)) for i in two], rows
+            ),
+            simple,
+        )
 
         @pl.when(jnp.logical_not(simple))
         def apart():
@@ -988,11 +979,6 @@
     gw, keep = refs[:2]
     copied, refs = refs[2:14], refs[14:]
     send_z, recv_z, send_s, recv_s, send_c, recv_c, load = refs
-    loads = [
-        pltpu.make_async_copy(sources[i], copied[i], load.at[i]) for i in range(len(sources))
-    ]
-    for copy in loads:
-        copy.start()
     w_qkv, w_out, w_heads, w_small, mfeat, qf, fm, qt, tc, tm, mt, mm = copied
     planes = n // 8
     me, core, square, plane = where_am_i(planes)
@@ -1001,6 +987,11 @@
     s_of = [plane * 8 + lax.rem(square + k, 4) * 2 + core for k in range(1, 4)]
     c_of = plane * 8 + square * 2 + (1 - core)
     barrier = greet(z_of + s_of + [c_of])
+    loads = [
+        pltpu.make_async_copy(sources[i], copied[i], load.at[i]) for i in range(len(sources))
+    ]
+    for copy in loads:
+        copy.start()
     for copy in loads:
         copy.wait()
 

time: 65.5 us -> 64.6 us (0.986); the launches traced: 65.2 us -> 65 us
  no operation moved by 1% of the time
where the time goes in v6:
time: 64.6 us; the launch traced here: 65 us
  Pallas kernels  62.1 us (96%)
  between operations  1.69 us (3%)
  local copies, waits for them, and re-layouts  1.23 us (2%)
    pallas_call x1, Pallas kernels, step_call(): pl.pallas_call(functools.partial(step_kernel, n, qs, num_mem, small_size)...  25.6 us
    pallas_call x1, Pallas kernels, reduce_call(): pl.pallas_call(functools.partial(reduce_kernel, n, per_small), out_shape=...  20.1 us
    pallas_call x1, Pallas kernels, gather_call(): pl.pallas_call(functools.partial(gather_kernel, n, num_q, num_mem), out_s...  15.5 us

profile of v6, /device:TPU:0, one launch (start us, length us, event | category | flops | bytes accessed | tf_op | source)
XLA Modules:
  0.0 65.0 jit_solution(15487236166689635097)
XLA Ops:
  1.3 15.5 %shard_map.340 = (bf16[44,80,128]{2,1,0:T(8,128)(2,1)}, f32[8,128]{1,0:T(8,128)}) custom-call(f32[48,128]{1,0:T(8,128)} %bitcast.37, f32[16,128]{1,0:T(8,128)} %bitcast.39, f32[1,192]{1,0:T(1,128)} %bitcast.57, f32[1,33]{1,0:T(1,128)} %bitcast.58, f32[8,64]{1,0:T(8,128)} %bitcast.53, f32[8,1024]{1,0:T(8,128)} %bitcast.49, s32[8,1024]{1,0:T(8,128)} %bitcast.50, ...), custom_call_target="tpu_custom_call" | custom-call | tf_op jit(solution)/shard_map/pallas_call | solution.py:1170
  16.8 0.0 copy-start
  16.8 1.2 %copy-done = bf16[44,80,128]{2,1,0:T(8,128)(2,1)S(1)} copy-done((bf16[44,80,128]{2,1,0:T(8,128)(2,1)S(1)}, bf16[44,80,128]{2,1,0:T(8,128)(2,1)}, u32[]{:S(2)}) %copy-start) | copy-done | bytes 901144
  18.0 25.6 %shard_map.341 = (f32[8,1536]{1,0:T(8,128)S(1)}, f32[8,1536]{1,0:T(8,128)S(1)}, bf16[256,1536]{1,0:T(8,128)(2,1)S(1)}, bf16[256,1536]{1,0:T(8,128)(2,1)S(1)}, bf...) custom-call(f32[1]{0:T(128)S(6)} %copy.39.an, ...), custom_call_target="tpu_custom_call" | custom-call | tf_op jit(solution)/shard_map/pallas_call | solution.py:934
  43.6 0.0 copy-start.1
  43.6 0.0 copy-start.2
  43.6 0.0 copy-start.3
  43.6 0.0 copy-start.4
  43.7 0.0 copy-start.5
  43.7 0.0 copy-start.6
  43.7 0.0 copy-start.7
  43.7 0.0 copy-start.8
  43.7 0.0 copy-start.9
  43.7 0.0 copy-start.10
  43.7 0.0 copy-start.11
  43.7 20.1 %shard_map.342 = (f32[80,128]{1,0:T(8,128)S(1)}, f32[1,128]{1,0:T(1,128)S(1)}) custom-call(f32[8,1536]{1,0:T(8,128)S(1)} %get-tuple-element.57.xs, f32[8,1536]{1,0:T(8,128)S(1)} %get-tuple-element.58.fs, bf16[256,1536]{1,0:T(8,128)(2,1)S(1)} %get-tuple-element.59.qn_s, bf16[256,1536]{1,0:T(8,128)(2,1)S(1)} %get-tuple-element.60.q_s, ...), custom_call_target="tpu_custom_call" | custom-call | tf_op jit(solution)/shard_map/pallas_call | solution.py:1372
  63.9 0.0 copy-done.1
  63.9 0.0 copy-done.2
  63.9 0.0 copy-done.3
  63.9 0.0 copy-done.4
  63.9 0.0 copy-done.5
  63.9 0.0 copy-done.6
  63.9 0.0 copy-done.7
  63.9 0.0 copy-done.8
  63.9 0.0 copy-done.9
  64.0 0.0 copy-done.10
  64.0 0.0 copy-done.11
  64.0 0.8 %shard_map.343 = (f32[48,128]{1,0:T(8,128)}, f32[16,128]{1,0:T(8,128)}, f32[1,192]{1,0:T(1,128)}, f32[1,33]{1,0:T(1,128)}, f32[48,128]{1,0:T(8,128)}, /*index=5*...) custom-call(f32[80,128]{1,0:T(8,128)S(1)} %get-tuple-element.73.g, ...), custom_call_target="tpu_custom_call" | custom-call | tf_op jit(solution)/shard_map/pallas_call | solution.py:1442
Async XLA Ops:
  16.8 1.2 %copy-start = (bf16[44,80,128]{2,1,0:T(8,128)(2,1)S(1)}, bf16[44,80,128]{2,1,0:T(8,128)(2,1)}, u32[]{:S(2)}) copy-start(bf16[44,80,128]{2,1,0:T(8,128)(2,1)} %get-tuple-element.56.gw) | copy-start | bytes 2703364
  43.6 20.3 %copy-start.1 = (f32[6144]{0:T(1024)S(1)}, f32[6144]{0:T(1024)}, u32[]{:S(2)}) copy-start(f32[6144]{0:T(1024)} %param.30) | copy-start | bytes 73732
  43.6 20.3 %copy-start.2 = (f32[2048]{0:T(1024)S(1)}, f32[2048]{0:T(1024)}, u32[]{:S(2)}) copy-start(f32[2048]{0:T(1024)} %param.31) | copy-start | bytes 24580
  43.6 20.3 %copy-start.3 = (f32[6144]{0:T(1024)S(1)}, f32[6144]{0:T(1024)}, u32[]{:S(2)}) copy-start(f32[6144]{0:T(1024)} %param.34) | copy-start | bytes 73732
  43.6 20.3 %copy-start.4 = (f32[6144]{0:T(1024)S(1)}, f32[6144]{0:T(1024)}, u32[]{:S(2)}) copy-start(f32[6144]{0:T(1024)} %param.38) | copy-start | bytes 73732
  43.7 20.3 %copy-start.5 = (f32[2048]{0:T(1024)S(1)}, f32[2048]{0:T(1024)}, u32[]{:S(2)}) copy-start(f32[2048]{0:T(1024)} %param.35) | copy-start | bytes 24580
  43.7 20.3 %copy-start.6 = (f32[2048]{0:T(1024)S(1)}, f32[2048]{0:T(1024)}, u32[]{:S(2)}) copy-start(f32[2048]{0:T(1024)} %param.39) | copy-start | bytes 24580
  43.7 20.2 %copy-start.7 = (f32[8,128]{1,0:T(8,128)S(1)}, f32[8,128]{1,0:T(8,128)}, u32[]{:S(2)}) copy-start(f32[8,128]{1,0:T(8,128)} %get-tuple-element.75.refs_2_) | copy-start | bytes 12292
  43.7 20.2 %copy-start.8 = (f32[192]{0:T(256)S(1)}, f32[192]{0:T(256)}, u32[]{:S(2)}) copy-start(f32[192]{0:T(256)} %param.36) | copy-start | bytes 2308
  43.7 20.2 %copy-start.9 = (f32[192]{0:T(256)S(1)}, f32[192]{0:T(256)}, u32[]{:S(2)}) copy-start(f32[192]{0:T(256)} %param.40) | copy-start | bytes 2308
  43.7 20.2 %copy-start.10 = (f32[33]{0:T(128)S(1)}, f32[33]{0:T(128)}, u32[]{:S(2)}) copy-start(f32[33]{0:T(128)} %param.37) | copy-start | bytes 400
  43.7 20.2 %copy-start.11 = (f32[33]{0:T(128)S(1)}, f32[33]{0:T(128)}, u32[]{:S(2)}) copy-start(f32[33]{0:T(128)} %param.41) | copy-start | bytes 400

commit v7 on v6

--- a/solution.py
+++ b/solution.py
@@ -424,7 +424,7 @@
 
 
 def blocks_of(num_q):
-    blocks = (num_q + TASKS * (QB - 1)) // QB
+    blocks = (num_q + TASKS * (QB - 1)) // QB + 1
     return -(-blocks // 4) * 4
 
 
@@ -440,7 +440,7 @@
     ct, w_s, wt_s, wh_s, wht_s,
     mfeat, kn, vn, kt_s, vt_s, mnt, gk, gv,
     il_s, dap, delta, ebuf, ecur, acc, m_s,
-    blk_c0, blk_nc, blk_tile, blk_rows, ch_base, ch_end, numbers, table, loaded,
+    blk_c0, blk_nc, blk_tile, blk_rows, whole, tails, tail_e, ch_base, ch_end, numbers, table, loaded,
 ):
     planes = n // 8
     per_small = small_size // n
@@ -452,15 +452,21 @@
     copy = pltpu.make_async_copy(numbers, table, loaded)
     copy.start()
     copy.wait()
-    m_base, m_count, m_units, q_base, q_units = (
-        [table[3, TASKS * k + t] for t in range(TASKS)] for k in range(5)
+    m_base, m_count, m_units, q_base, q_units, q_count = (
+        [table[3, TASKS * k + t] for t in range(TASKS)] for k in range(6)
     )
     num_blocks = q_units[0] + q_units[1] + q_units[2] + q_units[3]
     num_chunks = m_units[0] + m_units[1] + m_units[2] + m_units[3]
     for c in range(k_chunks):
         ch_base[c] = jnp.int32(c * KC)
         ch_end[c] = jnp.int32(c * KC)
+    spare = qs // QB - 1
+    blk_c0[spare] = jnp.int32(0)
+    blk_nc[spare] = jnp.int32(1)
+    blk_rows[spare] = jnp.int32(1)
     tile = jnp.int32(0)
+    num_whole = jnp.int32(0)
+    num_tails = jnp.int32(0)
     for t in range(TASKS):
         first_chunk = lax.div(m_base[t], jnp.int32(KC))
         first_block = lax.div(q_base[t], jnp.int32(QB))
@@ -477,9 +483,16 @@
             blk_nc[first_block + i] = m_units[t]
             blk_rows[first_block + i] = m_count[t]
             blk_tile[first_block + i] = tile_in
+            whole[num_whole + i] = first_block + i
             return tile_in + m_units[t]
 
-        tile = lax.fori_loop(0, q_units[t], fill_block, tile)
+        left = q_count[t] - QB * (q_units[t] - 1)
+        is_tail = ((q_units[t] > 0) & (left <= QB // 2) & (m_units[t] == 1)).astype(jnp.int32)
+        tile = lax.fori_loop(0, q_units[t], fill_block, tile) - is_tail
+        num_whole = num_whole + q_units[t] - is_tail
+        tails[num_tails] = first_block + q_units[t] - 1
+        num_tails = num_tails + is_tail
+    tails[num_tails] = jnp.int32(spare)
 
     pieces = [gw[place_of(d, planes)].astype(f32) for d in range(n)]
     for col in range(8):
@@ -699,20 +712,109 @@
         return carry
 
     def forward_pair(j, carry):
-        i = 2 * j
-        count = jnp.maximum(blk_rows[i], blk_rows[i + 1])
-
-        by_rows(count, lambda rows: forward_some([i, i + 1], rows))
+        two = [whole[2 * j], whole[2 * j + 1]]
+        count = jnp.maximum(blk_rows[two[0]], blk_rows[two[1]])
+
+        by_rows(count, lambda rows: forward_some(two, rows))
 
         @pl.when(count > KC)
         def apart():
-            lax.fori_loop(i, i + 2, forward_block, 0)
+            lax.fori_loop(2 * j, 2 * j + 2, forward_listed, 0)
 
         return carry
 
-    pairs = lax.div(num_blocks, jnp.int32(2))
+    def forward_listed(k, carry):
+        return forward_block(whole[k], carry)
+
+    pairs = lax.div(num_whole, jnp.int32(2))
     lax.fori_loop(0, pairs, forward_pair, 0)
-    lax.fori_loop(2 * pairs, num_blocks, forward_block, 0)
+    lax.fori_loop(2 * pairs, num_whole, forward_listed, 0)
+
+    front = iota((128, 128), 1) < 64
+    front_row = iota((1, 128), 1) < 64
+    zero_f = jnp.zeros((32, 128), f32)
+
+    def quad(a, width):
+        return slice(width * a, width * a + width)
+
+    def four_heads(ref, at, a):
+        x = ref[quad(a, 128), at].astype(f32)
+        first = jnp.where(front, x, 0.0)
+        second = jnp.where(front, 0.0, pltpu.roll(x, 64, 1))
+        return jnp.concatenate(
+            [
+                jnp.concatenate([first[0:32], zero_f], axis=1),
+                jnp.concatenate([second[32:64], zero_f], axis=1),
+                jnp.concatenate([zero_f, first[64:96]], axis=1),
+                jnp.concatenate([zero_f, second[96:128]], axis=1),
+            ],
+            axis=0,
+        ).astype(bf16)
+
+    def four_rows(first, second, a):
+        return jnp.concatenate(
+            [
+                jnp.where(front_row, first[4 * a + k : 4 * a + k + 1], second[4 * a + k + 1 : 4 * a + k + 2])
+                for k in (0, 2)
+            ],
+            axis=1,
+        )
+
+    def each_head(a, tile, row_of):
+        for k in range(4):
+            g = k // 2
+            x = tile[row_of(k), 128 * g : 128 * g + 128]
+            x = pltpu.roll(x, 64, 1) if k % 2 else x
+            yield 4 * a + k, jnp.where(iota(x.shape, 1) < 64, x, 0.0)
+
+    def value_rows(k):
+        start = VROWS * (k // 2) + 32 * (k % 2)
+        return slice(start, start + 32)
+
+    def tail_pair(j):
+        return [(tails[2 * j + k], 2 * j + k) for k in range(2)]
+
+    def tail_rows(j):
+        return jnp.maximum(blk_rows[tails[2 * j]], blk_rows[tails[2 * j + 1]])
+
+    coef_heads = jnp.concatenate([coefb[32 * h : 32 * h + 1, :] for h in range(H)], axis=0)
+    coef_four = [LOG2E * four_rows(coef_heads, coef_heads, a) for a in range(2)]
+
+    def forward_tails(two, rows):
+        work = []
+        for i, slot in two:
+            at = pl.ds(pl.multiple_of(i * QB, QB), QB)
+            first = blk_c0[i] * KC
+            keys = pl.ds(pl.multiple_of(first, KC), rows)
+            lanes = pl.ds(pl.multiple_of(first, KC), KC)
+            work += [
+                (
+                    kn[keys, quad(a, 128)], four_heads(q_s, at, a), coef_four[a],
+                    vt_s[quad(a, 2 * VROWS), lanes][:, :rows],
+                )
+                for a in range(2)
+            ]
+        scores = [nn(k, o) * c for k, o, c, unused in work]
+        tops = [jnp.max(s, axis=0, keepdims=True) for s in scores]
+        es = [jnp.exp2(s - top).astype(bf16) for s, top in zip(scores, tops)]
+        sums = [nn(w[3], e) for w, e in zip(work, es)]
+        for n_th, (i, slot) in enumerate(two):
+            at = pl.ds(pl.multiple_of(i * QB, QB), QB)
+            for a in range(2):
+                got = sums[2 * n_th + a]
+                tail_e[slot, :rows, quad(a, 256)] = es[2 * n_th + a]
+                inverse = 1.0 / got[64:65, :]
+                for h, value in each_head(a, got * inverse, value_rows):
+                    att[32 * h : 32 * h + 32, at] = value.astype(bf16)
+                for h, value in each_head(a, inverse, lambda k: slice(0, 1)):
+                    il_s[h : h + 1, at] = value
+
+    def forward_tail_pair(j, carry):
+        by_rows(tail_rows(j), lambda rows: forward_tails(tail_pair(j), rows))
+        return carry
+
+    tail_pairs = lax.div(num_tails + 1, jnp.int32(2))
+    lax.fori_loop(0, tail_pairs, forward_tail_pair, 0)
 
     weight_a = an[0]
     scale_t = weight_a / count_t
@@ -858,7 +960,7 @@
         return carry
 
     def backward_pair(j, carry):
-        two = (2 * j, 2 * j + 1)
+        two = (whole[2 * j], whole[2 * j + 1])
         count = jnp.maximum(blk_rows[two[0]], blk_rows[two[1]])
         simple = (count <= KC) & (blk_tile[two[1]] < E_CAP)
 
@@ -872,12 +974,61 @@
 
         @pl.when(jnp.logical_not(simple))
         def apart():
-            lax.fori_loop(two[0], two[0] + 2, backward_block, 0)
+            lax.fori_loop(2 * j, 2 * j + 2, backward_listed, 0)
 
         return carry
 
+    def backward_listed(k, carry):
+        return backward_block(whole[k], carry)
+
     lax.fori_loop(0, pairs, backward_pair, 0)
-    lax.fori_loop(2 * pairs, num_blocks, backward_block, 0)
+    lax.fori_loop(2 * pairs, num_whole, backward_listed, 0)
+
+    def backward_tails(two, rows):
+        work = []
+        for i, slot in two:
+            at = queries_of(i)
+            lanes = pl.ds(pl.multiple_of(blk_c0[i] * KC, KC), KC)
+            keys = pl.ds(pl.multiple_of(blk_c0[i] * KC, KC), rows)
+            first = delta[:, at]
+            second = pltpu.roll(first, 64, 1)
+            work.append(
+                (
+                    at,
+                    keys,
+                    [tail_e[slot, :rows, quad(a, 256)] for a in range(2)],
+                    [four_heads(dap, at, a) for a in range(2)],
+                    [four_heads(q_s, at, a) for a in range(2)],
+                    [kt_s[quad(a, 128), lanes][:, :rows] for a in range(2)],
+                    [vn[keys, quad(a, 128)] for a in range(2)],
+                    [four_rows(first, second, a) for a in range(2)],
+                )
+            )
+        dps = [[nn(w[6][a], w[3][a]) for a in range(2)] for w in work]
+        dss = [
+            [(w[2][a].astype(f32) * (dp[a] - w[7][a])).astype(bf16) for a in range(2)]
+            for w, dp in zip(work, dps)
+        ]
+        dqs = [[nn(w[5][a], ds[a]) for a in range(2)] for w, ds in zip(work, dss)]
+
+        def by_key(grads, others):
+            return jnp.concatenate([nt(grads[a], others[a]) for a in range(2)], axis=1)
+
+        new_gvs = [by_key(w[2], w[3]) for w in work]
+        new_gks = [by_key(ds, w[4]) for w, ds in zip(work, dss)]
+        for w, dq in zip(work, dqs):
+            for a in range(2):
+                for h, value in each_head(a, dq[a], lambda k: slice(32 * k, 32 * k + 32)):
+                    dq_s[32 * h : 32 * h + 32, w[0]] = value
+        for w, new_gk, new_gv in zip(work, new_gks, new_gvs):
+            gk[w[1], :] += new_gk
+            gv[w[1], :] += new_gv
+
+    def backward_tail_pair(j, carry):
+        by_rows(tail_rows(j), lambda rows: backward_tails(tail_pair(j), rows))
+        return carry
+
+    lax.fori_loop(0, tail_pairs, backward_tail_pair, 0)
 
     gkv[...] = jnp.zeros_like(gkv)
     w_q[...] = w_s[:, 0:D]
@@ -928,7 +1079,8 @@
         V((E_CAP + 1, KC, 1024), bf16), V((KC, 1024), bf16), V((4 * VROWS, 256), f32),
         V((q_blocks, 1, 1024), f32),
         S((q_blocks,), jnp.int32), S((q_blocks,), jnp.int32), S((q_blocks,), jnp.int32),
-        S((q_blocks,), jnp.int32), S((k_chunks,), jnp.int32), S((k_chunks,), jnp.int32),
+        S((q_blocks,), jnp.int32), S((q_blocks,), jnp.int32), S((TASKS + 2,), jnp.int32),
+        V((TASKS, KC, 512), bf16), S((k_chunks,), jnp.int32), S((k_chunks,), jnp.int32),
         V((8, num_mem // 16), jnp.int32), S((8, num_mem // 16), jnp.int32), pltpu.SemaphoreType.DMA,
     ]
     return pl.pallas_call(
@@ -1115,7 +1267,7 @@
     numbers = jnp.where(
         row_t == 0, as_row(starts), jnp.where(row_t == 1, as_row(totals), as_row(slots))
     )
-    for i, number in enumerate(m_base + m_count + m_units + q_base + q_units):
+    for i, number in enumerate(m_base + m_count + m_units + q_base + q_units + q_count):
         numbers = jnp.where((row_t == 3) & (lane_t == i), number.astype(f32), numbers)
     for i in range(cuts // 16):
         gw[n + 1 + i, 48:64, :] = jnp.concatenate(

time: 64.6 us -> 64.4 us (level); the launches traced: 65 us -> 63.8 us
  Pallas kernels: 62.1 us -> 60.8 us
    pallas_call x1, Pallas kernels: 25.6 us -> 24.1 us  [step_call(): pl.pallas_call(functools.partial(step_kernel, n, qs, num_mem, small_size)...]
where the time goes in v7:
time: 64.4 us; the launch traced here: 63.8 us
  Pallas kernels  60.8 us (94%)
  between operations  1.71 us (3%)
  local copies, waits for them, and re-layouts  1.23 us (2%)
    pallas_call x1, Pallas kernels, step_call(): pl.pallas_call(functools.partial(step_kernel, n, qs, num_mem, small_size)...  24.1 us
    pallas_call x1, Pallas kernels, reduce_call(): pl.pallas_call(functools.partial(reduce_kernel, n, per_small), out_shape=...  20.4 us
    pallas_call x1, Pallas kernels, gather_call(): pl.pallas_call(functools.partial(gather_kernel, n, num_q, num_mem), out_s...  15.5 us

profile of v7, /device:TPU:0, one launch (start us, length us, event | category | flops | bytes accessed | tf_op | source)
XLA Modules:
  0.0 63.8 jit_solution(2508514166222820315)
XLA Ops:
  1.3 15.5 %shard_map.340 = (bf16[44,80,128]{2,1,0:T(8,128)(2,1)}, f32[8,128]{1,0:T(8,128)}) custom-call(f32[48,128]{1,0:T(8,128)} %bitcast.37, f32[16,128]{1,0:T(8,128)} %bitcast.39, f32[1,192]{1,0:T(1,128)} %bitcast.57, f32[1,33]{1,0:T(1,128)} %bitcast.58, f32[8,64]{1,0:T(8,128)} %bitcast.53, f32[8,1024]{1,0:T(8,128)} %bitcast.49, s32[8,1024]{1,0:T(8,128)} %bitcast.50, ...), custom_call_target="tpu_custom_call" | custom-call | tf_op jit(solution)/shard_map/pallas_call | solution.py:1322
  16.8 0.0 copy-start
  16.8 1.2 %copy-done = bf16[44,80,128]{2,1,0:T(8,128)(2,1)S(1)} copy-done((bf16[44,80,128]{2,1,0:T(8,128)(2,1)S(1)}, bf16[44,80,128]{2,1,0:T(8,128)(2,1)}, u32[]{:S(2)}) %copy-start) | copy-done | bytes 901144
  18.0 24.1 %shard_map.341 = (f32[8,1536]{1,0:T(8,128)S(1)}, f32[8,1536]{1,0:T(8,128)S(1)}, bf16[256,1536]{1,0:T(8,128)(2,1)S(1)}, bf16[256,1536]{1,0:T(8,128)(2,1)S(1)}, bf...) custom-call(f32[1]{0:T(128)S(6)} %copy.39.an, ...), custom_call_target="tpu_custom_call" | custom-call | tf_op jit(solution)/shard_map/pallas_call | solution.py:1086
  42.1 0.0 copy-start.1
  42.1 0.0 copy-start.2
  42.1 0.0 copy-start.3
  42.1 0.0 copy-start.4
  42.1 0.0 copy-start.5
  42.1 0.0 copy-start.6
  42.1 0.0 copy-start.7
  42.1 0.0 copy-start.8
  42.2 0.0 copy-start.9
  42.2 0.0 copy-start.10
  42.2 0.0 copy-start.11
  42.2 20.4 %shard_map.342 = (f32[80,128]{1,0:T(8,128)S(1)}, f32[1,128]{1,0:T(1,128)S(1)}) custom-call(f32[8,1536]{1,0:T(8,128)S(1)} %get-tuple-element.57.xs, f32[8,1536]{1,0:T(8,128)S(1)} %get-tuple-element.58.fs, bf16[256,1536]{1,0:T(8,128)(2,1)S(1)} %get-tuple-element.59.qn_s, bf16[256,1536]{1,0:T(8,128)(2,1)S(1)} %get-tuple-element.60.q_s, ...), custom_call_target="tpu_custom_call" | custom-call | tf_op jit(solution)/shard_map/pallas_call | solution.py:1524
  62.6 0.0 copy-done.1
  62.6 0.0 copy-done.2
  62.6 0.0 copy-done.3
  62.6 0.0 copy-done.4
  62.6 0.0 copy-done.5
  62.7 0.0 copy-done.6
  62.7 0.0 copy-done.7
  62.7 0.0 copy-done.8
  62.7 0.0 copy-done.9
  62.7 0.0 copy-done.10
  62.7 0.0 copy-done.11
  62.7 0.8 %shard_map.343 = (f32[48,128]{1,0:T(8,128)}, f32[16,128]{1,0:T(8,128)}, f32[1,192]{1,0:T(1,128)}, f32[1,33]{1,0:T(1,128)}, f32[48,128]{1,0:T(8,128)}, /*index=5*...) custom-call(f32[80,128]{1,0:T(8,128)S(1)} %get-tuple-element.73.g, ...), custom_call_target="tpu_custom_call" | custom-call | tf_op jit(solution)/shard_map/pallas_call | solution.py:1594
Async XLA Ops:
  16.8 1.2 %copy-start = (bf16[44,80,128]{2,1,0:T(8,128)(2,1)S(1)}, bf16[44,80,128]{2,1,0:T(8,128)(2,1)}, u32[]{:S(2)}) copy-start(bf16[44,80,128]{2,1,0:T(8,128)(2,1)} %get-tuple-element.56.gw) | copy-start | bytes 2703364
  42.1 20.5 %copy-start.1 = (f32[6144]{0:T(1024)S(1)}, f32[6144]{0:T(1024)}, u32[]{:S(2)}) copy-start(f32[6144]{0:T(1024)} %param.30) | copy-start | bytes 73732
  42.1 20.5 %copy-start.2 = (f32[2048]{0:T(1024)S(1)}, f32[2048]{0:T(1024)}, u32[]{:S(2)}) copy-start(f32[2048]{0:T(1024)} %param.31) | copy-start | bytes 24580
  42.1 20.5 %copy-start.3 = (f32[6144]{0:T(1024)S(1)}, f32[6144]{0:T(1024)}, u32[]{:S(2)}) copy-start(f32[6144]{0:T(1024)} %param.34) | copy-start | bytes 73732
  42.1 20.5 %copy-start.4 = (f32[6144]{0:T(1024)S(1)}, f32[6144]{0:T(1024)}, u32[]{:S(2)}) copy-start(f32[6144]{0:T(1024)} %param.38) | copy-start | bytes 73732
  42.1 20.5 %copy-start.5 = (f32[2048]{0:T(1024)S(1)}, f32[2048]{0:T(1024)}, u32[]{:S(2)}) copy-start(f32[2048]{0:T(1024)} %param.35) | copy-start | bytes 24580
  42.1 20.5 %copy-start.6 = (f32[2048]{0:T(1024)S(1)}, f32[2048]{0:T(1024)}, u32[]{:S(2)}) copy-start(f32[2048]{0:T(1024)} %param.39) | copy-start | bytes 24580
  42.1 20.5 %copy-start.7 = (f32[8,128]{1,0:T(8,128)S(1)}, f32[8,128]{1,0:T(8,128)}, u32[]{:S(2)}) copy-start(f32[8,128]{1,0:T(8,128)} %get-tuple-element.75.refs_2_) | copy-start | bytes 12292
  42.1 20.5 %copy-start.8 = (f32[192]{0:T(256)S(1)}, f32[192]{0:T(256)}, u32[]{:S(2)}) copy-start(f32[192]{0:T(256)} %param.36) | copy-start | bytes 2308
  42.2 20.5 %copy-start.9 = (f32[192]{0:T(256)S(1)}, f32[192]{0:T(256)}, u32[]{:S(2)}) copy-start(f32[192]{0:T(256)} %param.40) | copy-start | bytes 2308
  42.2 20.5 %copy-start.10 = (f32[33]{0:T(128)S(1)}, f32[33]{0:T(128)}, u32[]{:S(2)}) copy-start(f32[33]{0:T(128)} %param.37) | copy-start | bytes 400
  42.2 20.5 %copy-start.11 = (f32[33]{0:T(128)S(1)}, f32[33]{0:T(128)}, u32[]{:S(2)}) copy-start(f32[33]{0:T(128)} %param.41) | copy-start | bytes 400
